TPU v7x, 128 devices: a whole 4x4x4 slice. The times are simulated.
128 devices in a mesh: shard: 8 (over x, y_hi), ctx: 16 (over z, y_lo, core).
Axes of the slice: x: 4, y: 4 (y_hi: 2, y_lo: 2; y = y_hi * 2 + y_lo), z: 4, core: 2. Of those that a mesh axis runs over, the one named last changes fastest.
Arguments:
- tokens: bfloat16 [16384, 2048], P(('shard', 'ctx')), may hold values from -6 to 6
- positions: int32 [8, 2048], P('shard'), may hold values from 0 to 2047, as said below
- out_grad: bfloat16 [16384, 2048], P(('shard', 'ctx')), may hold values from -6 to 6
- attn_gain: bfloat16 [2048], P('shard'), may hold values from 0.5 to 1.5
- w_query: bfloat16 [2048, 2048], P('shard'), may hold values from -0.125 to 0.125
- w_key: bfloat16 [256, 2048], P('shard'), may hold values from -0.125 to 0.125
- w_value: bfloat16 [256, 2048], P('shard'), may hold values from -0.125 to 0.125
- w_out: bfloat16 [2048, 2048], P('shard'), may hold values from -2 to 2
- ffn_gain: bfloat16 [2048], P('shard'), may hold values from 0.5 to 1.5
- w_gate: bfloat16 [5632, 2048], P('shard'), may hold values from -0.125 to 0.125
- w_up: bfloat16 [5632, 2048], P('shard'), may hold values from -0.125 to 0.125
- w_down: bfloat16 [5632, 2048], P('shard'), may hold values from -0.078125 to 0.078125
Outputs:
- activations: bfloat16 [16384, 2048], P(('shard', 'ctx'))
- input_grad: float32 [16384, 2048], P(('shard', 'ctx'))
- attn_gain_grad: float32 [2048], P('shard')
- w_query_grad: float32 [2048, 2048], P('shard')
- w_key_grad: float32 [256, 2048], P('shard')
- w_value_grad: float32 [256, 2048], P('shard')
- w_out_grad: float32 [2048, 2048], P('shard')
- ffn_gain_grad: float32 [2048], P('shard')
- w_gate_grad: float32 [5632, 2048], P('shard')
- w_up_grad: float32 [5632, 2048], P('shard')
- w_down_grad: float32 [5632, 2048], P('shard')
Inputs may be any that keep to these rules, and one draw needn't show every extreme that they name: Row s lists the positions of the rows of sequence s: each block of 128 rows is two runs of 64 consecutive positions, from j * 64 and from (31 - j) * 64, every j of 0 to 15 once in a row.
All inputs are finite; a program needn't handle non-finite values.
Results may differ from a plain program's by a relative error of at most 0.023.
Values may be sent and summed in bfloat16 or wider, within the bound.
A program may use at most 320 MiB of HBM per device.

v0:
```python
import jax
import jax.numpy as jnp
from jax import lax
from jax.sharding import PartitionSpec as P

D = 2048
HEADS = 32
KV_HEADS = 4
HEAD = 64


EPS = 1e-05
BASE = 10000.0
NEG = -1e30


def times(left, right):
    return jnp.dot(left, right, preferred_element_type=jnp.float32)


def times_transposed(left, right):
    return lax.dot_general(
        left, right, (((1,), (1,)), ((), ())), preferred_element_type=jnp.float32
    )


def transposed_times(left, right):
    return lax.dot_general(
        left, right, (((0,), (0,)), ((), ())), preferred_element_type=jnp.float32
    )


def rope_tables(places, width):
    half = width // 2
    freqs = BASE ** (-(jnp.arange(half).astype(jnp.float32) * 2.0 / width))
    angles = places.astype(jnp.float32)[:, None] * freqs[None, :]
    return (jnp.cos(angles), jnp.sin(angles))


def rotate(values, cosine, sine, sign):
    half = values.shape[-1] // 2
    first = values[..., :half]
    second = values[..., half:]
    cosine = cosine[:, None, :]
    sine = sign * sine[:, None, :]
    return jnp.concatenate(
        [first * cosine - second * sine, second * cosine + first * sine], axis=-1
    )


def rms_forward(values, gain):
    inverse = lax.rsqrt(jnp.mean(values * values, axis=-1, keepdims=True) + EPS)
    return (values * inverse * gain, inverse)


def rms_backward(values, inverse, gain, grads):
    scaled = grads * gain
    values_grad = inverse * scaled - values * inverse * inverse * inverse * jnp.mean(
        scaled * values, axis=-1, keepdims=True
    )
    gain_grad = jnp.sum(grads * values * inverse, axis=0)
    return (values_grad, gain_grad)


def split_heads(values, rows):
    return (
        values.reshape(rows, KV_HEADS, HEADS // KV_HEADS, HEAD)
        .transpose(1, 2, 0, 3)
        .reshape(KV_HEADS, -1, HEAD)
    )


def merge_heads(values, rows):
    return (
        values.reshape(KV_HEADS, HEADS // KV_HEADS, rows, HEAD)
        .transpose(2, 0, 1, 3)
        .reshape(rows, HEADS * HEAD)
    )


def alternated_term(parts, devices):
    part_rows = [gradient.shape[1] // devices for gradient, operand in parts]
    block_rows = sum(part_rows)

    def compute_term(start, count):
        blocks = count // block_rows
        pieces = []
        for (gradient, operand), row_count in zip(parts, part_rows):
            pieces.append(
                transposed_times(gradient, operand).reshape(blocks, row_count, operand.shape[1])
            )
        return jnp.concatenate(pieces, axis=1).reshape(blocks * block_rows, -1)

    return (compute_term, part_rows, block_rows)


def split_rows(stacked_rows, part_rows):
    results = []
    offset = 0
    for row_count in part_rows:
        results.append(stacked_rows[offset : offset + row_count])
        offset += row_count
    return results


def regroup(matrix, n_shard, n_ctx):
    rows, width = matrix.shape
    piece = width // (n_shard * n_ctx)
    return matrix.reshape(rows, n_shard, n_ctx, piece).transpose(0, 2, 1, 3).reshape(rows, width)


def local(
    tokens,
    positions,
    out_grad,
    attn_gain,
    w_query,
    w_key,
    w_value,
    w_out,
    ffn_gain,
    w_gate,
    w_up,
    w_down,
):
    tok_rows = tokens.shape[0]
    n_shard = lax.axis_size("shard")
    n_ctx = lax.axis_size("ctx")
    group_size = HEADS // KV_HEADS
    score_scale = HEAD ** (-0.5)
    places = positions[0]
    own_places = lax.dynamic_slice_in_dim(places, lax.axis_index("ctx") * tok_rows, tok_rows)
    query_full, key_full, value_full, out_full, gain_one, gain_two = (
        lax.all_gather(w_query, "shard", axis=0, tiled=True),
        lax.all_gather(w_key, "shard", axis=0, tiled=True),
        lax.all_gather(w_value, "shard", axis=0, tiled=True),
        lax.all_gather(w_out, "shard", axis=0, tiled=True),
        lax.all_gather(attn_gain, "shard", axis=0, tiled=True),
        lax.all_gather(ffn_gain, "shard", axis=0, tiled=True),
    )
    gain_one = gain_one.astype(jnp.float32)
    gain_two = gain_two.astype(jnp.float32)
    inputs = tokens.astype(jnp.float32)
    normed, inverse_one = rms_forward(inputs, gain_one)
    normed_low = normed.astype(jnp.bfloat16)
    cosine, sine = rope_tables(own_places, HEAD)
    query_pre = times_transposed(normed_low, query_full)
    key_pre = times_transposed(normed_low, key_full)
    value_pre = times_transposed(normed_low, value_full)
    queries = rotate(query_pre.reshape(tok_rows, HEADS, HEAD), cosine, sine, 1.0).astype(
        jnp.bfloat16
    )
    keys_own = (
        rotate(key_pre.reshape(tok_rows, KV_HEADS, HEAD), cosine, sine, 1.0)
        .reshape(tok_rows, KV_HEADS * HEAD)
        .astype(jnp.bfloat16)
    )
    values_own = value_pre.astype(jnp.bfloat16)
    keys_all, values_all = (
        lax.all_gather(keys_own, "ctx", axis=0, tiled=True),
        lax.all_gather(values_own, "ctx", axis=0, tiled=True),
    )
    query_heads = split_heads(queries, tok_rows)
    key_heads = keys_all.reshape(-1, KV_HEADS, HEAD).transpose(1, 0, 2)
    value_heads = values_all.reshape(-1, KV_HEADS, HEAD).transpose(1, 0, 2)
    query_places = jnp.tile(own_places, group_size)
    allowed = query_places[:, None] >= places[None, :]

    def head_scores(query_one, key_one):
        return jnp.where(allowed, times_transposed(query_one, key_one) * score_scale, NEG)

    def head_forward(operands):
        query_one, key_one, value_one = operands
        scores = head_scores(query_one, key_one)
        largest = jnp.max(scores, axis=-1, keepdims=True)
        exps = jnp.exp(scores - largest)
        totals = jnp.sum(exps, axis=-1, keepdims=True)
        probs = (exps / totals).astype(jnp.bfloat16)
        return (times(probs, value_one), (largest + jnp.log(totals))[:, 0])

    mixed, log_totals = lax.map(head_forward, (query_heads, key_heads, value_heads))
    attended = merge_heads(mixed, tok_rows).astype(jnp.bfloat16)
    hidden_state = inputs + times(attended, out_full)
    normed_two, inverse_two = rms_forward(hidden_state, gain_two)
    normed_two_low = normed_two.astype(jnp.bfloat16)
    gate_full, up_full, down_full = (
        lax.all_gather(w_gate, "shard", axis=0, tiled=True),
        lax.all_gather(w_up, "shard", axis=0, tiled=True),
        lax.all_gather(w_down, "shard", axis=0, tiled=True),
    )
    gate = times_transposed(normed_two_low, gate_full)
    up_part = times_transposed(normed_two_low, up_full)
    sigmoid = jax.nn.sigmoid(gate)
    activated = gate * sigmoid
    inner = (activated * up_part).astype(jnp.bfloat16)
    outputs = (hidden_state + times(inner, down_full)).astype(jnp.bfloat16)
    gate_full, up_full, down_full = (
        lax.all_gather(w_gate, "shard", axis=0, tiled=True),
        lax.all_gather(w_up, "shard", axis=0, tiled=True),
        lax.all_gather(w_down, "shard", axis=0, tiled=True),
    )
    inner_grad = times_transposed(out_grad, down_full)
    gate_grad = (inner_grad * up_part * sigmoid * (1.0 + gate * (1.0 - sigmoid))).astype(
        jnp.bfloat16
    )
    up_grad = (inner_grad * activated).astype(jnp.bfloat16)
    normed_two_grad = times(gate_grad, gate_full) + times(up_grad, up_full)
    hidden_grad, gain_two_grad = rms_backward(hidden_state, inverse_two, gain_two, normed_two_grad)
    hidden_grad = hidden_grad + out_grad.astype(jnp.float32)
    hidden_low = hidden_grad.astype(jnp.bfloat16)
    query_full, key_full, value_full, out_full = (
        lax.all_gather(w_query, "shard", axis=0, tiled=True),
        lax.all_gather(w_key, "shard", axis=0, tiled=True),
        lax.all_gather(w_value, "shard", axis=0, tiled=True),
        lax.all_gather(w_out, "shard", axis=0, tiled=True),
    )
    attended_grad = times_transposed(hidden_low, out_full).astype(jnp.bfloat16)
    grad_heads = split_heads(attended_grad, tok_rows)

    def head_backward(operands):
        query_one, key_one, value_one, grad_one, log_one = operands
        probs = jnp.exp(head_scores(query_one, key_one) - log_one[:, None])
        prob_grad = times_transposed(grad_one, value_one)
        inner_sum = jnp.sum(probs * prob_grad, axis=-1, keepdims=True)
        score_grad = (probs * (prob_grad - inner_sum)).astype(jnp.bfloat16)
        query_grad = times(score_grad, key_one) * score_scale
        key_grad = transposed_times(score_grad, query_one) * score_scale
        value_grad = transposed_times(probs.astype(jnp.bfloat16), grad_one)
        return (query_grad, key_grad, value_grad)

    query_grads, key_grads, value_grads = lax.map(
        head_backward, (query_heads, key_heads, value_heads, grad_heads, log_totals)
    )
    key_rows = key_grads.transpose(1, 0, 2).reshape(-1, KV_HEADS * HEAD)
    value_rows = value_grads.transpose(1, 0, 2).reshape(-1, KV_HEADS * HEAD)
    key_mine, value_mine = (
        lax.psum_scatter(
            key_rows.astype(jnp.bfloat16), "ctx", scatter_dimension=0, tiled=True
        ).astype(jnp.float32),
        lax.psum_scatter(
            value_rows.astype(jnp.bfloat16), "ctx", scatter_dimension=0, tiled=True
        ).astype(jnp.float32),
    )
    query_pre_grad = (
        rotate(
            merge_heads(query_grads, tok_rows).reshape(tok_rows, HEADS, HEAD), cosine, sine, -1.0
        )
        .reshape(tok_rows, HEADS * HEAD)
        .astype(jnp.bfloat16)
    )
    key_pre_grad = (
        rotate(key_mine.reshape(tok_rows, KV_HEADS, HEAD), cosine, sine, -1.0)
        .reshape(tok_rows, KV_HEADS * HEAD)
        .astype(jnp.bfloat16)
    )
    value_pre_grad = value_mine.astype(jnp.bfloat16)
    normed_grad = (
        times(query_pre_grad, query_full)
        + times(key_pre_grad, key_full)
        + times(value_pre_grad, value_full)
    )
    input_grad, gain_one_grad = rms_backward(inputs, inverse_one, gain_one, normed_grad)
    input_grad = input_grad + hidden_grad
    query_cols, key_cols, value_cols, attended_cols, gate_cols, up_cols, inner_cols = (
        lax.all_to_all(
            regroup(query_pre_grad, n_shard, n_ctx), "ctx", split_axis=1, concat_axis=0, tiled=True
        ),
        lax.all_to_all(
            regroup(key_pre_grad, n_shard, n_ctx), "ctx", split_axis=1, concat_axis=0, tiled=True
        ),
        lax.all_to_all(
            regroup(value_pre_grad, n_shard, n_ctx), "ctx", split_axis=1, concat_axis=0, tiled=True
        ),
        lax.all_to_all(
            regroup(attended, n_shard, n_ctx), "ctx", split_axis=1, concat_axis=0, tiled=True
        ),
        lax.all_to_all(
            regroup(gate_grad, n_shard, n_ctx), "ctx", split_axis=1, concat_axis=0, tiled=True
        ),
        lax.all_to_all(
            regroup(up_grad, n_shard, n_ctx), "ctx", split_axis=1, concat_axis=0, tiled=True
        ),
        lax.all_to_all(
            regroup(inner, n_shard, n_ctx), "ctx", split_axis=1, concat_axis=0, tiled=True
        ),
    )
    normed_all, hidden_all, normed_two_all, out_grad_all = (
        lax.all_gather(normed_low, "ctx", axis=0, tiled=True),
        lax.all_gather(hidden_low, "ctx", axis=0, tiled=True),
        lax.all_gather(normed_two_low, "ctx", axis=0, tiled=True),
        lax.all_gather(out_grad, "ctx", axis=0, tiled=True),
    )
    weight_parts = (
        (query_cols, normed_all),
        (key_cols, normed_all),
        (value_cols, normed_all),
        (attended_cols, hidden_all),
        (gate_cols, normed_two_all),
        (up_cols, normed_two_all),
        (inner_cols, out_grad_all),
    )
    weight_term, part_rows, block_rows = alternated_term(weight_parts, n_shard)
    summed_block = lax.psum_scatter(
        weight_term(jnp.int32(0), block_rows * lax.axis_size("shard")).astype(jnp.bfloat16),
        "shard",
        scatter_dimension=0,
        tiled=True,
    ).astype(jnp.float32)
    query_piece, key_piece, value_piece, out_piece, gate_piece, up_piece, down_piece = split_rows(
        summed_block, part_rows
    )
    query_wgrad, key_wgrad, value_wgrad, out_wgrad, gate_wgrad, up_wgrad, down_wgrad = (
        lax.all_gather(query_piece.astype(jnp.bfloat16), "ctx", axis=0, tiled=True).astype(
            query_piece.dtype
        ),
        lax.all_gather(key_piece.astype(jnp.bfloat16), "ctx", axis=0, tiled=True).astype(
            key_piece.dtype
        ),
        lax.all_gather(value_piece.astype(jnp.bfloat16), "ctx", axis=0, tiled=True).astype(
            value_piece.dtype
        ),
        lax.all_gather(out_piece.astype(jnp.bfloat16), "ctx", axis=0, tiled=True).astype(
            out_piece.dtype
        ),
        lax.all_gather(gate_piece.astype(jnp.bfloat16), "ctx", axis=0, tiled=True).astype(
            gate_piece.dtype
        ),
        lax.all_gather(up_piece.astype(jnp.bfloat16), "ctx", axis=0, tiled=True).astype(
            up_piece.dtype
        ),
        lax.all_gather(down_piece.astype(jnp.bfloat16), "ctx", axis=0, tiled=True).astype(
            down_piece.dtype
        ),
    )
    gain_one_sum, gain_two_sum = lax.psum((gain_one_grad, gain_two_grad), ("shard", "ctx"))
    slice_start = lax.axis_index("shard") * (D // n_shard)
    gain_one_out = lax.dynamic_slice_in_dim(gain_one_sum, slice_start, D // n_shard)
    gain_two_out = lax.dynamic_slice_in_dim(gain_two_sum, slice_start, D // n_shard)
    return (
        outputs,
        input_grad,
        gain_one_out,
        query_wgrad,
        key_wgrad,
        value_wgrad,
        out_wgrad,
        gain_two_out,
        gate_wgrad,
        up_wgrad,
        down_wgrad,
    )


def solution(mesh):
    in_specs = (
        P(("shard", "ctx"), None),
        P("shard", None),
        P(("shard", "ctx"), None),
        P("shard"),
        P("shard", None),
        P("shard", None),
        P("shard", None),
        P("shard", None),
        P("shard"),
        P("shard", None),
        P("shard", None),
        P("shard", None),
    )
    out_specs = (
        P(("shard", "ctx"), None),
        P(("shard", "ctx"), None),
        P("shard"),
        P("shard", None),
        P("shard", None),
        P("shard", None),
        P("shard", None),
        P("shard"),
        P("shard", None),
        P("shard", None),
        P("shard", None),
    )
    return jax.shard_map(local, mesh=mesh, in_specs=in_specs, out_specs=out_specs, check_vma=False)
```

profile of v0, /device:TPU:1, one launch (start us, length us, event | category | flops | bytes accessed | tf_op | source)
XLA Modules:
  0.0 1885.2 jit_solution(4011054686449860245)
XLA Ops:
  9.4 20.5 %all-gather = bf16[8,1,256]{2,1,0:T(2,128)(2,1)S(1)} all-gather(bf16[1,1,256]{2,1,0:T(2,128)(2,1)S(1)} %reshape.298), channel_id=1, replica_groups=mesh['shard'=8,'ctx'=16] {'shard'}, dimensions={0}, use_global_device_ids=true | all-gather | bytes 4608 | tf_op jit(solution)/shard_map/all_gather | solution.py:138
  33.9 26.1 %all-gather.28.cloned.1.call-done = bf16[256,2048]{1,0:T(8,128)(2,1)} async-done(((bf16[32,2048]{1,0:T(8,128)(2,1)}), bf16[256,2048]{1,0:T(8,128)(2,1)}) %all-gather.28.cloned.1.call-update) | async-done | bytes 1048592 | tf_op jit(solution)/shard_map/all_gather | solution.py:135
  62.4 46.1 %all-gather.32.cloned.1.call-done = bf16[256,2048]{1,0:T(8,128)(2,1)} async-done(((bf16[32,2048]{1,0:T(8,128)(2,1)}), bf16[256,2048]{1,0:T(8,128)(2,1)}) %all-gather.32.cloned.1.call-update) | async-done | bytes 1048592 | tf_op jit(solution)/shard_map/all_gather | solution.py:136
  115.0 16.0 all-gather.1
  131.9 13.2 all-gather.30.cloned.1.call-done
  147.2 32.6 %all-gather.34.cloned.1.call-done = bf16[2048,256]{1,0:T(8,128)(2,1)} async-done(((bf16[128,256]{1,0:T(8,128)(2,1)}), bf16[2048,256]{1,0:T(8,128)(2,1)}) %all-gather.34.cloned.1.call-update) | async-done | bytes 1048592 | tf_op jit(solution)/shard_map/all_gather | solution.py:161
  184.8 105.2 %all-gather.26.cloned.1.call-done = bf16[2048,2048]{1,0:T(8,128)(2,1)} async-done(((bf16[256,2048]{1,0:T(8,128)(2,1)}), bf16[2048,2048]{1,0:T(8,128)(2,1)}) %all-gather.26.cloned.1.call-update) | async-done | bytes 8388624 | tf_op jit(solution)/shard_map/all_gather | solution.py:134
  290.0 5.8 fusion.105
  298.3 35.0 %while.30 = (s32[]{:T(128)}, bf16[4,1024,64]{1,2,0:T(8,128)(2,1)}, f32[4,1024]{1,0:T(4,128)S(1)}, bf16[4,1024,64]{2,1,0:T(8,128)(2,1)S(1)}, bf16[4,2048,64]{2,1,...) while((s32[]{:T(128)}, bf16[4,1024,64]{1,2,0:T(8,128)(2,1)}, ...), condition=%wide.region_4.5_spmd.clone.clone, body=%wide.region_1.4_spmd.clone.sunk.clone | while | flops 568327168 | bytes 31013016 | solution.py:181
  335.8 63.2 %all-gather.36.cloned.1.call-done = bf16[2048,2048]{1,0:T(8,128)(2,1)} async-done(((bf16[256,2048]{1,0:T(8,128)(2,1)}), bf16[2048,2048]{1,0:T(8,128)(2,1)}) %all-gather.36.cloned.1.call-update) | async-done | bytes 8388624 | tf_op jit(solution)/shard_map/all_gather | solution.py:137
  405.4 237.6 %all-gather.38.cloned.1.call-done = bf16[5632,2048]{1,0:T(8,128)(2,1)} async-done(((bf16[704,2048]{1,0:T(8,128)(2,1)}), bf16[5632,2048]{1,0:T(8,128)(2,1)}) %all-gather.38.cloned.1.call-update) | async-done | bytes 23068688 | tf_op jit(solution)/shard_map/all_gather | solution.py:187
  643.0 13.3 fusion.107
  656.3 230.7 %all-gather.40.cloned.1.call-done = bf16[5632,2048]{1,0:T(8,128)(2,1)} async-done(((bf16[704,2048]{1,0:T(8,128)(2,1)}), bf16[5632,2048]{1,0:T(8,128)(2,1)}) %all-gather.40.cloned.1.call-update) | async-done | bytes 23068688 | tf_op jit(solution)/shard_map/all_gather | solution.py:188
  887.0 13.3 fusion.108
  900.3 230.7 %all-gather.42.cloned.1.call-done = bf16[5632,2048]{1,0:T(8,128)(2,1)} async-done(((bf16[704,2048]{1,0:T(8,128)(2,1)}), bf16[5632,2048]{1,0:T(8,128)(2,1)}) %all-gather.42.cloned.1.call-update) | async-done | bytes 23068688 | tf_op jit(solution)/shard_map/all_gather | solution.py:189
  1131.0 15.3 multiply_convert_fusion.1
  1146.3 10.3 fusion.109
  1156.6 11.0 multiply_reduce_fusion.1
  1169.8 6.6 convolution_convert_fusion
  1179.0 101.8 %while.31 = (s32[]{:T(128)}, f32[4,1024,64]{1,2,0:T(8,128)}, bf16[4,2048,64]{1,2,0:T(8,128)(2,1)}, bf16[4,2048,64]{1,2,0:T(8,128)(2,1)}, bf16[4,1024,64]{2,1,0:T...) while((s32[]{:T(128)}, f32[4,1024,64]{1,2,0:T(8,128)}, ...), condition=%wide.region_9.10_spmd.clone.clone, body=%wide.region_7.9_spmd.clone.sunk.clone | while | flops 1363344384 | bytes 154965360 | solution.py:231
  1181.8 7.0 multiply_reduce_fusion.6
  1188.8 6.6 multiply_convert_fusion.7
  1207.2 7.0 multiply_reduce_fusion.6
  1214.3 6.9 multiply_convert_fusion.7
  1232.9 7.0 multiply_reduce_fusion.6
  1240.0 6.6 multiply_convert_fusion.7
  1258.2 7.0 multiply_reduce_fusion.6
  1265.3 6.6 multiply_convert_fusion.7
  1286.8 5.5 all-to-all-start.3
  1293.6 10.2 all-to-all-done.3
  1314.3 5.5 all-to-all-done
  1328.3 20.1 %all-to-all-done.4 = bf16[128,16,352]{0,2,1:T(8,128)(2,1)} async-done(((bf16[128,16,352]{0,2,1:T(8,128)(2,1)}), bf16[128,16,352]{0,2,1:T(8,128)(2,1)}, u32[]{:S(2)}, u32[]{:S(2)}) %all-to-all-start.4) | async-done | bytes 1441824 | tf_op jit(solution)/shard_map/all_to_all | solution.py:277
  1362.7 22.3 %all-to-all-done.5 = bf16[128,16,352]{0,2,1:T(8,128)(2,1)} async-done(((bf16[128,16,352]{0,2,1:T(8,128)(2,1)}), bf16[128,16,352]{0,2,1:T(8,128)(2,1)}, u32[]{:S(2)}, u32[]{:S(2)}) %all-to-all-start.5) | async-done | bytes 1441824 | tf_op jit(solution)/shard_map/all_to_all | solution.py:280
  1385.0 5.6 all-to-all-start.6
  1390.7 5.8 fusion.76
  1406.6 18.0 all-to-all-done.6
  1427.5 8.6 fusion.67
  1449.8 7.9 fusion.73
  1457.7 30.0 %reduce-scatter.12.cloned.1.call-done = bf16[128,256]{1,0:T(8,128)(2,1)} async-done(((bf16[2048,256]{1,0:T(8,128)(2,1)}), bf16[128,256]{1,0:T(8,128)(2,1)}) %reduce-scatter.12.cloned.1.call-update) | async-done | bytes 65552
  1489.4 7.8 all-to-all-start.2
  1509.6 34.2 %all-gather.46.cloned.1.call-done = bf16[2048,2048]{1,0:T(8,128)(2,1)} async-done(((bf16[128,2048]{1,0:T(8,128)(2,1)}), bf16[2048,2048]{1,0:T(8,128)(2,1)}) %all-gather.46.cloned.1.call-update) | async-done | bytes 8388624 | tf_op jit(solution)/shard_map/all_gather | solution.py:289
  1548.5 46.0 %concatenate.29 = bf16[8,168,2048]{2,1,0:T(8,128)(2,1)} concatenate(bf16[8,16,2048]{2,1,0:T(8,128)(2,1)S(1)} %copy-done.24, bf16[8,2,2048]{2,1,0:T(2,128)(2,1)} %copy.194, bf16[8,2,2048]{2,1,0:T(2,128)(2,1)} %copy.195, bf16[8,16,2048]{2,1,0:T(8,128)(2,1)S(1)} %fusion.79, bf16[8,44,2048]{2,1,0:T(8,128)(2,1)} %fusion.67, bf16[8,44,2048]{2,1,0:T(8,128)(2,1)} %fusion.70, ...), dimensions={1} | concatenate | bytes 11010048 | tf_op jit(solution)/shard_map/concatenate | solution.py:92
  1594.6 93.6 %reduce-scatter.8.cloned.1.call-done = bf16[168,2048]{1,0:T(8,128)(2,1)} async-done(((bf16[1344,2048]{1,0:T(8,128)(2,1)}), bf16[168,2048]{1,0:T(8,128)(2,1)}) %reduce-scatter.8.cloned.1.call-update) | async-done | bytes 688144 | tf_op jit(solution)/shard_map/reduce_scatter | solution.py:303
  1698.6 11.7 fusion.82
  1712.2 65.4 %all-reduce = (f32[2048]{0:T(1024)S(1)}, f32[2048]{0:T(1024)S(1)}) all-reduce(f32[2048]{0:T(1024)S(1)} %get-tuple-element.251, f32[2048]{0:T(1024)S(1)} %copy-done.45), channel_id=1, replica_groups=mesh['shard'=8,'ctx'=16] {'shard','ctx'}, use_global_device_ids=true, to_apply=%region_14.15 | all-reduce | flops 4096 | bytes 32768 | tf_op jit(solution)/shard_map/psum | solution.py:335
  1782.8 18.7 all-gather.2
  1802.2 17.1 all-gather.3
  1839.6 33.2 %all-gather.60.cloned.1.call-done = bf16[16,44,2048]{2,1,0:T(8,128)(2,1)} async-done(((bf16[1,44,2048]{2,1,0:T(8,128)(2,1)}), bf16[16,44,2048]{2,1,0:T(8,128)(2,1)}) %all-gather.60.cloned.1.call-update) | async-done | bytes 2883600 | tf_op jit(solution)/shard_map/all_gather | solution.py:331
  (364 shorter events, 249.3 us)
Async XLA Ops:
  7.2 52.8 %all-gather.28.cloned.1.call-start = ((), (), s32[]{:S(2)}) async-start(), calls=%async_computation.11 | async-start | bytes 1179648 | tf_op jit(solution)/shard_map/all_gather | solution.py:135
  7.9 100.6 %all-gather.32.cloned.1.call-start = ((), (), s32[]{:S(2)}) async-start(), calls=%async_computation.13 | async-start | bytes 1179648 | tf_op jit(solution)/shard_map/all_gather | solution.py:136
  8.7 136.4 %all-gather.30.cloned.1.call-start = ((), (), s32[]{:S(2)}) async-start(), calls=%async_computation.12 | async-start | bytes 1114112 | tf_op jit(solution)/shard_map/all_gather | solution.py:160
  29.9 82.9 %copy-start.43 = (f32[8,1,256]{2,1,0:T(1,128)}, f32[8,1,256]{2,1,0:T(1,128)S(1)}, u32[]{:S(2)}) copy-start(f32[8,1,256]{2,1,0:T(1,128)S(1)} %convert_element_type.201) | copy-start | bytes 24580
  32.6 263.2 %copy-start.37 = (f32[128,32]{0,1:T(8,128)}, f32[128,32]{0,1:T(8,128)S(1)}, u32[]{:S(2)}) copy-start(f32[128,32]{0,1:T(8,128)S(1)} %get-tuple-element.319) | copy-start | bytes 49156
  33.9 79.0 %copy-start.6 = (bf16[128,2048]{1,0:T(8,128)(2,1)}, bf16[128,2048]{1,0:T(8,128)(2,1)S(1)}, u32[]{:S(2)}) copy-start(bf16[128,2048]{1,0:T(8,128)(2,1)S(1)} %fusion.91) | copy-start | bytes 1572868
  62.3 117.4 %all-gather.34.cloned.1.call-start = ((), (), s32[]{:S(2)}) async-start(), calls=%async_computation.14 | async-start | bytes 1114112 | tf_op jit(solution)/shard_map/all_gather | solution.py:161
  110.9 179.1 %all-gather.26.cloned.1.call-start = ((), (), s32[]{:S(2)}) async-start(), calls=%async_computation.10 | async-start | bytes 9437184 | tf_op jit(solution)/shard_map/all_gather | solution.py:134
  111.5 287.5 %all-gather.36.cloned.1.call-start = ((), (), s32[]{:S(2)}) async-start(), calls=%async_computation.15 | async-start | bytes 9437184 | tf_op jit(solution)/shard_map/all_gather | solution.py:137
  112.1 530.9 %all-gather.38.cloned.1.call-start = ((), (), s32[]{:S(2)}) async-start(), calls=%async_computation.16 | async-start | bytes 25952256 | tf_op jit(solution)/shard_map/all_gather | solution.py:187
  112.9 774.2 %all-gather.40.cloned.1.call-start = ((), (), s32[]{:S(2)}) async-start(), calls=%async_computation.17 | async-start | bytes 25952256 | tf_op jit(solution)/shard_map/all_gather | solution.py:188
  113.6 1017.4 %all-gather.42.cloned.1.call-start = ((), (), s32[]{:S(2)}) async-start(), calls=%async_computation.18 | async-start | bytes 25952256 | tf_op jit(solution)/shard_map/all_gather | solution.py:189
  114.3 1276.3 %all-gather.44.cloned.1.call-start = ((), (), s32[]{:S(2)}) async-start(), calls=%async_computation.19 | async-start | bytes 8912896 | tf_op jit(solution)/shard_map/all_gather | solution.py:288
  114.9 1312.5 %all-gather.48.cloned.1.call-start = ((), (), s32[]{:S(2)}) async-start(), calls=%async_computation.21 | async-start | bytes 8912896 | tf_op jit(solution)/shard_map/all_gather | solution.py:290
  131.0 1036.6 %copy-start.40 = (f32[8,1,256]{2,1,0:T(1,128)}, f32[8,1,256]{2,1,0:T(1,128)S(1)}, u32[]{:S(2)}) copy-start(f32[8,1,256]{2,1,0:T(1,128)S(1)} %convert_element_type.202) | copy-start | bytes 24580
  145.1 144.9 %copy-start.7 = (bf16[128,2048]{1,0:T(8,128)(2,1)S(1)}, bf16[128,2048]{1,0:T(8,128)(2,1)}, u32[]{:S(2)}) copy-start(bf16[128,2048]{1,0:T(8,128)(2,1)} %copy-done.6) | copy-start | bytes 1572868
  333.3 65.7 %copy-start.9 = (bf16[4,1024,64]{2,1,0:T(8,128)(2,1)}, bf16[4,1024,64]{2,1,0:T(8,128)(2,1)S(1)}, u32[]{:S(2)}) copy-start(bf16[4,1024,64]{2,1,0:T(8,128)(2,1)S(1)} %get-tuple-element.585) | copy-start | bytes 1572868
  404.0 763.6 %copy-start.2 = (f32[128,2048]{1,0:T(8,128)}, f32[128,2048]{1,0:T(8,128)S(1)}, u32[]{:S(2)}) copy-start(f32[128,2048]{1,0:T(8,128)S(1)} %get-tuple-element.321) | copy-start | bytes 3145732
  404.0 763.6 %copy-start.46 = (f32[128]{0:T(128)}, f32[128]{0:T(128)S(1)}, u32[]{:S(2)}) copy-start(f32[128]{0:T(128)S(1)} %add_rsqrt_fusion) | copy-start | bytes 1540
  405.2 1035.3 %reduce-scatter.10.cloned.1.call-start = ((), (), s32[]{:S(2)}) async-start(), calls=%async_computation.29 | async-start | bytes 1114112
  1283.2 166.6 %all-gather.50.cloned.1.call-start = ((), (), s32[]{:S(2)}) async-start(), calls=%async_computation.22 | async-start | bytes 8912896 | tf_op jit(solution)/shard_map/all_gather | solution.py:291
  1284.0 203.8 %reduce-scatter.12.cloned.1.call-start = ((), (), s32[]{:S(2)}) async-start(), calls=%async_computation.30 | async-start | bytes 1114112
  1285.4 258.4 %all-gather.46.cloned.1.call-start = ((), (), s32[]{:S(2)}) async-start(), calls=%async_computation.20 | async-start | bytes 8912896 | tf_op jit(solution)/shard_map/all_gather | solution.py:289
  1286.8 21.8 %copy-start.16 = (bf16[128,5632]{1,0:T(8,128)(2,1)S(1)}, bf16[128,5632]{1,0:T(8,128)(2,1)}, u32[]{:S(2)}) copy-start(bf16[128,5632]{1,0:T(8,128)(2,1)} %get-tuple-element.300) | copy-start | bytes 4325380
  1286.8 17.0 all-to-all-start.3
  1303.8 16.0 all-to-all-start
  1312.5 12.8 copy-start.18
  1319.8 28.5 %all-to-all-start.4 = ((bf16[128,16,352]{0,2,1:T(8,128)(2,1)}), bf16[128,16,352]{0,2,1:T(8,128)(2,1)}, u32[]{:S(2)}, u32[]{:S(2)}) async-start(bf16[128,16,352]{0,2,1:T(8,128)(2,1)} %copy.184), calls=%async_computation.4 | async-start | bytes 2883584 | tf_op jit(solution)/shard_map/all_to_all | solution.py:277
  1326.8 26.6 %copy-start.26 = (bf16[128,16,128]{0,2,1:T(8,128)(2,1)S(1)}, bf16[128,16,128]{0,2,1:T(8,128)(2,1)}, u32[]{:S(2)}) copy-start(bf16[128,16,128]{0,2,1:T(8,128)(2,1)} %copy-done.25) | copy-start | bytes 1572868
  1326.8 27.9 %copy-start.15 = (bf16[128,5632]{1,0:T(8,128)(2,1)S(1)}, bf16[128,5632]{1,0:T(8,128)(2,1)}, u32[]{:S(2)}) copy-start(bf16[128,5632]{1,0:T(8,128)(2,1)} %get-tuple-element.301) | copy-start | bytes 4325380
  1348.3 36.7 %all-to-all-start.5 = ((bf16[128,16,352]{0,2,1:T(8,128)(2,1)}), bf16[128,16,352]{0,2,1:T(8,128)(2,1)}, u32[]{:S(2)}, u32[]{:S(2)}) async-start(bf16[128,16,352]{0,2,1:T(8,128)(2,1)} %copy.188), calls=%async_computation.5 | async-start | bytes 2883584 | tf_op jit(solution)/shard_map/all_to_all | solution.py:280
  1385.0 39.6 %all-to-all-start.6 = ((bf16[128,16,352]{0,2,1:T(8,128)(2,1)}), bf16[128,16,352]{0,2,1:T(8,128)(2,1)S(1)}, u32[]{:S(2)}, u32[]{:S(2)}) async-start(bf16[128,16,352]{0,2,1:T(8,128)(2,1)} %copy.192), calls=%async_computation.6 | async-start | bytes 2883584 | tf_op jit(solution)/shard_map/all_to_all | solution.py:283
  1445.0 44.4 %all-to-all-start.1 = ((bf16[128,16,16]{0,2,1:T(8,128)(2,1)}), bf16[128,16,16]{0,2,1:T(8,128)(2,1)}, u32[]{:S(2)}, u32[]{:S(2)}) async-start(bf16[128,16,16]{0,2,1:T(8,128)(2,1)} %copy.171), calls=%async_computation.1 | async-start | bytes 131072 | tf_op jit(solution)/shard_map/all_to_all | solution.py:268
  1489.4 14.6 all-to-all-start.2
  1497.2 191.0 %reduce-scatter.8.cloned.1.call-start = ((), (), s32[]{:S(2)}) async-start(), calls=%async_computation.23 | async-start | bytes 6193152 | tf_op jit(solution)/shard_map/reduce_scatter | solution.py:303
  1504.1 39.7 %copy-start.23 = (bf16[128,2048]{1,0:T(8,128)(2,1)S(1)}, bf16[128,2048]{1,0:T(8,128)(2,1)}, u32[]{:S(2)}) copy-start(bf16[128,2048]{1,0:T(8,128)(2,1)} %copy.181) | copy-start | bytes 1572868
  1594.5 225.5 %all-gather.52.cloned.1.call-start = ((), (), s32[]{:S(2)}) async-start(), calls=%async_computation.24 | async-start | bytes 1114112 | tf_op jit(solution)/shard_map/all_gather | solution.py:313
  1689.7 133.1 %all-gather.54.cloned.1.call-start = ((), (), s32[]{:S(2)}) async-start(), calls=%async_computation.25 | async-start | bytes 1114112 | tf_op jit(solution)/shard_map/all_gather | solution.py:322
  1690.3 135.3 %all-gather.56.cloned.1.call-start = ((), (), s32[]{:S(2)}) async-start(), calls=%async_computation.26 | async-start | bytes 3342336 | tf_op jit(solution)/shard_map/all_gather | solution.py:325
  1692.4 142.3 %all-gather.58.cloned.1.call-start = ((), (), s32[]{:S(2)}) async-start(), calls=%async_computation.27 | async-start | bytes 3342336 | tf_op jit(solution)/shard_map/all_gather | solution.py:328
  1693.0 179.9 %all-gather.60.cloned.1.call-start = ((), (), s32[]{:S(2)}) async-start(), calls=%async_computation.28 | async-start | bytes 3342336 | tf_op jit(solution)/shard_map/all_gather | solution.py:331
  1698.5 12.2 copy-start.8
  1698.5 12.2 copy-start.22
  1710.3 68.6 %copy-start.13 = (f32[128,2048]{1,0:T(8,128)S(1)}, f32[128,2048]{1,0:T(8,128)}, u32[]{:S(2)}) copy-start(f32[128,2048]{1,0:T(8,128)} %copy-done.12) | copy-start | bytes 3145732
  1710.3 68.6 %copy-start.20 = (bf16[128,2048]{1,0:T(8,128)(2,1)S(1)}, bf16[128,2048]{1,0:T(8,128)(2,1)}, u32[]{:S(2)}) copy-start(bf16[128,2048]{1,0:T(8,128)(2,1)} %param.18) | copy-start | bytes 1572868
  1710.3 68.6 %copy-start.41 = (f32[8,1,256]{2,1,0:T(1,128)S(1)}, f32[8,1,256]{2,1,0:T(1,128)}, u32[]{:S(2)}) copy-start(f32[8,1,256]{2,1,0:T(1,128)} %copy-done.40) | copy-start | bytes 24580
  1710.3 68.6 %copy-start.47 = (f32[128]{0:T(128)S(1)}, f32[128]{0:T(128)}, u32[]{:S(2)}) copy-start(f32[128]{0:T(128)} %copy-done.46) | copy-start | bytes 1540
  1710.3 68.6 %copy-start.51 = (f32[128]{0:T(128)S(1)}, f32[128]{0:T(128)}, u32[]{:S(2)}) copy-start(f32[128]{0:T(128)} %copy-done.50) | copy-start | bytes 1540
  (64 other events, 287.3 us)
Sparse Core Ops, SparseCore 0:
  10.3 49.5 all-gather.27
  62.3 46.1 all-gather.31
  110.7 34.3 all-gather.29
  147.2 32.4 all-gather.33
  182.0 107.9 all-gather.25
  292.2 106.8 all-gather.35
  401.4 241.6 all-gather.37
  645.4 241.6 all-gather.39
  889.4 241.6 all-gather.41
  1132.6 50.9 all-gather.43
  1185.2 53.1 all-gather.47
  1283.3 60.2 reduce-scatter.9
  1345.5 83.0 all-gather.49
  1431.0 56.7 reduce-scatter.11
  1489.3 54.3 all-gather.45
  1594.7 93.4 reduce-scatter.7
  1690.4 32.3 all-gather.51
  1725.0 32.5 all-gather.53
  1760.0 35.9 all-gather.55
  1798.2 36.4 all-gather.57
  1837.1 35.7 all-gather.59
where the time goes:
time: 1900 us; the launch traced here: 1890 us
  waiting for transfers between devices  1260 us (66%)
  matrix products  236 us (12%)
  blocking collectives  138 us (7%)
  local copies, waits for them, and re-layouts  134 us (7%)
  other arithmetic  56 us (3%)
  starting transfers between devices  40.3 us (2%)
    all_gather x1, waiting for transfers between devices, local(): lax.all_gather(w_gate, 'shard', axis=0, tiled=True)  238 us
    all_gather x1, waiting for transfers between devices, local(): lax.all_gather(w_up, 'shard', axis=0, tiled=True)  231 us
    all_gather x1, waiting for transfers between devices, local(): lax.all_gather(w_down, 'shard', axis=0, tiled=True)  231 us
    all_gather x1, waiting for transfers between devices, local(): lax.all_gather(w_query, 'shard', axis=0, tiled=True)  105 us
    dot_general x19, matrix products, times_transposed(): lax.dot_general(left, right, (((1,), (1,)), ((), ())), preferred_element_...  103 us
    reduce_scatter x1, waiting for transfers between devices, local(): lax.psum_scatter(weight_term(jnp.int32(0), block_rows * lax.axis_size('sh...  93.6 us
    dot_general x15, matrix products, times(): return jnp.dot(left, right, preferred_element_type=jnp.float32)  73.1 us
    psum x1, blocking collectives, local(): lax.psum((gain_one_grad, gain_two_grad), ('shard', 'ctx'))  65.4 us
  transfers between devices with their start and end apart: 28, of which 19 were waited for; matrix products, arithmetic and copies ran while one was open for 19% of the time, Pallas kernels for 0%

commit v1 on v0

--- a/solution.py
+++ b/solution.py
@@ -78,22 +78,6 @@
     )
 
 
-def alternated_term(parts, devices):
-    part_rows = [gradient.shape[1] // devices for gradient, operand in parts]
-    block_rows = sum(part_rows)
-
-    def compute_term(start, count):
-        blocks = count // block_rows
-        pieces = []
-        for (gradient, operand), row_count in zip(parts, part_rows):
-            pieces.append(
-                transposed_times(gradient, operand).reshape(blocks, row_count, operand.shape[1])
-            )
-        return jnp.concatenate(pieces, axis=1).reshape(blocks * block_rows, -1)
-
-    return (compute_term, part_rows, block_rows)
-
-
 def split_rows(stacked_rows, part_rows):
     results = []
     offset = 0
@@ -103,10 +87,19 @@
     return results
 
 
-def regroup(matrix, n_shard, n_ctx):
-    rows, width = matrix.shape
-    piece = width // (n_shard * n_ctx)
-    return matrix.reshape(rows, n_shard, n_ctx, piece).transpose(0, 2, 1, 3).reshape(rows, width)
+def by_shard(matrix, n_shard):
+    return matrix.reshape(matrix.shape[0], n_shard, -1)
+
+
+def swap_columns(matrix):
+    return lax.all_to_all(matrix, "shard", split_axis=1, concat_axis=0, tiled=True)
+
+
+def sum_over_ctx(partial):
+    piece = lax.psum_scatter(
+        partial.astype(jnp.bfloat16), "ctx", scatter_dimension=0, tiled=True
+    )
+    return lax.all_gather(piece, "ctx", axis=0, tiled=True).astype(jnp.float32)
 
 
 def local(
@@ -138,11 +131,13 @@
         lax.all_gather(attn_gain, "shard", axis=0, tiled=True),
         lax.all_gather(ffn_gain, "shard", axis=0, tiled=True),
     )
+    out_grad_rows = lax.all_gather(out_grad, "shard", axis=0, tiled=True)
     gain_one = gain_one.astype(jnp.float32)
     gain_two = gain_two.astype(jnp.float32)
     inputs = tokens.astype(jnp.float32)
     normed, inverse_one = rms_forward(inputs, gain_one)
     normed_low = normed.astype(jnp.bfloat16)
+    normed_rows = lax.all_gather(normed_low, "shard", axis=0, tiled=True)
     cosine, sine = rope_tables(own_places, HEAD)
     query_pre = times_transposed(normed_low, query_full)
     key_pre = times_transposed(normed_low, key_full)
@@ -183,37 +178,41 @@
     hidden_state = inputs + times(attended, out_full)
     normed_two, inverse_two = rms_forward(hidden_state, gain_two)
     normed_two_low = normed_two.astype(jnp.bfloat16)
-    gate_full, up_full, down_full = (
-        lax.all_gather(w_gate, "shard", axis=0, tiled=True),
-        lax.all_gather(w_up, "shard", axis=0, tiled=True),
-        lax.all_gather(w_down, "shard", axis=0, tiled=True),
-    )
-    gate = times_transposed(normed_two_low, gate_full)
-    up_part = times_transposed(normed_two_low, up_full)
+    normed_two_rows = lax.all_gather(normed_two_low, "shard", axis=0, tiled=True)
+    gate = times_transposed(normed_two_rows, w_gate)
+    up_part = times_transposed(normed_two_rows, w_up)
+    inner_grad = times_transposed(out_grad_rows, w_down)
     sigmoid = jax.nn.sigmoid(gate)
     activated = gate * sigmoid
     inner = (activated * up_part).astype(jnp.bfloat16)
-    outputs = (hidden_state + times(inner, down_full)).astype(jnp.bfloat16)
-    gate_full, up_full, down_full = (
-        lax.all_gather(w_gate, "shard", axis=0, tiled=True),
-        lax.all_gather(w_up, "shard", axis=0, tiled=True),
-        lax.all_gather(w_down, "shard", axis=0, tiled=True),
-    )
-    inner_grad = times_transposed(out_grad, down_full)
     gate_grad = (inner_grad * up_part * sigmoid * (1.0 + gate * (1.0 - sigmoid))).astype(
         jnp.bfloat16
     )
     up_grad = (inner_grad * activated).astype(jnp.bfloat16)
-    normed_two_grad = times(gate_grad, gate_full) + times(up_grad, up_full)
+    normed_two_grad = lax.psum_scatter(
+        (times(gate_grad, w_gate) + times(up_grad, w_up)).astype(jnp.bfloat16),
+        "shard",
+        scatter_dimension=0,
+        tiled=True,
+    ).astype(jnp.float32)
+    down_sum = lax.psum_scatter(
+        times(inner, w_down).astype(jnp.bfloat16), "shard", scatter_dimension=0, tiled=True
+    ).astype(jnp.float32)
+    outputs = (hidden_state + down_sum).astype(jnp.bfloat16)
+    ffn_grads = sum_over_ctx(
+        jnp.concatenate(
+            [
+                transposed_times(gate_grad, normed_two_rows),
+                transposed_times(up_grad, normed_two_rows),
+                transposed_times(inner, out_grad_rows),
+            ],
+            axis=0,
+        )
+    )
     hidden_grad, gain_two_grad = rms_backward(hidden_state, inverse_two, gain_two, normed_two_grad)
     hidden_grad = hidden_grad + out_grad.astype(jnp.float32)
     hidden_low = hidden_grad.astype(jnp.bfloat16)
-    query_full, key_full, value_full, out_full = (
-        lax.all_gather(w_query, "shard", axis=0, tiled=True),
-        lax.all_gather(w_key, "shard", axis=0, tiled=True),
-        lax.all_gather(w_value, "shard", axis=0, tiled=True),
-        lax.all_gather(w_out, "shard", axis=0, tiled=True),
-    )
+    hidden_rows = lax.all_gather(hidden_low, "shard", axis=0, tiled=True)
     attended_grad = times_transposed(hidden_low, out_full).astype(jnp.bfloat16)
     grad_heads = split_heads(attended_grad, tok_rows)
 
@@ -261,77 +260,26 @@
     )
     input_grad, gain_one_grad = rms_backward(inputs, inverse_one, gain_one, normed_grad)
     input_grad = input_grad + hidden_grad
-    query_cols, key_cols, value_cols, attended_cols, gate_cols, up_cols, inner_cols = (
-        lax.all_to_all(
-            regroup(query_pre_grad, n_shard, n_ctx), "ctx", split_axis=1, concat_axis=0, tiled=True
+    out_grads_attn = transposed_times(swap_columns(attended), hidden_rows)
+    factor_grads = transposed_times(
+        swap_columns(
+            jnp.concatenate(
+                [
+                    by_shard(query_pre_grad, n_shard),
+                    by_shard(key_pre_grad, n_shard),
+                    by_shard(value_pre_grad, n_shard),
+                ],
+                axis=2,
+            ).reshape(tok_rows, -1)
         ),
-        lax.all_to_all(
-            regroup(key_pre_grad, n_shard, n_ctx), "ctx", split_axis=1, concat_axis=0, tiled=True
-        ),
-        lax.all_to_all(
-            regroup(value_pre_grad, n_shard, n_ctx), "ctx", split_axis=1, concat_axis=0, tiled=True
-        ),
-        lax.all_to_all(
-            regroup(attended, n_shard, n_ctx), "ctx", split_axis=1, concat_axis=0, tiled=True
-        ),
-        lax.all_to_all(
-            regroup(gate_grad, n_shard, n_ctx), "ctx", split_axis=1, concat_axis=0, tiled=True
-        ),
-        lax.all_to_all(
-            regroup(up_grad, n_shard, n_ctx), "ctx", split_axis=1, concat_axis=0, tiled=True
-        ),
-        lax.all_to_all(
-            regroup(inner, n_shard, n_ctx), "ctx", split_axis=1, concat_axis=0, tiled=True
-        ),
-    )
-    normed_all, hidden_all, normed_two_all, out_grad_all = (
-        lax.all_gather(normed_low, "ctx", axis=0, tiled=True),
-        lax.all_gather(hidden_low, "ctx", axis=0, tiled=True),
-        lax.all_gather(normed_two_low, "ctx", axis=0, tiled=True),
-        lax.all_gather(out_grad, "ctx", axis=0, tiled=True),
-    )
-    weight_parts = (
-        (query_cols, normed_all),
-        (key_cols, normed_all),
-        (value_cols, normed_all),
-        (attended_cols, hidden_all),
-        (gate_cols, normed_two_all),
-        (up_cols, normed_two_all),
-        (inner_cols, out_grad_all),
-    )
-    weight_term, part_rows, block_rows = alternated_term(weight_parts, n_shard)
-    summed_block = lax.psum_scatter(
-        weight_term(jnp.int32(0), block_rows * lax.axis_size("shard")).astype(jnp.bfloat16),
-        "shard",
-        scatter_dimension=0,
-        tiled=True,
-    ).astype(jnp.float32)
-    query_piece, key_piece, value_piece, out_piece, gate_piece, up_piece, down_piece = split_rows(
-        summed_block, part_rows
-    )
-    query_wgrad, key_wgrad, value_wgrad, out_wgrad, gate_wgrad, up_wgrad, down_wgrad = (
-        lax.all_gather(query_piece.astype(jnp.bfloat16), "ctx", axis=0, tiled=True).astype(
-            query_piece.dtype
-        ),
-        lax.all_gather(key_piece.astype(jnp.bfloat16), "ctx", axis=0, tiled=True).astype(
-            key_piece.dtype
-        ),
-        lax.all_gather(value_piece.astype(jnp.bfloat16), "ctx", axis=0, tiled=True).astype(
-            value_piece.dtype
-        ),
-        lax.all_gather(out_piece.astype(jnp.bfloat16), "ctx", axis=0, tiled=True).astype(
-            out_piece.dtype
-        ),
-        lax.all_gather(gate_piece.astype(jnp.bfloat16), "ctx", axis=0, tiled=True).astype(
-            gate_piece.dtype
-        ),
-        lax.all_gather(up_piece.astype(jnp.bfloat16), "ctx", axis=0, tiled=True).astype(
-            up_piece.dtype
-        ),
-        lax.all_gather(down_piece.astype(jnp.bfloat16), "ctx", axis=0, tiled=True).astype(
-            down_piece.dtype
-        ),
-    )
+        normed_rows,
+    )
+    attn_grads = sum_over_ctx(jnp.concatenate([factor_grads, out_grads_attn], axis=0))
+    q_rows, kv_rows = w_query.shape[0], w_key.shape[0]
+    query_wgrad, key_wgrad, value_wgrad, out_wgrad = split_rows(
+        attn_grads, [q_rows, kv_rows, kv_rows, q_rows]
+    )
+    gate_wgrad, up_wgrad, down_wgrad = split_rows(ffn_grads, [w_gate.shape[0]] * 3)
     gain_one_sum, gain_two_sum = lax.psum((gain_one_grad, gain_two_grad), ("shard", "ctx"))
     slice_start = lax.axis_index("shard") * (D // n_shard)
     gain_one_out = lax.dynamic_slice_in_dim(gain_one_sum, slice_start, D // n_shard)

time: 1900 us -> 1370 us (0.72)
  waiting for transfers between devices: 1260 us -> 702 us
  blocking collectives: 138 us -> 263 us
  local copies, waits for them, and re-layouts: 134 us -> 82.9 us
  matrix products: 236 us -> 197 us
  starting transfers between devices: 40.3 us -> 20.1 us
    all_gather x12 -> x6, waiting for transfers between devices: 771 us -> 254 us  [the longest x1 68.3 us: local(): lax.all_gather(normed_two_low, 'shard', axis=0, tiled=True)]
    unnamed x0 -> x1, blocking collectives: none -> 149 us
    all_to_all x7 -> x1, waiting for transfers between devices: 76.1 us -> 0.01 us  [swap_columns(): lax.all_to_all(matrix, 'shard', split_axis=1, concat_axis=0, tiled=True)]
    unnamed x23 -> x21, waiting for transfers between devices: 38.2 us -> 88.4 us
    concatenate x1 -> x0, local copies, waits for them, and re-layouts: 46 us -> none  [compute_term(): return jnp.concatenate(pieces, axis=1).reshape(blocks * block_rows, -1)]
    all_gather x2 -> x0, blocking collectives: 35.8 us -> none  [the longest x1 18.7 us: local(): lax.all_gather(key_piece.astype(jnp.bfloat16), 'ctx', axis=0, tiled=True)]
    all_to_all x7 -> x1, starting transfers between devices: 39 us -> 6.35 us  [swap_columns(): lax.all_to_all(matrix, 'shard', split_axis=1, concat_axis=0, tiled=True)]
    reduce_scatter x1 -> x2, waiting for transfers between devices: 93.6 us -> 81.9 us  [the longest x1 81.9 us: local(): lax.psum_scatter((times(gate_grad, w_gate) + times(up_grad, w_up)).astype...]
  transfers between devices with their start and end apart: 28 -> 20, of which waited for: 19 -> 15; matrix products, arithmetic and copies ran while one was open for 19% -> 24% of each run, Pallas kernels for 0% -> 0%
where the time goes in v1:
time: 1370 us; the launch traced here: 1360 us
  waiting for transfers between devices  702 us (51%)
  blocking collectives  263 us (19%)
  matrix products  197 us (14%)
  local copies, waits for them, and re-layouts  82.9 us (6%)
  other arithmetic  73 us (5%)
  starting transfers between devices  20.1 us (1%)
  between operations  15.7 us (1%)
    unnamed x1, blocking collectives  149 us
    all_gather x1, waiting for transfers between devices, local(): lax.all_gather(w_query, 'shard', axis=0, tiled=True)  105 us
    unnamed x21, waiting for transfers between devices  88.4 us
    dot_general x19, matrix products, times_transposed(): lax.dot_general(left, right, (((1,), (1,)), ((), ())), preferred_element_...  87.5 us
    reduce_scatter x1, waiting for transfers between devices, local(): lax.psum_scatter((times(gate_grad, w_gate) + times(up_grad, w_up)).astype...  81.9 us
    all_gather x1, waiting for transfers between devices, local(): lax.all_gather(normed_two_low, 'shard', axis=0, tiled=True)  68.3 us
    all_gather x1, waiting for transfers between devices, local(): hidden_rows = lax.all_gather(hidden_low, 'shard', axis=0, tiled=True)  66.8 us
    psum x1, blocking collectives, local(): lax.psum((gain_one_grad, gain_two_grad), ('shard', 'ctx'))  65.6 us
  transfers between devices with their start and end apart: 20, of which 15 were waited for; matrix products, arithmetic and copies ran while one was open for 24% of the time, Pallas kernels for 0%

profile of v1, /device:TPU:1, one launch (start us, length us, event | category | flops | bytes accessed | tf_op | source)
XLA Modules:
  0.0 1355.1 jit_solution(6301919022995792254)
XLA Ops:
  9.4 20.5 %all-gather = bf16[8,1,256]{2,1,0:T(2,128)(2,1)S(1)} all-gather(bf16[1,1,256]{2,1,0:T(2,128)(2,1)S(1)} %reshape.242), channel_id=1, replica_groups=mesh['shard'=8,'ctx'=16] {'shard'}, dimensions={0}, use_global_device_ids=true | all-gather | bytes 4608 | tf_op jit(solution)/shard_map/all_gather | solution.py:131
  33.9 26.1 %all-gather.19.cloned.1.call-done = bf16[256,2048]{1,0:T(8,128)(2,1)} async-done(((bf16[32,2048]{1,0:T(8,128)(2,1)}), bf16[256,2048]{1,0:T(8,128)(2,1)}) %all-gather.19.cloned.1.call-update) | async-done | bytes 1048592 | tf_op jit(solution)/shard_map/all_gather | solution.py:128
  62.4 46.2 %all-gather.23.cloned.1.call-done = bf16[256,2048]{1,0:T(8,128)(2,1)} async-done(((bf16[32,2048]{1,0:T(8,128)(2,1)}), bf16[256,2048]{1,0:T(8,128)(2,1)}) %all-gather.23.cloned.1.call-update) | async-done | bytes 1048592 | tf_op jit(solution)/shard_map/all_gather | solution.py:129
  112.2 16.0 %all-gather.1 = bf16[8,1,256]{2,1,0:T(2,128)(2,1)S(1)} all-gather(bf16[1,1,256]{2,1,0:T(2,128)(2,1)S(1)} %reshape.244), channel_id=1, replica_groups=mesh['shard'=8,'ctx'=16] {'shard'}, dimensions={0}, use_global_device_ids=true | all-gather | bytes 4608 | tf_op jit(solution)/shard_map/all_gather | solution.py:132
  129.1 16.0 %all-gather.21.cloned.1.call-done = bf16[2048,256]{0,1:T(8,128)(2,1)} async-done(((bf16[128,256]{0,1:T(8,128)(2,1)}), bf16[2048,256]{0,1:T(8,128)(2,1)}) %all-gather.21.cloned.1.call-update) | async-done | bytes 1048592 | tf_op jit(solution)/shard_map/all_gather | solution.py:155
  147.8 32.1 %all-gather.25.cloned.1.call-done = bf16[2048,256]{1,0:T(8,128)(2,1)} async-done(((bf16[128,256]{1,0:T(8,128)(2,1)}), bf16[2048,256]{1,0:T(8,128)(2,1)}) %all-gather.25.cloned.1.call-update) | async-done | bytes 1048592 | tf_op jit(solution)/shard_map/all_gather | solution.py:156
  184.9 105.2 %all-gather.17.cloned.1.call-done = bf16[2048,2048]{1,0:T(8,128)(2,1)} async-done(((bf16[256,2048]{1,0:T(8,128)(2,1)}), bf16[2048,2048]{1,0:T(8,128)(2,1)}) %all-gather.17.cloned.1.call-update) | async-done | bytes 8388624 | tf_op jit(solution)/shard_map/all_gather | solution.py:127
  290.1 5.8 fusion.81
  297.5 47.6 %while.30 = (s32[]{:T(128)}, bf16[4,1024,64]{1,2,0:T(8,128)(2,1)}, f32[4,1024]{1,0:T(4,128)S(1)}, bf16[4,1024,64]{2,1,0:T(8,128)(2,1)}, bf16[4,2048,64]{2,1,0:T(...) while((s32[]{:T(128)}, bf16[4,1024,64]{1,2,0:T(8,128)(2,1)}, ...), condition=%wide.region_4.5_spmd.clone.clone, body=%wide.region_1.4_spmd.clone.sunk.clone | while | flops 568327168 | bytes 60373108 | solution.py:176
  303.8 5.7 fusion.163
  315.5 5.8 fusion.163
  327.3 5.7 fusion.163
  339.3 5.7 fusion.163
  347.1 52.0 %all-gather.27.cloned.1.call-done = bf16[2048,2048]{1,0:T(8,128)(2,1)} async-done(((bf16[256,2048]{1,0:T(8,128)(2,1)}), bf16[2048,2048]{1,0:T(8,128)(2,1)}) %all-gather.27.cloned.1.call-update) | async-done | bytes 8388624 | tf_op jit(solution)/shard_map/all_gather | solution.py:130
  399.1 4.9 multiply_reduce_fusion.1
  407.3 68.3 %all-gather.29.cloned.1.call-done = bf16[1024,2048]{1,0:T(8,128)(2,1)} async-done(((bf16[128,2048]{1,0:T(8,128)(2,1)}), bf16[1024,2048]{1,0:T(8,128)(2,1)}) %all-gather.29.cloned.1.call-update) | async-done | bytes 4194320 | tf_op jit(solution)/shard_map/all_gather | solution.py:181
  475.6 8.0 fusion.83
  488.4 59.1 %all-gather.31.cloned.1.call-done = bf16[1024,2048]{1,0:T(8,128)(2,1)} async-done(((bf16[128,2048]{1,0:T(8,128)(2,1)}), bf16[1024,2048]{1,0:T(8,128)(2,1)}) %all-gather.31.cloned.1.call-update) | async-done | bytes 4194320 | tf_op jit(solution)/shard_map/all_gather | solution.py:134
  547.5 8.5 multiply_convert_fusion.1
  559.5 5.3 add_convert_fusion
  564.9 81.9 %reduce-scatter.15.cloned.1.call-done = bf16[128,2048]{1,0:T(8,128)(2,1)} async-done(((bf16[1024,2048]{1,0:T(8,128)(2,1)}), bf16[128,2048]{1,0:T(8,128)(2,1)}) %reduce-scatter.15.cloned.1.call-update) | async-done | bytes 524304 | tf_op jit(solution)/shard_map/reduce_scatter | solution.py:192
  651.1 7.3 convolution_convert_fusion.6
  662.8 109.3 %while.31 = (s32[]{:T(128)}, f32[4,1024,64]{1,2,0:T(8,128)}, bf16[4,2048,64]{1,2,0:T(8,128)(2,1)}, bf16[4,2048,64]{1,2,0:T(8,128)(2,1)}, bf16[4,1024,64]{2,1,0:T...) while((s32[]{:T(128)}, f32[4,1024,64]{1,2,0:T(8,128)}, ...), condition=%wide.region_11.12_spmd.clone.clone, body=%wide.region_9.11_spmd.clone.sunk.clone | while | flops 1363344384 | bytes 154965232 | solution.py:230
  665.5 7.1 multiply_reduce_fusion.4
  672.7 8.9 multiply_convert_fusion.7
  692.8 7.1 multiply_reduce_fusion.4
  700.0 8.9 multiply_convert_fusion.7
  720.1 7.1 multiply_reduce_fusion.4
  727.2 8.9 multiply_convert_fusion.7
  747.4 7.1 multiply_reduce_fusion.4
  754.5 8.9 multiply_convert_fusion.7
  778.1 12.1 all_to_all.32
  792.3 6.4 convolution_convert_fusion
  798.7 7.5 convolution_convert_fusion.2
  815.7 18.3 %reduce-scatter.17.cloned.1.call-done = bf16[128,256]{1,0:T(8,128)(2,1)} async-done(((bf16[2048,256]{1,0:T(8,128)(2,1)}), bf16[128,256]{1,0:T(8,128)(2,1)}) %reduce-scatter.17.cloned.1.call-update) | async-done | bytes 65552
  836.5 61.5 %reduce-scatter.19.cloned.1.call-done = bf16[128,256]{1,0:T(8,128)(2,1)} async-done(((bf16[2048,256]{1,0:T(8,128)(2,1)}), bf16[128,256]{1,0:T(8,128)(2,1)}) %reduce-scatter.19.cloned.1.call-update) | async-done | bytes 65552
  902.0 6.3 all-to-all-start
  908.4 7.3 pad_maximum_fusion
  915.8 60.3 %all-gather.33.cloned.1.call-done = bf16[1024,2048]{1,0:T(8,128)(2,1)} async-done(((bf16[128,2048]{1,0:T(8,128)(2,1)}), bf16[1024,2048]{1,0:T(8,128)(2,1)}) %all-gather.33.cloned.1.call-update) | async-done | bytes 4194320 | tf_op jit(solution)/shard_map/all_gather | solution.py:140
  976.0 5.0 convolution_convert_fusion.4
  981.1 66.8 %all-gather.35.cloned.1.call-done = bf16[1024,2048]{1,0:T(8,128)(2,1)} async-done(((bf16[128,2048]{1,0:T(8,128)(2,1)}), bf16[1024,2048]{1,0:T(8,128)(2,1)}) %all-gather.35.cloned.1.call-update) | async-done | bytes 4194320 | tf_op jit(solution)/shard_map/all_gather | solution.py:215
  1053.0 149.2 %fusion.76 = (bf16[40,2048]{1,0:T(8,128)(2,1)}, bf16[136,2048]{1,0:T(8,128)(2,1)S(1)}) fusion(bf16[576,2048]{1,0:T(8,128)(2,1)} %pad_maximum_fusion.1, bf16[2112,2048]{1,0:T(8,128)(2,1)} %pad_maximum_fusion), kind=kCustom, calls=%all-reduce-scatter.2 | all-reduce-scatter fusion | flops 5767170 | bytes 11731456
  1214.3 4.9 concatenate.39
  1228.4 5.5 concatenate.40
  1236.0 5.1 fusion.86
  1243.0 65.6 %all-reduce.4 = (f32[2048]{0:T(1024)S(1)}, f32[2048]{0:T(1024)S(1)}) all-reduce(f32[2048]{0:T(1024)S(1)} %get-tuple-element.213, f32[2048]{0:T(1024)S(1)} %copy-done.27), channel_id=1, replica_groups=mesh['shard'=8,'ctx'=16] {'shard','ctx'}, use_global_device_ids=true, to_apply=%region_16.17 | all-reduce | flops 4096 | bytes 32768 | tf_op jit(solution)/shard_map/psum | solution.py:283
  1324.8 10.8 reshape.253
  1335.5 12.5 fusion.78
  (267 shorter events, 183.5 us)
Async XLA Ops:
  7.2 540.3 %copy-start = (bf16[704,2048]{1,0:T(8,128)(2,1)S(1)}, bf16[704,2048]{1,0:T(8,128)(2,1)}, u32[]{:S(2)}) copy-start(bf16[704,2048]{1,0:T(8,128)(2,1)} %param.27) | copy-start | bytes 8650756
  7.2 105.0 %copy-start.41 = (bf16[256]{0:T(256)(128)(2,1)S(1)}, bf16[256]{0:T(256)(128)(2,1)}, u32[]{:S(2)}) copy-start(bf16[256]{0:T(256)(128)(2,1)} %param.24) | copy-start | bytes 1540
  7.2 52.8 %all-gather.19.cloned.1.call-start = ((), (), s32[]{:S(2)}) async-start(), calls=%async_computation.7 | async-start | bytes 1179648 | tf_op jit(solution)/shard_map/all_gather | solution.py:128
  7.9 100.6 %all-gather.23.cloned.1.call-start = ((), (), s32[]{:S(2)}) async-start(), calls=%async_computation.9 | async-start | bytes 1179648 | tf_op jit(solution)/shard_map/all_gather | solution.py:129
  8.7 136.4 %all-gather.21.cloned.1.call-start = ((), (), s32[]{:S(2)}) async-start(), calls=%async_computation.8 | async-start | bytes 1114112 | tf_op jit(solution)/shard_map/all_gather | solution.py:155
  30.0 82.2 %copy-start.25 = (f32[8,1,256]{2,1,0:T(1,128)}, f32[8,1,256]{2,1,0:T(1,128)S(1)}, u32[]{:S(2)}) copy-start(f32[8,1,256]{2,1,0:T(1,128)S(1)} %convert_element_type.186) | copy-start | bytes 24580
  31.9 80.3 %copy-start.30 = (f32[128]{0:T(128)}, f32[128]{0:T(128)S(1)}, u32[]{:S(2)}) copy-start(f32[128]{0:T(128)S(1)} %add_rsqrt_fusion.1) | copy-start | bytes 1540
  32.6 263.3 %copy-start.19 = (f32[128,32]{0,1:T(8,128)}, f32[128,32]{0,1:T(8,128)S(1)}, u32[]{:S(2)}) copy-start(f32[128,32]{0,1:T(8,128)S(1)} %get-tuple-element.287) | copy-start | bytes 49156
  33.9 256.2 %copy-start.7 = (bf16[128,2048]{1,0:T(8,128)(2,1)}, bf16[128,2048]{1,0:T(8,128)(2,1)S(1)}, u32[]{:S(2)}) copy-start(bf16[128,2048]{1,0:T(8,128)(2,1)S(1)} %fusion.59) | copy-start | bytes 1572868
  62.4 117.5 %all-gather.25.cloned.1.call-start = ((), (), s32[]{:S(2)}) async-start(), calls=%async_computation.10 | async-start | bytes 1114112 | tf_op jit(solution)/shard_map/all_gather | solution.py:156
  110.9 179.2 %all-gather.17.cloned.1.call-start = ((), (), s32[]{:S(2)}) async-start(), calls=%async_computation.6 | async-start | bytes 9437184 | tf_op jit(solution)/shard_map/all_gather | solution.py:127
  111.5 287.6 %all-gather.27.cloned.1.call-start = ((), (), s32[]{:S(2)}) async-start(), calls=%async_computation.11 | async-start | bytes 9437184 | tf_op jit(solution)/shard_map/all_gather | solution.py:130
  112.1 363.5 %all-gather.29.cloned.1.call-start = ((), (), s32[]{:S(2)}) async-start(), calls=%async_computation.12 | async-start | bytes 4718592 | tf_op jit(solution)/shard_map/all_gather | solution.py:181
  128.2 520.9 %copy-start.22 = (f32[8,1,256]{2,1,0:T(1,128)}, f32[8,1,256]{2,1,0:T(1,128)S(1)}, u32[]{:S(2)}) copy-start(f32[8,1,256]{2,1,0:T(1,128)S(1)} %convert_element_type.187) | copy-start | bytes 24580
  297.5 101.7 %copy-start.8 = (bf16[128,2048]{1,0:T(8,128)(2,1)S(1)}, bf16[128,2048]{1,0:T(8,128)(2,1)}, u32[]{:S(2)}) copy-start(bf16[128,2048]{1,0:T(8,128)(2,1)} %param.16) | copy-start | bytes 1572868
  404.1 245.1 %copy-start.28 = (f32[128]{0:T(128)}, f32[128]{0:T(128)S(1)}, u32[]{:S(2)}) copy-start(f32[128]{0:T(128)S(1)} %add_rsqrt_fusion) | copy-start | bytes 1540
  406.0 141.4 %all-gather.31.cloned.1.call-start = ((), (), s32[]{:S(2)}) async-start(), calls=%async_computation.14 | async-start | bytes 4718592 | tf_op jit(solution)/shard_map/all_gather | solution.py:134
  406.8 240.1 %reduce-scatter.15.cloned.1.call-start = ((), (), s32[]{:S(2)}) async-start(), calls=%async_computation.15 | async-start | bytes 4718592 | tf_op jit(solution)/shard_map/reduce_scatter | solution.py:192
  475.6 8.0 copy-start.35
  475.6 8.0 copy-start.39
  547.5 8.5 copy-start.38
  564.9 269.2 %reduce-scatter.17.cloned.1.call-start = ((), (), s32[]{:S(2)}) async-start(), calls=%async_computation.20 | async-start | bytes 1114112
  649.1 9.2 copy-start.32
  651.1 7.3 copy-start.12
  665.5 7.2 copy-start.2
  681.6 6.1 copy-start.1
  692.8 7.2 copy-start.2
  708.9 6.1 copy-start.1
  720.0 7.2 copy-start.2
  747.3 7.2 copy-start.2
  774.4 123.6 %reduce-scatter.19.cloned.1.call-start = ((), (), s32[]{:S(2)}) async-start(), calls=%async_computation.21 | async-start | bytes 1114112
  776.7 199.3 %all-gather.33.cloned.1.call-start = ((), (), s32[]{:S(2)}) async-start(), calls=%async_computation.16 | async-start | bytes 4718592 | tf_op jit(solution)/shard_map/all_gather | solution.py:140
  777.3 270.5 %all-gather.35.cloned.1.call-start = ((), (), s32[]{:S(2)}) async-start(), calls=%async_computation.17 | async-start | bytes 4718592 | tf_op jit(solution)/shard_map/all_gather | solution.py:215
  778.1 531.8 %reduce-scatter.13.cloned.1.call-start = ((), (), s32[]{:S(2)}) async-start(), calls=%async_computation.13 | async-start | bytes 4718592 | tf_op jit(solution)/shard_map/reduce_scatter | solution.py:198
  798.7 7.5 copy-start.36
  798.7 7.5 copy-start.43
  815.7 100.1 %copy-start.11 = (bf16[128,32,64]{0,2,1:T(8,128)(2,1)}, bf16[128,32,64]{0,2,1:T(8,128)(2,1)S(1)}, u32[]{:S(2)}) copy-start(bf16[128,32,64]{0,2,1:T(8,128)(2,1)S(1)} %maximum_convert_fusion) | copy-start | bytes 1572868
  902.0 74.0 %all-to-all-start = ((bf16[128,8,320]{0,2,1:T(8,128)(2,1)}), bf16[128,8,320]{0,2,1:T(8,128)(2,1)}, u32[]{:S(2)}, u32[]{:S(2)}) async-start(bf16[128,8,320]{0,2,1:T(8,128)(2,1)} %pad_maximum_fusion.2), calls=%async_computation.2 | async-start | bytes 1310720 | tf_op jit(solution)/shard_map/all_to_all | solution.py:95
  908.4 405.3 %all-gather.37.cloned.1.call-start = ((), (), s32[]{:S(2)}) async-start(), calls=%async_computation.18 | async-start | bytes 2785280 | tf_op jit(solution)/shard_map/all_gather | solution.py:102
  976.0 71.8 %copy-start.18 = (bf16[8,128,256]{2,1,0:T(8,128)(2,1)S(1)}, bf16[8,128,256]{2,1,0:T(8,128)(2,1)}, u32[]{:S(2)}) copy-start(bf16[8,128,256]{2,1,0:T(8,128)(2,1)} %copy.73) | copy-start | bytes 1572868
  1053.0 159.4 %copy-start.34 = (u32[128]{0:T(128)S(1)}, u32[128]{0:T(128)}, u32[]{:S(2)}) copy-start(u32[128]{0:T(128)} %constant.90) | copy-start | bytes 1540
  1202.2 12.2 collective-permute-start
  1208.1 6.2 collective-permute-start.1
  1220.9 103.9 %all-gather.39.cloned.1.call-start = ((), (), s32[]{:S(2)}) async-start(), calls=%async_computation.19 | async-start | bytes 9469952 | tf_op jit(solution)/shard_map/all_gather | solution.py:102
  1221.0 7.4 collective-permute-start.2
  1241.1 68.7 %copy-start.23 = (f32[8,1,256]{2,1,0:T(1,128)S(1)}, f32[8,1,256]{2,1,0:T(1,128)}, u32[]{:S(2)}) copy-start(f32[8,1,256]{2,1,0:T(1,128)} %copy-done.22) | copy-start | bytes 24580
  1241.1 68.7 %copy-start.29 = (f32[128]{0:T(128)S(1)}, f32[128]{0:T(128)}, u32[]{:S(2)}) copy-start(f32[128]{0:T(128)} %copy-done.28) | copy-start | bytes 1540
  1241.1 68.7 %copy-start.33 = (f32[128]{0:T(128)S(1)}, f32[128]{0:T(128)}, u32[]{:S(2)}) copy-start(f32[128]{0:T(128)} %copy-done.32) | copy-start | bytes 1540
  (33 other events, 132.5 us)
Sparse Core Ops, SparseCore 0:
  10.4 49.5 all-gather.18
  62.4 46.1 all-gather.22
  110.8 34.2 all-gather.20
  147.2 32.6 all-gather.24
  182.1 107.9 all-gather.16
  292.3 106.7 all-gather.26
  406.2 69.4 all-gather.28
  478.0 69.4 all-gather.30
  565.0 81.8 reduce-scatter.14
  774.5 59.4 reduce-scatter.16
  837.1 60.8 reduce-scatter.18
  900.2 75.8 all-gather.32
  978.4 69.4 all-gather.34
  1052.1 114.1 reduce-scatter.12
  1221.0 34.9 all-gather.36
  1258.2 55.4 all-gather.38

commit v2 on v1

v2 whole, which is shorter than its diff:
```python
import functools

import jax
import jax.numpy as jnp
from jax import lax
from jax.experimental import pallas as pl
from jax.experimental.pallas import tpu as pltpu
from jax.sharding import PartitionSpec as P

D = 2048
HEADS = 32
KV_HEADS = 4
HEAD = 64
LANES = 128

EPS = 1e-05
BASE = 10000.0
NEG = -1e30
F32 = jnp.float32
LOW = jnp.bfloat16
MESH = pl.DeviceIdType.MESH
VMEM_LIMIT = 56 * 1024 * 1024


def times(left, right):
    return jnp.dot(left, right, preferred_element_type=F32)


def times_transposed(left, right):
    return lax.dot_general(left, right, (((1,), (1,)), ((), ())), preferred_element_type=F32)


def transposed_times(left, right):
    return lax.dot_general(left, right, (((0,), (0,)), ((), ())), preferred_element_type=F32)


def at(axis, ring, pair, core=0):
    index = lax.axis_index(axis)
    cores = 2 if axis == "ctx" else 1
    ring_at = lax.rem(index // (2 * cores) + ring % 4, 4)
    pair_at = lax.rem(lax.rem(index // cores, 2) + pair, 2)
    core_at = lax.rem(lax.rem(index, cores) + core, cores)
    return (ring_at * 2 + pair_at) * cores + core_at


def chip(axis, ring=0, pair=0):
    return at(axis, ring, pair) // (2 if axis == "ctx" else 1)


class Link:
    def __init__(self, send_sems, recv_sems, local_sems):
        self.send_sems, self.recv_sems, self.local_sems = send_sems, recv_sems, local_sems
        self.sent, self.kept = [], []

    def greet(self, offsets):
        barrier = pltpu.get_barrier_semaphore()
        for axis, ring, pair, core in offsets:
            pl.semaphore_signal(
                barrier, inc=1, device_id={axis: at(axis, ring, pair, core)}, device_id_type=MESH
            )
        pl.semaphore_wait(barrier, len(offsets))

    def send(self, source, target, axis, ring, pair, core=0):
        number = len(self.sent)
        copy = pltpu.make_async_remote_copy(
            src_ref=source,
            dst_ref=target,
            send_sem=self.send_sems.at[number],
            recv_sem=self.recv_sems.at[number],
            device_id={axis: at(axis, ring, pair, core)},
            device_id_type=MESH,
        )
        copy.start()
        self.sent.append(copy)
        return copy

    def keep(self, source, target):
        copy = pltpu.make_async_copy(source, target, self.local_sems.at[len(self.kept)])
        copy.start()
        self.kept.append(copy)
        return copy

    def kept_now(self, copy):
        copy.wait()
        self.kept = [None if other is copy else other for other in self.kept]

    def finish(self):
        for copy in self.kept:
            if copy is not None:
                copy.wait()
        for copy in self.sent:
            copy.wait_send()


NEAR = [(1, 0), (3, 0), (0, 1)]
ALL = [(r, p) for r in range(4) for p in range(2) if (r, p) != (0, 0)]
near = lambda axis: [(axis, r, p, 0) for r, p in NEAR]
whole = lambda axis: [(axis, r, p, 0) for r, p in ALL]
SIBLING = [("ctx", 0, 0, 1)]


def run(*jobs):
    jobs = list(jobs)
    while jobs:
        for job in list(jobs):
            if next(job, "end") == "end":
                jobs.remove(job)


def gather_job(link, axis, own, slot, share=None):
    me, pair = chip(axis), chip(axis, 0, 1)
    sharing = lambda index: share(index, slot(index)) if share else None
    kept = link.keep(own, slot(me))
    to_pair = link.send(own, slot(me), axis, 0, 1)
    down = link.send(own, slot(me), axis, -1, 0)
    up = link.send(own, slot(me), axis, 1, 0)
    if share:
        share(me, own)
    yield
    to_pair.wait_recv()
    pair_down = link.send(slot(pair), slot(pair), axis, -1, 0)
    pair_up = link.send(slot(pair), slot(pair), axis, 1, 0)
    sharing(pair)
    yield
    down.wait_recv()
    next_one = chip(axis, 1, 0)
    far_down = link.send(slot(next_one), slot(next_one), axis, -1, 0)
    sharing(next_one)
    yield
    up.wait_recv()
    sharing(chip(axis, -1, 0))
    yield
    pair_up.wait_recv()
    last_pair = chip(axis, -1, 1)
    far_up = link.send(slot(last_pair), slot(last_pair), axis, 1, 0)
    sharing(last_pair)
    yield
    pair_down.wait_recv()
    sharing(chip(axis, 1, 1))
    yield
    far_down.wait_recv()
    sharing(chip(axis, 2, 0))
    yield
    far_up.wait_recv()
    sharing(chip(axis, 2, 1))
    link.kept_now(kept)


def add_rows(target, terms, step=16):
    def body(i, _):
        rows = pl.ds(pl.multiple_of(i * step, step), step)
        total = terms[0][rows, :].astype(F32)
        for term in terms[1:]:
            total = total + term[rows, :].astype(F32)
        target[rows, :] = total.astype(target.dtype)
        return 0

    lax.fori_loop(0, target.shape[0] // step, body, 0)


def scatter_job(link, axis, part, landing, work, result):
    here = lambda ring, pair: part(chip(axis, ring, pair))
    to_next = link.send(here(2, 0), landing.at[0], axis, 1, 0)
    to_last = link.send(here(2, 1), landing.at[1], axis, -1, 0)
    pair_up = link.send(here(1, 1), landing.at[2], axis, 1, 0)
    mine_down = link.send(here(3, 0), landing.at[3], axis, -1, 0)
    yield
    to_last.wait_recv()
    add_rows(work.at[0], [here(3, 1), landing.at[1]])
    pair_down = link.send(work.at[0], landing.at[4], axis, -1, 0)
    yield
    to_next.wait_recv()
    add_rows(work.at[1], [here(1, 0), landing.at[0]])
    mine_up = link.send(work.at[1], landing.at[5], axis, 1, 0)
    yield
    pair_up.wait_recv()
    yield
    mine_down.wait_recv()
    yield
    pair_down.wait_recv()
    add_rows(work.at[2], [here(0, 1), landing.at[2], landing.at[4]])
    across = link.send(work.at[2], landing.at[6], axis, 0, 1)
    yield
    mine_up.wait_recv()
    yield
    across.wait_recv()
    add_rows(result, [here(0, 0), landing.at[3], landing.at[5], landing.at[6]])


def exchange_job(link, axis, part, slot):
    me = chip(axis)
    kept = link.keep(part(me), slot(me))
    copies = [link.send(part(chip(axis, r, p)), slot(me), axis, r, p) for r, p in ALL]
    yield
    for copy in copies:
        copy.wait_recv()
        yield
    link.kept_now(kept)


ANY = pl.BlockSpec(memory_space=pl.ANY)
INSIDE = pl.BlockSpec(memory_space=pltpu.VMEM)


def comm_call(kernel, number, inputs, in_specs, outputs, out_specs, scratch=()):
    sems = [pltpu.SemaphoreType.DMA((64,)), pltpu.SemaphoreType.DMA((64,)), pltpu.SemaphoreType.DMA((8,))]

    def body(*refs):
        link = Link(*refs[-3:])
        kernel(link, *refs[:-3])
        link.finish()

    return pl.pallas_call(
        body,
        out_shape=outputs,
        in_specs=in_specs,
        out_specs=out_specs,
        scratch_shapes=[*scratch, *sems],
        compiler_params=pltpu.CompilerParams(
            collective_id=number, has_side_effects=True, vmem_limit_bytes=VMEM_LIMIT
        ),
    )(*inputs)


shape = jax.ShapeDtypeStruct


def front_kernel(link, tokens, small, kv_send, w_out, token_rows, smalls, kv_other, out_full):
    link.greet(whole("shard") + [("ctx", 1, 0, 0), ("ctx", 3, 0, 0)] + SIBLING)
    core = lax.rem(lax.axis_index("ctx"), 2)
    ring = lax.axis_index("ctx") // 4

    def strip(ring_index, core_index):
        return pl.ds(pl.multiple_of((core_index * 4 + ring_index) * 32, 32), 32)

    mine = strip(ring, core)

    def out_job():
        yield from gather_job(link, "shard", w_out.at[mine], lambda i: out_full.at[i, mine])
        block = lambda rows, first=0, count=8: out_full.at[pl.ds(first, count), rows]
        up = link.send(block(mine), block(mine), "ctx", 1, 0)
        down = link.send(block(mine), block(mine), "ctx", -1, 0)
        sibs = [link.send(block(mine), block(mine), "ctx", 0, 0, 1)]
        yield
        up.wait_recv()
        rows = strip(lax.rem(ring + 3, 4), core)
        far_up = link.send(block(rows, 0, 4), block(rows, 0, 4), "ctx", 1, 0)
        sibs.append(link.send(block(rows), block(rows), "ctx", 0, 0, 1))
        yield
        down.wait_recv()
        rows = strip(lax.rem(ring + 1, 4), core)
        far_down = link.send(block(rows, 4, 4), block(rows, 4, 4), "ctx", -1, 0)
        sibs.append(link.send(block(rows), block(rows), "ctx", 0, 0, 1))
        yield
        far_up.wait_recv()
        far_down.wait_recv()
        rows = strip(lax.rem(ring + 2, 4), core)
        sibs.append(link.send(block(rows), block(rows), "ctx", 0, 0, 1))
        yield
        for copy in sibs:
            copy.wait_recv()

    def kv_job():
        copy = link.send(kv_send, kv_other, "shard", 0, 1)
        yield
        copy.wait_recv()

    run(
        exchange_job(link, "shard", lambda i: small, lambda i: smalls.at[i]),
        kv_job(),
        out_job(),
        gather_job(link, "shard", tokens, lambda i: token_rows.at[i]),
    )


def qkv_kernel(link, queries, kv, queries_got, kv_all, kv_got, kv_own):
    link.greet(whole("shard") + near("ctx") + SIBLING)
    core = lax.rem(lax.axis_index("ctx"), 2)

    def kv_job():
        yield from exchange_job(link, "shard", lambda i: kv.at[i], lambda i: kv_got.at[i])
        for head in range(KV_HEADS):
            kv_own[:, head * 128 : (head + 1) * 128] = kv_got[2 * head] + kv_got[2 * head + 1]
        slot = lambda i: kv_all.at[i * 2 + core]
        sibs = []

        def share(index, block):
            sibs.append(link.send(block, slot(index), "ctx", 0, 0, 1))

        yield from gather_job(link, "ctx", kv_own, slot, share)
        for copy in sibs:
            copy.wait_recv()

    run(kv_job(), exchange_job(link, "shard", lambda i: queries.at[i], lambda i: queries_got.at[i]))


def gather_kernel(link, own, slots):
    link.greet(near("shard"))
    run(gather_job(link, "shard", own, lambda i: slots.at[i]))


def reduced(link, theirs, mine, from_sibling, landing, work, summed):
    copy = link.send(theirs, from_sibling, "ctx", 0, 0, 1)
    yield
    copy.wait_recv()
    add_rows(from_sibling, [mine, from_sibling])
    columns = lambda i: from_sibling.at[:, pl.ds(pl.multiple_of(i * LANES, LANES), LANES)]
    yield from scatter_job(link, "ctx", columns, landing, work, summed)


def spread(link, summed, full):
    core = lax.rem(lax.axis_index("ctx"), 2)
    slot = lambda i: full.at[:, pl.ds(pl.multiple_of((core * 8 + i) * LANES, LANES), LANES)]
    sibs = []

    def share(index, block):
        sibs.append(link.send(block, slot(index), "ctx", 0, 0, 1))

    yield from gather_job(link, "ctx", summed, slot, share)
    for copy in sibs:
        copy.wait_recv()


def middle_kernel(link, parts, theirs, mine, result, summed, land_a, work_a, sib, land_b, work_b):
    link.greet(near("shard") + near("ctx") + SIBLING)
    run(
        scatter_job(link, "shard", lambda i: parts.at[i], land_a, work_a, result),
        reduced(link, theirs, mine, sib, land_b, work_b, summed),
    )


def back_kernel(link, kv_parts, summed, parts, queries, attended, kv_grad, full, down, query_cols, attended_cols,
                sib, land_k, work_k, land_d, work_d):
    link.greet(whole("shard") + near("ctx") + SIBLING)
    core = lax.rem(lax.axis_index("ctx"), 2)

    def kv_job():
        copies = [
            link.send(kv_parts.at[i * 2 + 1 - core], sib.at[i], "ctx", 0, 0, 1) for i in range(8)
        ]
        yield
        for i, copy in enumerate(copies):
            copy.wait_recv()
            add_rows(sib.at[i], [sib.at[i], kv_parts.at[i * 2 + core]])
        yield from scatter_job(link, "ctx", lambda i: sib.at[i], land_k, work_k, kv_grad)

    columns = lambda ref: lambda i: ref.at[:, pl.ds(pl.multiple_of(i * 256, 256), 256)]
    run(
        kv_job(),
        exchange_job(link, "shard", columns(queries), lambda i: query_cols.at[i]),
        exchange_job(link, "shard", columns(attended), lambda i: attended_cols.at[i]),
        scatter_job(link, "shard", lambda i: parts.at[i], land_d, work_d, down),
        spread(link, summed, full),
    )


def swap_kernel(link, parts, slots):
    link.greet(whole("shard"))
    run(exchange_job(link, "shard", lambda i: parts.at[i], lambda i: slots.at[i]))


def last_kernel(link, parts, theirs, mine, gains, result, full, gain_sum,
                land_a, work_a, sib, land_b, work_b, summed, gain_land, gain_work, gain_ctx):
    link.greet(whole("shard") + whole("ctx") + SIBLING)

    def weight_job():
        yield from reduced(link, theirs, mine, sib, land_b, work_b, summed)
        yield from spread(link, summed, full)

    def gain_job():
        yield from exchange_job(link, "shard", lambda i: gains.at[i], lambda i: gain_land.at[i])
        gain_work[0] = sum(gain_land[i] for i in range(8))
        copy = link.send(gain_work.at[0], gain_work.at[1], "ctx", 0, 0, 1)
        yield
        copy.wait_recv()
        gain_work[2] = gain_work[0] + gain_work[1]
        copies = [
            link.send(gain_work.at[2], gain_ctx.at[i], "ctx", r, p) for i, (r, p) in enumerate(ALL)
        ]
        yield
        for copy in copies:
            copy.wait_recv()
        gain_sum[...] = gain_work[2] + sum(gain_ctx[i] for i in range(7))

    run(
        gain_job(),
        scatter_job(link, "shard", lambda i: parts.at[i], land_a, work_a, result),
        weight_job(),
    )


def rope_tables(places, width):
    half = width // 2
    freqs = BASE ** (-(jnp.arange(half).astype(F32) * 2.0 / width))
    angles = places.astype(F32)[:, None] * freqs[None, :]
    return jnp.cos(angles), jnp.sin(angles)


def wide_tables(places, heads):
    cosine, sine = rope_tables(places, HEAD)
    return (
        jnp.tile(jnp.concatenate([cosine, cosine], axis=1), (1, heads)),
        jnp.tile(jnp.concatenate([-sine, sine], axis=1), (1, heads)),
    )


def swap_halves(values):
    half = HEAD // 2
    lane = lax.broadcasted_iota(jnp.int32, values.shape, 1) % HEAD
    return jnp.where(lane < half, jnp.roll(values, -half, 1), jnp.roll(values, half, 1))


def swap_rows(weight):
    return weight.reshape(-1, 2, HEAD // 2, D)[:, ::-1].reshape(weight.shape)


def rms_forward(values, gain):
    inverse = lax.rsqrt(jnp.mean(values * values, axis=-1, keepdims=True) + EPS)
    return (values * inverse * gain, inverse)


def rms_backward(values, inverse, gain, grads):
    scaled = grads * gain
    return inverse * scaled - values * inverse * inverse * inverse * jnp.mean(
        scaled * values, axis=-1, keepdims=True
    )


def attend(queries, kv_all, places, own_places):
    rows = own_places.shape[0]
    heads = queries.reshape(4, 2, rows, 4, HEAD).transpose(0, 1, 3, 2, 4).reshape(4, -1, HEAD)
    kv = kv_all.reshape(-1, KV_HEADS, 2, HEAD).transpose(2, 1, 0, 3)
    allowed = jnp.tile(own_places, 8)[:, None] >= places[None, :]

    def head_forward(operands):
        query_one, key_one, value_one = operands
        scores = jnp.where(allowed, times_transposed(query_one, key_one) * HEAD**-0.5, NEG)
        largest = jnp.max(scores, axis=-1, keepdims=True)
        exps = jnp.exp(scores - largest)
        totals = jnp.sum(exps, axis=-1, keepdims=True)
        probs = (exps / totals).astype(LOW)
        return (times(probs, value_one), (largest + jnp.log(totals))[:, 0])

    mixed, log_totals = lax.map(head_forward, (heads, kv[0], kv[1]))
    attended = mixed.reshape(4, 8, rows, HEAD).transpose(2, 0, 1, 3).reshape(rows, D).astype(LOW)
    return attended, (heads, log_totals)


def attend_back(kept, attended, attended_grad, kv_all, places, own_places):
    heads, log_totals = kept
    rows = own_places.shape[0]
    kv = kv_all.reshape(-1, KV_HEADS, 2, HEAD).transpose(2, 1, 0, 3)
    grads = attended_grad.reshape(rows, 4, 8, HEAD).transpose(1, 2, 0, 3).reshape(4, -1, HEAD)
    allowed = jnp.tile(own_places, 8)[:, None] >= places[None, :]
    scale = HEAD**-0.5

    def head_backward(operands):
        query_one, key_one, value_one, grad_one, log_one = operands
        scores = jnp.where(allowed, times_transposed(query_one, key_one) * scale, NEG)
        probs = jnp.exp(scores - log_one[:, None])
        prob_grad = times_transposed(grad_one, value_one)
        inner_sum = jnp.sum(probs * prob_grad, axis=-1, keepdims=True)
        score_grad = (probs * (prob_grad - inner_sum)).astype(LOW)
        query_grad = times(score_grad, key_one) * scale
        key_grad = transposed_times(score_grad, query_one) * scale
        value_grad = transposed_times(probs.astype(LOW), grad_one)
        return (query_grad, jnp.concatenate([key_grad, value_grad], axis=1).astype(LOW))

    query_grads, kv_grads = lax.map(head_backward, (heads, kv[0], kv[1], grads, log_totals))
    query_grads = query_grads.reshape(4, 8, rows, HEAD).transpose(2, 0, 1, 3).reshape(rows, D)
    return query_grads, kv_grads.transpose(1, 0, 2).reshape(16, rows, 512)


def local(
    tokens,
    positions,
    out_grad,
    attn_gain,
    w_query,
    w_key,
    w_value,
    w_out,
    ffn_gain,
    w_gate,
    w_up,
    w_down,
):
    rows = tokens.shape[0]
    shard, ctx = lax.axis_index("shard"), lax.axis_index("ctx")
    shard_pair, core = shard % 2, ctx % 2
    score_scale = HEAD ** (-0.5)
    places = positions[0]
    own_places = lax.dynamic_slice_in_dim(places, ctx * rows, rows)
    blocks = lambda m: m.reshape(8, rows, -1)

    small = jnp.stack(
        [attn_gain, ffn_gain, jnp.concatenate([own_places // 64, own_places % 64]).astype(LOW)]
    )
    small = jnp.concatenate([small, jnp.zeros((13, 256), LOW)], axis=0)
    out_grad_rows = lax.all_gather(out_grad, "shard", axis=0, tiled=True)
    token_rows, smalls, kv_other, out_full = comm_call(
        front_kernel,
        0,
        [tokens, small, jnp.where(shard_pair == 0, w_value, w_key), w_out],
        [ANY] * 4,
        [shape((8, rows, D), LOW), shape((8, 16, 256), LOW), shape((32, D), LOW), shape((8, 256, D), LOW)],
        [ANY] * 4,
    )
    token_rows, out_full = token_rows.reshape(-1, D), out_full.reshape(D, D)
    gain_one = smalls[:, 0].reshape(-1).astype(F32)
    gain_two = smalls[:, 1].reshape(-1).astype(F32)
    place_rows = (smalls[:, 2, :rows].astype(F32) * 64.0 + smalls[:, 2, rows:].astype(F32)).reshape(-1)
    nothing = jnp.zeros((64, D), LOW)
    w_first = jnp.where(
        shard_pair == 0,
        jnp.concatenate([w_query, w_key, kv_other, nothing], axis=0),
        jnp.concatenate([w_query, nothing, kv_other, w_value], axis=0),
    )

    inputs_rows = token_rows.astype(F32)
    normed, inverse_rows = rms_forward(inputs_rows, gain_one)
    normed_rows = normed.astype(LOW)
    first = times_transposed(normed_rows, w_first)
    turned = times_transposed(normed_rows, swap_rows(w_first[:320]))
    cosine, sine = wide_tables(place_rows, 5)
    rotated = first[:, :320] * cosine + turned * sine
    queries = rotated[:, :256].astype(LOW)
    plain = jnp.where(shard_pair == 1, first[:, 256:320], rotated[:, 256:])
    kv_part = jnp.concatenate([plain, first[:, 320:]], axis=1).astype(LOW)
    queries, kv_all = comm_call(
        qkv_kernel,
        1,
        [blocks(queries), blocks(kv_part)],
        [ANY] * 2,
        [shape((8, rows, 256), LOW), shape((16, rows, 512), LOW)],
        [ANY] * 2,
        [pltpu.VMEM((8, rows, 128), LOW), pltpu.VMEM((rows, 512), LOW)],
    )

    attended, for_back = attend(queries, kv_all, places, own_places)

    inputs = tokens.astype(F32)
    hidden_state = inputs + times(attended, out_full)
    normed_two, inverse_two = rms_forward(hidden_state, gain_two)
    (normed_two_rows,) = comm_call(
        gather_kernel, 2, [normed_two.astype(LOW)], [ANY], [shape((8, rows, D), LOW)], [ANY]
    )
    normed_two_rows = normed_two_rows.reshape(-1, D)

    gate = times_transposed(normed_two_rows, w_gate)
    up_part = times_transposed(normed_two_rows, w_up)
    inner_grad = times_transposed(out_grad_rows, w_down)
    sigmoid = jax.nn.sigmoid(gate)
    activated = gate * sigmoid
    inner = (activated * up_part).astype(LOW)
    gate_grad = (inner_grad * up_part * sigmoid * (1.0 + gate * (1.0 - sigmoid))).astype(LOW)
    up_grad = (inner_grad * activated).astype(LOW)
    normed_two_parts = (times(gate_grad, w_gate) + times(up_grad, w_up)).astype(LOW)
    down_parts = times(inner, w_down).astype(LOW)

    def halves(terms):
        def one(which):
            cut = lambda m: lax.dynamic_slice_in_dim(m, which * 1024, 1024, axis=1)
            return jnp.concatenate(
                [transposed_times(left, cut(right)).astype(LOW) for left, right in terms], axis=0
            )

        return one(1 - core), one(core)

    ff = w_gate.shape[0]
    theirs, mine = halves(
        [(gate_grad, normed_two_rows), (up_grad, normed_two_rows), (inner, out_grad_rows)]
    )
    vmem = lambda count, *dims: pltpu.VMEM((count, *dims), LOW)
    normed_two_grad, summed = comm_call(
        middle_kernel,
        3,
        [blocks(normed_two_parts), theirs, mine],
        [INSIDE, ANY, INSIDE],
        [shape((rows, D), F32), shape((3 * ff, LANES), LOW)],
        [INSIDE, INSIDE],
        [
            vmem(7, rows, D),
            vmem(3, rows, D),
            pltpu.VMEM((3 * ff, 1024), LOW),
            vmem(7, 3 * ff, LANES),
            vmem(3, 3 * ff, LANES),
        ],
    )

    gain_two_part = jnp.sum(normed_two_grad * hidden_state * inverse_two, axis=0)
    hidden_grad = out_grad.astype(F32) + rms_backward(
        hidden_state, inverse_two, gain_two, normed_two_grad
    )
    hidden_low = hidden_grad.astype(LOW)
    hidden_rows = lax.all_gather(hidden_low, "shard", axis=0, tiled=True)
    attended_grad = times_transposed(hidden_low, out_full).astype(LOW)
    query_grads, kv_parts = attend_back(for_back, attended, attended_grad, kv_all, places, own_places)

    cosine_own, sine_own = wide_tables(own_places, HEADS)
    turn_back = lambda v: v * cosine_own[:, : v.shape[1]] - swap_halves(v) * sine_own[:, : v.shape[1]]
    query_pre_grad = turn_back(query_grads).astype(LOW)
    kv_grad, ffn_full, down_sum, query_cols, attended_cols = comm_call(
        back_kernel,
        4,
        [kv_parts, summed, blocks(down_parts), query_pre_grad, attended],
        [INSIDE, INSIDE, INSIDE, ANY, ANY],
        [
            shape((rows, 512), F32),
            shape((3 * ff, D), LOW),
            shape((rows, D), F32),
            shape((8, rows, 256), LOW),
            shape((8, rows, 256), LOW),
        ],
        [INSIDE, ANY, INSIDE, ANY, ANY],
        [vmem(8, rows, 512), vmem(7, rows, 512), vmem(3, rows, 512), vmem(7, rows, D), vmem(3, rows, D)],
    )
    outputs = (hidden_state + down_sum).astype(LOW)
    gate_wgrad, up_wgrad, down_wgrad = (
        ffn_full[i * ff : (i + 1) * ff].astype(F32) for i in range(3)
    )

    by_head = kv_grad.reshape(rows, KV_HEADS, 2 * HEAD)
    key_grad = turn_back(by_head[:, :, :HEAD].reshape(rows, 256)).astype(LOW)
    value_grad = by_head[:, :, HEAD:].reshape(rows, 256).astype(LOW)
    kv_factors = jnp.concatenate(
        [key_grad.reshape(rows, 8, 32), value_grad.reshape(rows, 8, 32), jnp.zeros((rows, 8, 64), LOW)],
        axis=2,
    ).transpose(1, 0, 2)
    (kv_cols,) = comm_call(
        swap_kernel, 5, [kv_factors], [ANY], [shape((8, rows, 128), LOW)], [ANY]
    )
    query_cols, attended_cols = query_cols.reshape(-1, 256), attended_cols.reshape(-1, 256)
    kv_cols = kv_cols.reshape(-1, 128)
    kv_weights = jnp.concatenate([w_key, w_value, jnp.zeros((64, D), LOW)], axis=0)
    normed_parts = times(query_cols, w_query) + times(kv_cols, kv_weights)
    gain_one_part = jnp.sum(normed_parts * inputs_rows * inverse_rows, axis=0)
    theirs, mine = halves(
        [(query_cols, normed_rows), (kv_cols[:, :64], normed_rows), (attended_cols, hidden_rows)]
    )
    gains = jnp.stack([gain_one_part, gain_two_part]).reshape(2, 8, 256).transpose(1, 0, 2)
    gains = jnp.concatenate([gains, jnp.zeros((8, 6, 256), F32)], axis=1)
    normed_grad, attn_full, gain_sum = comm_call(
        last_kernel,
        6,
        [blocks(normed_parts.astype(LOW)), theirs, mine, gains],
        [INSIDE, ANY, INSIDE, INSIDE],
        [shape((rows, D), F32), shape((576, D), LOW), shape((8, 256), F32)],
        [INSIDE, ANY, INSIDE],
        [
            vmem(7, rows, D),
            vmem(3, rows, D),
            pltpu.VMEM((576, 1024), LOW),
            vmem(7, 576, LANES),
            vmem(3, 576, LANES),
            pltpu.VMEM((576, LANES), LOW),
            pltpu.VMEM((8, 8, 256), F32),
            pltpu.VMEM((3, 8, 256), F32),
            pltpu.VMEM((7, 8, 256), F32),
        ],
    )
    inverse_one = lax.dynamic_slice_in_dim(inverse_rows, shard * rows, rows)
    input_grad = hidden_grad + rms_backward(inputs, inverse_one, gain_one, normed_grad)
    query_wgrad, key_wgrad, value_wgrad, out_wgrad = (
        attn_full[a:b].astype(F32) for a, b in ((0, 256), (256, 288), (288, 320), (320, 576))
    )
    return (
        outputs,
        input_grad,
        gain_sum[0],
        query_wgrad,
        key_wgrad,
        value_wgrad,
        out_wgrad,
        gain_sum[1],
        gate_wgrad,
        up_wgrad,
        down_wgrad,
    )


def solution(mesh):
    rows = P(("shard", "ctx"), None)
    matrix = P("shard", None)
    vector = P("shard")
    in_specs = (rows, matrix, rows, vector, matrix, matrix, matrix, matrix, vector) + (matrix,) * 3
    out_specs = (rows, rows, vector, matrix, matrix, matrix, matrix, vector) + (matrix,) * 3
    return jax.shard_map(local, mesh=mesh, in_specs=in_specs, out_specs=out_specs, check_vma=False)
```

time: 1370 us -> 787 us (0.57)
  waiting for transfers between devices: 702 us -> 0.7 us
  Pallas kernels: 0 us -> 415 us
  blocking collectives: 263 us -> 0 us
  other arithmetic: 73 us -> 106 us
  matrix products: 197 us -> 174 us
  starting transfers between devices: 20.1 us -> 0.08 us
    pallas_call x0 -> x7, Pallas kernels: none -> 415 us  [comm_call(): pl.pallas_call(body, out_shape=outputs, in_specs=in_specs, out_specs=out_...]
    all_gather x10 -> x0, waiting for transfers between devices: 406 us -> none  [the longest x1 105 us: local(): lax.all_gather(w_query, 'shard', axis=0, tiled=True)]
    unnamed x1 -> x0, blocking collectives: 149 us -> none
    unnamed x21 -> x2, waiting for transfers between devices: 88.4 us -> 0.7 us
    reduce_scatter x2 -> x0, waiting for transfers between devices: 81.9 us -> none  [the longest x1 81.9 us: local(): lax.psum_scatter((times(gate_grad, w_gate) + times(up_grad, w_up)).astype...]
    all_gather x1, waiting for transfers between devices: 66.8 us -> 0.01 us  [local(): hidden_rows = lax.all_gather(hidden_low, 'shard', axis=0, tiled=True)]
    psum x1 -> x0, blocking collectives: 65.6 us -> none  [local(): lax.psum((gain_one_grad, gain_two_grad), ('shard', 'ctx'))]
    all_gather x1, waiting for transfers between devices: 59.1 us -> 0.01 us  [local(): out_grad_rows = lax.all_gather(out_grad, 'shard', axis=0, tiled=True)]
  transfers between devices with their start and end apart: 20 -> 2, of which waited for: 15 -> 0; matrix products, arithmetic and copies ran while one was open for 24% -> 36% of each run, Pallas kernels for 0% -> 34%
where the time goes in v2:
time: 787 us; the launch traced here: 783 us
  Pallas kernels  415 us (53%)
  matrix products  174 us (22%)
  other arithmetic  106 us (13%)
  local copies, waits for them, and re-layouts  70.3 us (9%)
  between operations  15.3 us (2%)
    pallas_call x7, Pallas kernels, comm_call(): pl.pallas_call(body, out_shape=outputs, in_specs=in_specs, out_specs=out_...  415 us
    dot_general x18, matrix products, times_transposed(): lax.dot_general(left, right, (((1,), (1,)), ((), ())), preferred_element_...  74.1 us
    dot_general x14, matrix products, times(): return jnp.dot(left, right, preferred_element_type=F32)  54.1 us
    dot_general x20, matrix products, transposed_times(): lax.dot_general(left, right, (((0,), (0,)), ((), ())), preferred_element_...  45.9 us
    convert_element_type x4, other arithmetic, head_backward(): score_grad = (probs * (prob_grad - inner_sum)).astype(LOW)  34.9 us
    unnamed x139, local copies, waits for them, and re-layouts  20.3 us
  transfers between devices with their start and end apart: 2, of which 0 were waited for; matrix products, arithmetic and copies ran while one was open for 36% of the time, Pallas kernels for 34%

profile of v2, /device:TPU:1, one launch (start us, length us, event | category | flops | bytes accessed | tf_op | source)
XLA Modules:
  0.0 782.8 jit_solution(7824067999996356334)
XLA Ops:
  13.5 111.4 %shard_map.203 = (bf16[8,128,2048]{2,1,0:T(8,128)(2,1)}, bf16[8,16,256]{2,1,0:T(8,128)(2,1)}, bf16[32,2048]{1,0:T(8,128)(2,1)}, bf16[8,256,2048]{2,1,0:T(8,128)(2,1)}) custom-call(bf16[128,2048]{1,0:T(8,128)(2,1)} %refs_0_.1, bf16[16,256]{1,0:T(8,128)(2,1)} %maximum_maximum_fusion.refs_1_, bf16[32,2048]{1,0:T(8,128)(2,1)} %broadcast_select_fusion.refs_2_, ...), custom_call_target="tpu_custom_call" | custom-call | tf_op jit(solution)/shard_map/pallas_call | solution.py:213
  128.0 3.2 fusion.52
  131.3 4.7 fusion.104
  149.0 3.4 fusion.107
  159.6 32.0 %shard_map.204 = (bf16[8,128,256]{2,1,0:T(8,128)(2,1)}, bf16[16,128,512]{2,1,0:T(8,128)(2,1)}) custom-call(bf16[8,128,256]{2,1,0:T(8,128)(2,1)} %bitcast.266, bf16[8,128,128]{2,1,0:T(8,128)(2,1)} %pad_maximum_fusion.8.refs_1_), custom_call_target="tpu_custom_call" | custom-call | tf_op jit(solution)/shard_map/pallas_call | solution.py:213
  191.6 4.5 copy.60
  196.1 4.2 reshape.318
  200.3 3.1 slice_bitcast_fusion
  211.5 47.8 %while.28 = (s32[]{:T(128)}, bf16[4,1024,64]{1,2,0:T(8,128)(2,1)}, f32[4,1024]{1,0:T(4,128)S(1)}, bf16[4,1024,64]{2,1,0:T(8,128)(2,1)}, bf16[4,2048,64]{2,1,0:T(...) while((s32[]{:T(128)}, bf16[4,1024,64]{1,2,0:T(8,128)(2,1)}, ...), condition=%wide.region_4.5_spmd.clone.clone, body=%wide.region_1.4_spmd.clone.sunk.clone | while | flops 568327168 | bytes 64567468 | solution.py:444
  217.7 5.1 fusion.250
  229.6 5.1 fusion.250
  241.5 5.1 fusion.250
  253.4 5.1 fusion.250
  263.5 4.9 multiply_reduce_fusion.3
  270.3 41.1 %shard_map.205 = bf16[8,128,2048]{2,1,0:T(8,128)(2,1)} custom-call(bf16[128,2048]{1,0:T(8,128)(2,1)} %multiply_convert_fusion.4.refs_0_), custom_call_target="tpu_custom_call" | custom-call | tf_op jit(solution)/shard_map/pallas_call | solution.py:213
  323.1 7.8 %fusion.178 = f32[1024,704]{0,1:T(8,128)} fusion(bf16[1024,2048]{1,0:T(8,128)(2,1)} %bitcast.250, bf16[704,2048]{1,0:T(8,128)(2,1)} %param.25), kind=kOutput, calls=%fused_computation.241 | convolution fusion | flops 2952790016 | bytes 9961472 | tf_op jit(solution)/shard_map/dot_general | solution.py:30
  330.9 6.2 fusion.177
  337.2 4.3 multiply_convert_fusion.1
  348.3 3.6 fusion.179
  351.9 5.6 add_convert_fusion
  365.5 70.1 %shard_map.206 = (f32[128,2048]{1,0:T(8,128)}, bf16[2112,128]{1,0:T(8,128)(2,1)}) custom-call(bf16[8,128,2048]{2,1,0:T(8,128)(2,1)} %bitcast.249, bf16[2112,1024]{1,0:T(8,128)(2,1)} %pad_maximum_fusion.refs_1_, bf16[2112,1024]{1,0:T(8,128)(2,1)} %pad_maximum_fusion.1.refs_2_), custom_call_target="tpu_custom_call" | custom-call | tf_op jit(solution)/shard_map/pallas_call | solution.py:213
  438.8 6.4 convolution_convert_fusion.1
  446.9 110.3 %while.29 = (s32[]{:T(128)}, f32[4,1024,64]{1,2,0:T(8,128)}, bf16[4,2048,128]{1,2,0:T(8,128)(2,1)}, bf16[4,1024,64]{2,1,0:T(8,128)(2,1)}, bf16[4,2048,64]{2,1,0:...) while((s32[]{:T(128)}, f32[4,1024,64]{1,2,0:T(8,128)}, ...), condition=%wide.region_9.10_spmd.clone.clone, body=%wide.region_7.9_spmd.clone.sunk.clone | while | flops 1364655104 | bytes 119836872 | solution.py:469
  449.6 5.7 multiply_reduce_fusion.6
  455.3 9.1 %multiply_convert_fusion.7 = bf16[1024,2048]{1,0:T(8,128)(2,1)} fusion(f32[1024,2048]{1,0:T(8,128)} %get-tuple-element.458, f32[1024,2048]{1,0:T(8,128)} %copy-done.2, f32[1024]{0:T(1024)S(1)} %get-tuple-element.459), kind=kLoop, calls=%fused_computation.22.clone.1.clone | loop fusion | flops 6291456 | bytes 20975616 | tf_op jit(solution)/shard_map/while/body/eval_jaxpr/convert_element_type | solution.py:463
  464.4 3.1 fusion.262
  467.6 4.5 fusion.261
  477.5 5.7 multiply_reduce_fusion.6
  483.3 8.6 %multiply_convert_fusion.7 = bf16[1024,2048]{1,0:T(8,128)(2,1)} fusion(f32[1024,2048]{1,0:T(8,128)} %get-tuple-element.458, f32[1024,2048]{1,0:T(8,128)} %copy-done.2, f32[1024]{0:T(1024)S(1)} %get-tuple-element.459), kind=kLoop, calls=%fused_computation.22.clone.1.clone | loop fusion | flops 6291456 | bytes 20975616 | tf_op jit(solution)/shard_map/while/body/eval_jaxpr/convert_element_type | solution.py:463
  491.9 3.1 fusion.262
  495.0 4.5 fusion.261
  504.9 5.7 multiply_reduce_fusion.6
  510.7 8.6 %multiply_convert_fusion.7 = bf16[1024,2048]{1,0:T(8,128)(2,1)} fusion(f32[1024,2048]{1,0:T(8,128)} %get-tuple-element.458, f32[1024,2048]{1,0:T(8,128)} %copy-done.2, f32[1024]{0:T(1024)S(1)} %get-tuple-element.459), kind=kLoop, calls=%fused_computation.22.clone.1.clone | loop fusion | flops 6291456 | bytes 20975616 | tf_op jit(solution)/shard_map/while/body/eval_jaxpr/convert_element_type | solution.py:463
  519.4 3.1 fusion.262
  522.5 4.4 fusion.261
  532.3 5.7 multiply_reduce_fusion.6
  538.1 8.6 %multiply_convert_fusion.7 = bf16[1024,2048]{1,0:T(8,128)(2,1)} fusion(f32[1024,2048]{1,0:T(8,128)} %get-tuple-element.458, f32[1024,2048]{1,0:T(8,128)} %copy-done.2, f32[1024]{0:T(1024)S(1)} %get-tuple-element.459), kind=kLoop, calls=%fused_computation.22.clone.1.clone | loop fusion | flops 6291456 | bytes 20975616 | tf_op jit(solution)/shard_map/while/body/eval_jaxpr/convert_element_type | solution.py:463
  546.7 3.1 fusion.262
  549.8 4.4 fusion.261
  559.1 3.5 copy.92
  562.7 4.3 copy.86.refs_0_
  570.9 5.0 convolution_convert_fusion
  575.9 70.4 %shard_map.207 = (f32[128,512]{1,0:T(8,128)}, bf16[2112,2048]{1,0:T(8,128)(2,1)}, f32[128,2048]{1,0:T(8,128)}, bf16[8,128,256]{2,1,0:T(8,128)(2,1)}, bf16[8,128,256]{2,1,0:T(8,128)(2,1)}) custom-call(bf16[16,128,512]{2,1,0:T(8,128)(2,1)} %copy.86.refs_0_, bf16[2112,128]{1,0:T(8,128)(2,1)} %get-tuple-element.123.refs_1_, bf16[8,128,2048]{2,1,0:T(8,128)(2,1)} %bitcast.259, ...), custom_call_target="tpu_custom_call" | custom-call | tf_op jit(solution)/shard_map/pallas_call | solution.py:213
  650.0 13.6 %shard_map.208 = bf16[8,128,128]{2,1,0:T(8,128)(2,1)} custom-call(bf16[8,128,128]{2,1,0:T(8,128)(2,1)} %maximum_bitcast_fusion.refs_0_), custom_call_target="tpu_custom_call" | custom-call | tf_op jit(solution)/shard_map/pallas_call | solution.py:213
  666.3 3.7 fusion.58
  673.3 10.5 %slice_convert_fusion = (f32[704,2048]{1,0:T(8,128)}, f32[704,2048]{1,0:T(8,128)}, f32[704,2048]{1,0:T(8,128)}) fusion(bf16[2112,2048]{1,0:T(8,128)(2,1)} %get-tuple-element.132), kind=kLoop, calls=%fused_computation.73 | loop fusion | flops 4325376 | bytes 25952256 | tf_op jit(solution)/shard_map/convert_element_type | solution.py:620
  689.2 76.5 %shard_map.209 = (f32[128,2048]{1,0:T(8,128)}, bf16[576,2048]{1,0:T(8,128)(2,1)}, f32[8,256]{1,0:T(8,128)}) custom-call(bf16[8,128,2048]{2,1,0:T(8,128)(2,1)} %bitcast.234, bf16[576,1024]{1,0:T(8,128)(2,1)} %pad_maximum_fusion.4.refs_1_, bf16[576,1024]{1,0:T(8,128)(2,1)} %pad_maximum_fusion.5.refs_2_, f32[8,8,256]{2,1,0:T(8,128)} %concatenate.115.refs_3_), custom_call_target="tpu_custom_call" | custom-call | tf_op jit(solution)/shard_map/pallas_call | solution.py:213
  765.8 4.2 slice_convert_fusion.4
  (317 shorter events, 150.3 us)
Async XLA Ops:
  7.2 330.0 %copy-start = (bf16[704,2048]{1,0:T(8,128)(2,1)S(1)}, bf16[704,2048]{1,0:T(8,128)(2,1)}, u32[]{:S(2)}) copy-start(bf16[704,2048]{1,0:T(8,128)(2,1)} %param.26) | copy-start | bytes 8650756
  7.2 323.7 %all-gather.3.cloned.1.call-start = ((), (), s32[]{:S(2)}) async-start(), calls=%async_computation | async-start | bytes 4718592 | tf_op jit(solution)/shard_map/all_gather | solution.py:500
  7.9 675.9 %all-gather.5.cloned.1.call-start = ((), (), s32[]{:S(2)}) async-start(), calls=%async_computation.1 | async-start | bytes 4718592 | tf_op jit(solution)/shard_map/all_gather | solution.py:596
  124.9 6.3 copy-start.32
  124.9 6.3 copy-start.34
  124.9 6.3 copy-start.43
  126.4 14.9 %copy-start.41 = (f32[8,1,256]{2,1,0:T(1,128)}, f32[8,1,256]{2,1,0:T(1,128)S(1)}, u32[]{:S(2)}) copy-start(f32[8,1,256]{2,1,0:T(1,128)S(1)} %get-tuple-element.284) | copy-start | bytes 24580
  127.1 19.7 %copy-start.56 = (f32[32]{0:T(128)}, f32[32]{0:T(128)S(1)}, u32[]{:S(2)}) copy-start(f32[32]{0:T(128)S(1)} %negate_power_fusion) | copy-start | bytes 388
  131.2 6.0 copy-start.44
  131.2 10.0 %copy-start.48 = (f32[8,128]{1,0:T(8,128)}, f32[8,128]{1,0:T(8,128)S(1)}, u32[]{:S(2)}) copy-start(f32[8,128]{1,0:T(8,128)S(1)} %get-tuple-element.291) | copy-start | bytes 12292
  131.3 5.9 copy-start.28
  131.3 5.9 copy-start.5
  206.1 5.4 copy-start.37
  263.5 5.9 copy-start.39
  268.4 168.7 %copy-start.50 = (f32[128]{0:T(128)}, f32[128]{0:T(128)S(1)}, u32[]{:S(2)}) copy-start(f32[128]{0:T(128)S(1)} %add_rsqrt_fusion.1) | copy-start | bytes 1540
  269.4 42.1 %copy-start.57 = (f32[32]{0:T(128)S(1)}, f32[32]{0:T(128)}, u32[]{:S(2)}) copy-start(f32[32]{0:T(128)} %copy-done.56) | copy-start | bytes 388
  269.4 42.1 %copy-start.58 = (f32[128]{0:T(128)S(1)}, f32[128]{0:T(128)}, u32[]{:S(2)}) copy-start(f32[128]{0:T(128)} %get-tuple-element.251) | copy-start | bytes 1540
  330.9 6.2 copy-start.24
  330.9 6.2 copy-start.71
  341.5 20.0 %copy-start.69 = (bf16[1024,704]{0,1:T(8,128)(2,1)}, bf16[1024,704]{0,1:T(8,128)(2,1)S(1)}, u32[]{:S(2)}) copy-start(bf16[1024,704]{0,1:T(8,128)(2,1)S(1)} %get-tuple-element.262) | copy-start | bytes 4325380
  351.9 5.6 copy-start.64
  365.5 70.1 %copy-start.8 = (f32[128,2048]{1,0:T(8,128)S(1)}, f32[128,2048]{1,0:T(8,128)}, u32[]{:S(2)}) copy-start(f32[128,2048]{1,0:T(8,128)} %copy-done.7) | copy-start | bytes 3145732
  365.5 71.6 %copy-start.18 = (bf16[128,2048]{1,0:T(8,128)(2,1)S(1)}, bf16[128,2048]{1,0:T(8,128)(2,1)}, u32[]{:S(2)}) copy-start(bf16[128,2048]{1,0:T(8,128)(2,1)} %param.18) | copy-start | bytes 1572868
  437.1 8.1 %copy-start.54 = (f32[128]{0:T(128)}, f32[128]{0:T(128)S(1)}, u32[]{:S(2)}) copy-start(f32[128]{0:T(128)S(1)} %broadcast_multiply_fusion.1) | copy-start | bytes 1540
  438.8 6.5 copy-start.20
  449.5 5.8 copy-start.2
  477.5 5.8 copy-start.2
  504.9 5.8 copy-start.2
  532.3 5.8 copy-start.2
  575.9 71.7 %copy-start.52 = (s32[256]{0:T(256)S(1)}, s32[256]{0:T(256)}, u32[]{:S(2)}) copy-start(s32[256]{0:T(256)} %get-tuple-element.306) | copy-start | bytes 3076
  575.9 71.7 %copy-start.53 = (s32[256]{0:T(256)S(1)}, s32[256]{0:T(256)}, u32[]{:S(2)}) copy-start(s32[256]{0:T(256)} %get-tuple-element.307) | copy-start | bytes 3076
  575.9 71.7 %copy-start.62 = (pred[256]{0:T(512)(128)(4,1)S(1)}, pred[256]{0:T(512)(128)(4,1)}, u32[]{:S(2)}) copy-start(pred[256]{0:T(512)(128)(4,1)} %compare_and_fusion) | copy-start | bytes 772
  575.9 73.2 %copy-start.63 = (bf16[128]{0:T(256)(128)(2,1)S(1)}, bf16[128]{0:T(256)(128)(2,1)}, u32[]{:S(2)}) copy-start(bf16[128]{0:T(256)(128)(2,1)} %pad.16.clone) | copy-start | bytes 772
  646.4 17.3 %copy-start.29 = (bf16[64,2048]{1,0:T(8,128)(2,1)S(1)}, bf16[64,2048]{1,0:T(8,128)(2,1)}, u32[]{:S(2)}) copy-start(bf16[64,2048]{1,0:T(8,128)(2,1)} %copy-done.28) | copy-start | bytes 786436
  646.4 17.3 %copy-start.33 = (bf16[32,2048]{1,0:T(8,128)(2,1)S(1)}, bf16[32,2048]{1,0:T(8,128)(2,1)}, u32[]{:S(2)}) copy-start(bf16[32,2048]{1,0:T(8,128)(2,1)} %param.22) | copy-start | bytes 393220
  646.4 17.3 %copy-start.35 = (bf16[32,2048]{1,0:T(8,128)(2,1)S(1)}, bf16[32,2048]{1,0:T(8,128)(2,1)}, u32[]{:S(2)}) copy-start(bf16[32,2048]{1,0:T(8,128)(2,1)} %param.21) | copy-start | bytes 393220
  673.3 10.5 %copy-start.68 = (bf16[8,128,256]{2,1,0:T(8,128)(2,1)S(1)}, bf16[8,128,256]{2,1,0:T(8,128)(2,1)}, u32[]{:S(2)}) copy-start(bf16[8,128,256]{2,1,0:T(8,128)(2,1)} %get-tuple-element.128) | copy-start | bytes 1572868
  765.7 6.1 copy-start.16
  765.7 6.1 copy-start.23
  765.7 6.1 copy-start.42
  765.7 7.7 copy-start.9
  765.8 7.7 copy-start.14
  765.8 7.7 copy-start.19
  765.8 7.7 copy-start.36
  765.8 7.7 copy-start.40
  765.8 7.7 copy-start.51
  765.8 7.7 copy-start.55
  765.8 7.7 copy-start.61
  (44 other events, 121.0 us)
Sparse Core Ops, SparseCore 0:
  10.4 81.1 all-gather.2
  445.4 72.9 all-gather.4

commit v3 on v2

v3 whole, which is shorter than its diff:
```python
import functools

import jax
import jax.numpy as jnp
from jax import lax
from jax.experimental import pallas as pl
from jax.experimental.pallas import tpu as pltpu
from jax.sharding import PartitionSpec as P

D = 2048
HEADS = 32
KV_HEADS = 4
HEAD = 64
LANES = 128

EPS = 1e-05
BASE = 10000.0
NEG = -1e30
F32 = jnp.float32
LOW = jnp.bfloat16
MESH = pl.DeviceIdType.MESH
VMEM_LIMIT = 56 * 1024 * 1024


def times(left, right):
    return jnp.dot(left, right, preferred_element_type=F32)


def times_transposed(left, right):
    return lax.dot_general(left, right, (((1,), (1,)), ((), ())), preferred_element_type=F32)


def transposed_times(left, right):
    return lax.dot_general(left, right, (((0,), (0,)), ((), ())), preferred_element_type=F32)


def rope_tables(places, width):
    half = width // 2
    freqs = BASE ** (-(jnp.arange(half).astype(F32) * 2.0 / width))
    angles = places.astype(F32)[:, None] * freqs[None, :]
    return jnp.cos(angles), jnp.sin(angles)


def wide_tables(places, heads):
    cosine, sine = rope_tables(places, HEAD)
    return (
        jnp.tile(jnp.concatenate([cosine, cosine], axis=1), (1, heads)),
        jnp.tile(jnp.concatenate([-sine, sine], axis=1), (1, heads)),
    )


def inverse_of(values):
    return lax.rsqrt(jnp.mean(values * values, axis=-1, keepdims=True) + EPS)


def rms_forward(values, gain):
    inverse = inverse_of(values)
    return (values * inverse * gain, inverse)


def rms_backward(values, inverse, gain, grads):
    scaled = grads * gain
    return inverse * scaled - values * inverse * inverse * inverse * jnp.mean(
        scaled * values, axis=-1, keepdims=True
    )


def at(axis, ring, pair, core=0):
    index = lax.axis_index(axis)
    cores = 2 if axis == "ctx" else 1
    ring_at = lax.rem(index // (2 * cores) + ring % 4, 4)
    pair_at = lax.rem(lax.rem(index // cores, 2) + pair, 2)
    core_at = lax.rem(lax.rem(index, cores) + core, cores)
    return (ring_at * 2 + pair_at) * cores + core_at


def chip(axis, ring=0, pair=0):
    return at(axis, ring, pair) // (2 if axis == "ctx" else 1)


class Link:
    def __init__(self, send_sems, recv_sems, local_sems):
        self.send_sems, self.recv_sems, self.local_sems = send_sems, recv_sems, local_sems
        self.sent, self.kept = [], []

    def greet(self, offsets):
        barrier = pltpu.get_barrier_semaphore()
        for axis, ring, pair, core in offsets:
            pl.semaphore_signal(
                barrier, inc=1, device_id={axis: at(axis, ring, pair, core)}, device_id_type=MESH
            )
        pl.semaphore_wait(barrier, len(offsets))

    def send(self, source, target, axis, ring, pair, core=0):
        number = len(self.sent)
        copy = pltpu.make_async_remote_copy(
            src_ref=source,
            dst_ref=target,
            send_sem=self.send_sems.at[number],
            recv_sem=self.recv_sems.at[number],
            device_id={axis: at(axis, ring, pair, core)},
            device_id_type=MESH,
        )
        copy.start()
        self.sent.append(copy)
        return copy

    def keep(self, source, target):
        copy = pltpu.make_async_copy(source, target, self.local_sems.at[len(self.kept)])
        copy.start()
        self.kept.append(copy)
        return copy

    def kept_now(self, copy):
        copy.wait()
        self.kept = [None if other is copy else other for other in self.kept]

    def finish(self):
        for copy in self.kept:
            if copy is not None:
                copy.wait()
        for copy in self.sent:
            copy.wait_send()


NEAR = [(1, 0), (3, 0), (0, 1)]
ALL = [(r, p) for r in range(4) for p in range(2) if (r, p) != (0, 0)]
near = lambda axis: [(axis, r, p, 0) for r, p in NEAR]
whole = lambda axis: [(axis, r, p, 0) for r, p in ALL]
SIBLING = [("ctx", 0, 0, 1)]


def run(*jobs):
    waiting = [(next(job), number, job) for number, job in enumerate(jobs)]
    while waiting:
        waiting.sort(key=lambda entry: entry[:2])
        _, number, job = waiting.pop(0)
        after = next(job, None)
        if after is not None:
            waiting.append((after, number, job))


def gather_job(link, axis, own, slot, share=None, start=0.0, block=10.5):
    me, pair = chip(axis), chip(axis, 0, 1)
    sharing = lambda index: share(index, slot(index)) if share else None
    yield start
    kept = link.keep(own, slot(me))
    to_pair = link.send(own, slot(me), axis, 0, 1)
    down = link.send(own, slot(me), axis, -1, 0)
    up = link.send(own, slot(me), axis, 1, 0)
    if share:
        share(me, own)
    yield start + block + 3.0
    to_pair.wait_recv()
    pair_down = link.send(slot(pair), slot(pair), axis, -1, 0)
    pair_up = link.send(slot(pair), slot(pair), axis, 1, 0)
    sharing(pair)
    yield start + block + 3.1
    down.wait_recv()
    next_one = chip(axis, 1, 0)
    far_down = link.send(slot(next_one), slot(next_one), axis, -1, 0)
    sharing(next_one)
    yield start + block + 3.2
    up.wait_recv()
    sharing(chip(axis, -1, 0))
    yield start + 2 * block + 4.0
    pair_up.wait_recv()
    last_pair = chip(axis, -1, 1)
    far_up = link.send(slot(last_pair), slot(last_pair), axis, 1, 0)
    sharing(last_pair)
    yield start + 2 * block + 4.1
    pair_down.wait_recv()
    sharing(chip(axis, 1, 1))
    yield start + 3 * block + 5.0
    far_down.wait_recv()
    sharing(chip(axis, 2, 0))
    yield start + 3 * block + 5.1
    far_up.wait_recv()
    sharing(chip(axis, 2, 1))
    link.kept_now(kept)


def add_rows(target, terms, step=16):
    def body(i, _):
        rows = pl.ds(pl.multiple_of(i * step, step), step)
        total = terms[0][rows, :].astype(F32)
        for term in terms[1:]:
            total = total + term[rows, :].astype(F32)
        target[rows, :] = total.astype(target.dtype)
        return 0

    lax.fori_loop(0, target.shape[0] // step, body, 0)


def scatter_job(link, axis, part, landing, work, result, start=0.0, block=10.5):
    here = lambda ring, pair: part(chip(axis, ring, pair))
    yield start
    to_last = link.send(here(2, 1), landing.at[1], axis, -1, 0)
    to_next = link.send(here(2, 0), landing.at[0], axis, 1, 0)
    pair_up = link.send(here(1, 1), landing.at[2], axis, 1, 0)
    mine_down = link.send(here(3, 0), landing.at[3], axis, -1, 0)
    spare = [here(3, 1), here(1, 0), here(0, 1), here(0, 0)]
    yield start + block + 3.0
    to_last.wait_recv()
    add_rows(work.at[0], [spare[0], landing.at[1]])
    pair_down = link.send(work.at[0], landing.at[4], axis, -1, 0)
    yield start + block + 3.1
    to_next.wait_recv()
    add_rows(work.at[1], [spare[1], landing.at[0]])
    mine_up = link.send(work.at[1], landing.at[5], axis, 1, 0)
    yield start + 2 * block + 3.0
    pair_up.wait_recv()
    mine_down.wait_recv()
    yield start + 3 * block + 4.0
    pair_down.wait_recv()
    add_rows(work.at[2], [spare[2], landing.at[2], landing.at[4]])
    across = link.send(work.at[2], landing.at[6], axis, 0, 1)
    yield start + 3 * block + 4.1
    mine_up.wait_recv()
    yield start + 4 * block + 8.0
    across.wait_recv()
    add_rows(result, [spare[3], landing.at[3], landing.at[5], landing.at[6]])


def exchange_job(link, axis, part, slot, start=0.0, length=8.0):
    me = chip(axis)
    yield start
    kept = link.keep(part(me), slot(me))
    copies = [link.send(part(chip(axis, r, p)), slot(me), axis, r, p) for r, p in ALL]
    yield start + length
    for copy in copies:
        copy.wait_recv()
    link.kept_now(kept)


ANY = pl.BlockSpec(memory_space=pl.ANY)
INSIDE = pl.BlockSpec(memory_space=pltpu.VMEM)


def comm_call(kernel, number, inputs, in_specs, outputs, out_specs, scratch=()):
    sems = [pltpu.SemaphoreType.DMA((96,)), pltpu.SemaphoreType.DMA((96,)), pltpu.SemaphoreType.DMA((8,))]

    def body(*refs):
        link = Link(*refs[-3:])
        kernel(link, *refs[:-3])
        link.finish()

    return pl.pallas_call(
        body,
        out_shape=outputs,
        in_specs=in_specs,
        out_specs=out_specs,
        scratch_shapes=[*scratch, *sems],
        compiler_params=pltpu.CompilerParams(
            collective_id=number, has_side_effects=True, vmem_limit_bytes=VMEM_LIMIT
        ),
    )(*inputs)


shape = jax.ShapeDtypeStruct


def front_kernel(link, tokens, small, kv_send, w_out, token_rows, smalls, kv_other, out_full):
    link.greet(whole("shard") + [("ctx", 1, 0, 0), ("ctx", 3, 0, 0)] + SIBLING)
    core = lax.rem(lax.axis_index("ctx"), 2)
    ring = lax.axis_index("ctx") // 4

    def block(index, ring_further=0):
        at_ring = lax.rem(ring + ring_further, 4)
        rows = pl.ds(pl.multiple_of((core * 4 + at_ring) * 32, 32), 32)
        return out_full.at[index, rows]

    mine = pl.ds(pl.multiple_of((core * 4 + ring) * 32, 32), 32)
    passing, sibs = [], []

    def share(index, source):
        sibs.append(link.send(source, block(index), "ctx", 0, 0, 1))
        up = link.send(source, block(index), "ctx", 1, 0)
        passing.append((index, up, link.send(source, block(index), "ctx", -1, 0)))

    def ring_job():
        far = []
        for number in range(8):
            yield 10.0 + 3.8 * number
            index, up, down = passing[number]
            up.wait_recv()
            if number % 2 == 0:
                far.append((index, link.send(block(index, 3), block(index, 3), "ctx", 1, 0)))
            sibs.append(link.send(block(index, 3), block(index, 3), "ctx", 0, 0, 1))
            down.wait_recv()
            if number % 2 == 1:
                far.append((index, link.send(block(index, 1), block(index, 1), "ctx", -1, 0)))
            sibs.append(link.send(block(index, 1), block(index, 1), "ctx", 0, 0, 1))
        for number, (index, copy) in enumerate(far):
            yield 38.0 + number
            copy.wait_recv()
            sibs.append(link.send(block(index, 2), block(index, 2), "ctx", 0, 0, 1))
        yield 50.0
        for copy in sibs:
            copy.wait_recv()

    def kv_job():
        yield 0.0
        copy = link.send(kv_send, kv_other, "shard", 0, 1)
        yield 9.0
        copy.wait_recv()

    run(
        gather_job(link, "shard", w_out.at[mine], lambda i: out_full.at[i, mine], share, 0.0, 4.0),
        exchange_job(link, "shard", lambda i: small, lambda i: smalls.at[i], 0.0, 9.0),
        kv_job(),
        gather_job(link, "shard", tokens, lambda i: token_rows.at[i], None, 0.1, 12.0),
        ring_job(),
    )


def qkv_kernel(link, queries, kv, queries_got, kv_all, kv_got, kv_own):
    link.greet(whole("shard") + near("ctx") + SIBLING)
    core = lax.rem(lax.axis_index("ctx"), 2)

    def kv_job():
        yield from exchange_job(link, "shard", lambda i: kv.at[i], lambda i: kv_got.at[i], 0.0, 6.0)
        for head in range(KV_HEADS):
            kv_own[:, head * 128 : (head + 1) * 128] = kv_got[2 * head] + kv_got[2 * head + 1]
        slot = lambda i: kv_all.at[i * 2 + core]
        sibs = []

        def share(index, block):
            sibs.append(link.send(block, slot(index), "ctx", 0, 0, 1))

        yield from gather_job(link, "ctx", kv_own, slot, share, 6.0, 2.7)
        for copy in sibs:
            copy.wait_recv()

    run(
        kv_job(),
        exchange_job(link, "shard", lambda i: queries.at[i], lambda i: queries_got.at[i], 0.1, 30.0),
    )


def gather_kernel(link, own, slots):
    link.greet(near("shard"))
    run(gather_job(link, "shard", own, lambda i: slots.at[i]))


REDUCE_ORDER = [(2, 1), (2, 0), (1, 1), (3, 0), (3, 1), (1, 0), (0, 1), (0, 0)]


def reduced(link, theirs, mine, from_sibling, landing, work, summed, start=0.0, block=10.8):
    columns = lambda ref, i: ref.at[:, pl.ds(pl.multiple_of(i * LANES, LANES), LANES)]
    copies = {}
    for r, p in REDUCE_ORDER:
        i = chip("ctx", r, p)
        copies[r, p] = link.send(columns(theirs, i), columns(from_sibling, i), "ctx", 0, 0, 1)
    offsets = iter(REDUCE_ORDER)

    def part(i):
        r, p = reduce_at[0]
        copies[r, p].wait_recv()
        add_rows(columns(from_sibling, i), [columns(mine, i), columns(from_sibling, i)])
        return columns(from_sibling, i)

    reduce_at = [None]

    class Parts:
        def __call__(self, i):
            reduce_at[0] = next(offsets)
            return part(i)

    yield from scatter_job(link, "ctx", Parts(), landing, work, summed, start, block)


def spread(link, summed, full, start=0.0, block=10.8):
    core = lax.rem(lax.axis_index("ctx"), 2)
    slot = lambda i: full.at[:, pl.ds(pl.multiple_of((core * 8 + i) * LANES, LANES), LANES)]
    sibs = []

    def share(index, block):
        sibs.append(link.send(block, slot(index), "ctx", 0, 0, 1))

    yield from gather_job(link, "ctx", summed, slot, share, start, block)
    for copy in sibs:
        copy.wait_recv()


def middle_kernel(link, parts, theirs, mine, result, summed, land_a, work_a, sib, land_b, work_b):
    link.greet(near("shard") + near("ctx") + SIBLING)
    run(
        scatter_job(link, "shard", lambda i: parts.at[i], land_a, work_a, result),
        reduced(link, theirs, mine, sib, land_b, work_b, summed, 4.0),
    )


def swap_lanes(values):
    width = values.shape[1]
    low_half = lax.broadcasted_iota(jnp.int32, values.shape, 1) % HEAD < 32
    return jnp.where(low_half, pltpu.roll(values, width - 32, 1), pltpu.roll(values, 32, 1))


def back_kernel(link, kv_parts, summed, hidden, queries, attended, cosine, sine,
                full, hidden_rows, query_cols, attended_cols, kv_cols,
                sib, land_k, work_k, kv_grad, kv_turned):
    link.greet(whole("shard") + near("ctx") + SIBLING)
    core = lax.rem(lax.axis_index("ctx"), 2)

    def kv_job():
        yield 0.0
        copies = [
            link.send(kv_parts.at[i * 2 + 1 - core], sib.at[i], "ctx", 0, 0, 1) for i in range(8)
        ]
        yield 3.0
        for i, copy in enumerate(copies):
            copy.wait_recv()
            add_rows(sib.at[i], [sib.at[i], kv_parts.at[i * 2 + core]])
        yield from scatter_job(link, "ctx", lambda i: sib.at[i], land_k, work_k, kv_grad, 4.0, 2.7)
        key_lanes = lax.broadcasted_iota(jnp.int32, cosine.shape, 1) < HEAD
        for head in range(KV_HEADS):
            lanes = slice(head * 128, head * 128 + 128)
            both = kv_grad[:, lanes]
            turned = both * cosine[...] - swap_lanes(both) * sine[...]
            kv_turned[:, lanes] = jnp.where(key_lanes, turned, both).astype(LOW)
        part = lambda i: kv_turned.at[:, pl.ds(pl.multiple_of(i // 2 * 128, 128), 128)]
        yield from exchange_job(link, "shard", part, lambda i: kv_cols.at[i], 26.0, 12.0)

    columns = lambda ref: lambda i: ref.at[:, pl.ds(pl.multiple_of(i * 256, 256), 256)]
    run(
        kv_job(),
        gather_job(link, "shard", hidden, lambda i: hidden_rows.at[i], None, 0.2),
        spread(link, summed, full, 5.0),
        exchange_job(link, "shard", columns(queries), lambda i: query_cols.at[i], 27.0, 20.0),
        exchange_job(link, "shard", columns(attended), lambda i: attended_cols.at[i], 27.1, 21.0),
    )


def last_kernel(link, parts, theirs, mine, gains, result, full, gain_sum,
                land_a, work_a, sib, land_b, work_b, summed, gain_land, gain_work, gain_ctx):
    link.greet(whole("shard") + whole("ctx") + SIBLING)

    def weight_job():
        yield from reduced(link, theirs, mine, sib, land_b, work_b, summed, 0.0, 3.0)
        yield from spread(link, summed, full, 24.0, 3.0)

    def gain_job():
        yield from exchange_job(link, "shard", lambda i: gains.at[i], lambda i: gain_land.at[i], 0.2, 8.0)
        gain_work[0] = sum(gain_land[i] for i in range(8))
        copy = link.send(gain_work.at[0], gain_work.at[1], "ctx", 0, 0, 1)
        yield 11.0
        copy.wait_recv()
        gain_work[2] = gain_work[0] + gain_work[1]
        copies = [
            link.send(gain_work.at[2], gain_ctx.at[i], "ctx", r, p) for i, (r, p) in enumerate(ALL)
        ]
        yield 40.0
        for copy in copies:
            copy.wait_recv()
        gain_sum[...] = gain_work[2] + sum(gain_ctx[i] for i in range(7))

    run(
        scatter_job(link, "shard", lambda i: parts.at[i], land_a, work_a, result),
        weight_job(),
        gain_job(),
    )


def first_kernel(pair_ref, tokens, gain, w_query, w_key, w_value, kv_other, cosine, sine,
                 normed_ref, q_ref, kv_ref, w_kv):
    @pl.when(pl.program_id(0) == 0)
    def _():
        leads = pair_ref[0] == 0
        nothing = jnp.zeros((32, D), LOW)
        choose = lambda yes, ref, other: jnp.where(yes, ref[...], other)
        w_kv[0:32, :] = choose(leads, w_key, nothing)
        w_kv[32:64, :] = choose(leads, kv_other, nothing)
        w_kv[64:96, :] = choose(jnp.logical_not(leads), kv_other, nothing)
        w_kv[96:128, :] = choose(jnp.logical_not(leads), w_value, nothing)

    values = tokens[...].astype(F32)
    normed = rms_forward(values, gain[...])[0].astype(LOW)
    normed_ref[...] = normed
    cosine, sine = cosine[...], sine[...]
    turn = lambda v: v * cosine + swap_lanes(v) * sine
    q = times_transposed(normed, w_query[...])
    for i in range(2):
        lanes = slice(i * 128, i * 128 + 128)
        q_ref[:, :, lanes] = turn(q[:, lanes]).astype(LOW).reshape(2, 128, 128)
    kv = times_transposed(normed, w_kv[...])
    keys = lax.broadcasted_iota(jnp.int32, kv.shape, 1) < HEAD
    kv_ref[...] = jnp.where(keys, turn(kv), kv).astype(LOW).reshape(2, 128, 128)


def first_part(pair, token_rows, gain, w_query, w_key, w_value, kv_other, cosine, sine):
    held = lambda *dims: pl.BlockSpec(dims, lambda i, *_: (0,) * len(dims))
    rows = lambda width: pl.BlockSpec((256, width), lambda i, *_: (i, 0))
    slots = lambda width: pl.BlockSpec((2, 128, width), lambda i, *_: (i, 0, 0))
    return pl.pallas_call(
        first_kernel,
        grid_spec=pltpu.PrefetchScalarGridSpec(
            num_scalar_prefetch=1,
            grid=(4,),
            in_specs=[rows(D), held(1, D), held(256, D), held(32, D), held(32, D), held(32, D), rows(128), rows(128)],
            out_specs=[rows(D), slots(256), slots(128)],
            scratch_shapes=[pltpu.VMEM((128, D), LOW)],
        ),
        out_shape=[shape((1024, D), LOW), shape((8, 128, 256), LOW), shape((8, 128, 128), LOW)],
        compiler_params=pltpu.CompilerParams(vmem_limit_bytes=VMEM_LIMIT),
        cost_estimate=pl.CostEstimate(flops=1 << 31, bytes_accessed=10 << 20, transcendentals=1024),
    )(pair, token_rows, gain, w_query, w_key, w_value, kv_other, cosine, sine)


BLOCK = 256
LOG2E = 1.4426950408889634


def sort_keys(order_ref, kv_ref, sorted_ref, flipped_ref):
    for c in range(16):
        lead = pl.multiple_of(order_ref[c] * 64, 64)
        trail = pl.multiple_of((31 - order_ref[c]) * 64, 64)
        sorted_ref[pl.ds(lead, 64), :] = kv_ref[c, 0:64, :]
        sorted_ref[pl.ds(trail, 64), :] = kv_ref[c, 64:128, :]
    for i in range(8):
        rows = slice(i * BLOCK, (i + 1) * BLOCK)
        flipped_ref[i] = jnp.transpose(sorted_ref[rows, :].astype(F32)).astype(LOW)


def spread_heads(blocks, high):
    pieces = []
    for block in blocks:
        block = block.astype(F32)
        turned = pltpu.roll(block, 64, 1)
        lane = lax.broadcasted_iota(jnp.int32, block.shape, 1)
        keep = (lane >= 64) if high else (lane < 64)
        first, second = (turned, block) if high else (block, turned)
        pieces += [jnp.where(keep, first, 0.0), jnp.where(keep, second, 0.0)]
    return jnp.concatenate(pieces, axis=0)


def join_heads(flipped):
    upright = jnp.transpose(flipped)
    return [
        jnp.concatenate([upright[i * 128 : i * 128 + 64], upright[i * 128 + 64 : i * 128 + 128]], axis=1)
        for i in range(4)
    ]


def query_blocks(ref, run):
    rows = slice(run * 64, run * 64 + 64)
    return [ref[s, rows, p * 128 : p * 128 + 128] for s in range(2) for p in range(2)]


def row_blocks(ref, run):
    rows = slice(run * 64, run * 64 + 64)
    return [ref[rows, i * 128 : i * 128 + 128] for i in range(4)]


def above(block, first_place):
    key = lax.broadcasted_iota(jnp.int32, (BLOCK, 512), 0) + block * BLOCK
    query = lax.broadcasted_iota(jnp.int32, (BLOCK, 512), 1) % 64 + first_place
    return key > query


def dot_kt(left, right):
    return lax.dot_general(left, right, (((1,), (1,)), ((), ())), preferred_element_type=F32)


def attend_kernel(order_ref, own_ref, q_ref, kv_ref, out_ref, lse_ref, sorted_ref, flipped_ref):
    sort_keys(order_ref, kv_ref, sorted_ref, flipped_ref)
    factor = HEAD**-0.5 * LOG2E
    for run in range(2):
        first_place = jnp.where(run == 0, own_ref[0], 31 - own_ref[0]) * 64
        last = first_place // BLOCK
        q = spread_heads(query_blocks(q_ref, run), False).astype(LOW)

        def step(block, carry, masked):
            largest, total, mixed = carry
            rows = pl.ds(pl.multiple_of(block * BLOCK, BLOCK), BLOCK)
            scores = dot_kt(sorted_ref[rows, :], q) * factor
            if masked:
                scores = jnp.where(above(block, first_place), NEG, scores)
            top = jnp.maximum(largest, jnp.max(scores, axis=0, keepdims=True))
            fade = jnp.exp2(largest - top)
            exps = jnp.exp2(scores - top)
            total = total * fade + jnp.sum(exps, axis=0, keepdims=True)
            mixed = mixed * fade + times(flipped_ref[block, 64:128, :], exps.astype(LOW))
            return top, total, mixed

        carry = (jnp.full((1, 512), NEG, F32), jnp.zeros((1, 512), F32), jnp.zeros((64, 512), F32))
        carry = lax.fori_loop(0, last, functools.partial(step, masked=False), carry)
        largest, total, mixed = step(last, carry, True)
        for i, block in enumerate(join_heads(mixed / total)):
            out_ref[run * 64 : run * 64 + 64, i * 128 : i * 128 + 128] = block.astype(LOW)
        lse_ref[0, run : run + 1, :] = largest + jnp.log2(total)


def attend_back_kernel(order_ref, own_ref, q_ref, kv_ref, out_ref, grad_ref, lse_ref, cos_ref, sin_ref,
                       dq_ref, dkv_ref, sorted_ref, flipped_ref, total_ref):
    sort_keys(order_ref, kv_ref, sorted_ref, flipped_ref)
    total_ref[...] = jnp.zeros_like(total_ref)
    scale = HEAD**-0.5
    factor = scale * LOG2E
    for run in range(2):
        first_place = jnp.where(run == 0, own_ref[0], 31 - own_ref[0]) * 64
        last = first_place // BLOCK
        q = spread_heads(query_blocks(q_ref, run), False).astype(LOW)
        grad_wide = spread_heads(row_blocks(grad_ref, run), True)
        out_wide = spread_heads(row_blocks(out_ref, run), True)
        grad = grad_wide.astype(LOW)
        inner = lax.dot_general(
            jnp.ones((8, 128), F32),
            grad_wide * out_wide,
            (((1,), (1,)), ((), ())),
            precision=lax.Precision.HIGHEST,
            preferred_element_type=F32,
        )[:1]
        lse = lse_ref[0, run : run + 1, :]

        def step(block, dq, masked):
            rows = pl.ds(pl.multiple_of(block * BLOCK, BLOCK), BLOCK)
            kv = sorted_ref[rows, :]
            probs = jnp.exp2(dot_kt(kv, q) * factor - lse)
            if masked:
                probs = jnp.where(above(block, first_place), 0.0, probs)
            score_grad = (probs * (dot_kt(kv, grad) - inner)).astype(LOW)
            total_ref[rows, :] += times(score_grad, q) + times(probs.astype(LOW), grad)
            return dq + times(flipped_ref[block, 0:64, :], score_grad)

        dq = lax.fori_loop(0, last, functools.partial(step, masked=False), jnp.zeros((64, 512), F32))
        dq = step(last, dq, True)
        cosine, sine = cos_ref[run * 64 : run * 64 + 64, :], sin_ref[run * 64 : run * 64 + 64, :]
        low_half = lax.broadcasted_iota(jnp.int32, (64, 128), 1) % 64 < 32
        for i, block in enumerate(join_heads(dq * scale)):
            turned = jnp.where(low_half, pltpu.roll(block, 96, 1), pltpu.roll(block, 32, 1))
            dq_ref[run * 64 : run * 64 + 64, i * 128 : i * 128 + 128] = (
                block * cosine - turned * sine
            ).astype(LOW)
    weight = jnp.where(lax.broadcasted_iota(jnp.int32, (64, 128), 1) < 64, scale, 1.0)
    for c in range(16):
        lead = pl.multiple_of(order_ref[c] * 64, 64)
        trail = pl.multiple_of((31 - order_ref[c]) * 64, 64)
        dkv_ref[c, 0:64, :] = (total_ref[pl.ds(lead, 64), :] * weight).astype(LOW)
        dkv_ref[c, 64:128, :] = (total_ref[pl.ds(trail, 64), :] * weight).astype(LOW)


def attention_call(kernel, scalars, inputs, kinds, outputs, out_kinds, scratch, flops):
    specs = {
        "q": pl.BlockSpec((2, 128, 256), lambda g, *_: (g, 0, 0)),
        "kv": pl.BlockSpec((16, 128, 128), lambda g, *_: (0, 0, g)),
        "rows": pl.BlockSpec((128, 512), lambda g, *_: (0, g)),
        "lse": pl.BlockSpec((1, 8, 512), lambda g, *_: (g, 0, 0)),
        "table": pl.BlockSpec((128, 128), lambda g, *_: (0, 0)),
    }
    keys = [pltpu.VMEM((2048, 128), LOW), pltpu.VMEM((8, 128, BLOCK), LOW)]
    return pl.pallas_call(
        kernel,
        grid_spec=pltpu.PrefetchScalarGridSpec(
            num_scalar_prefetch=2,
            grid=(KV_HEADS,),
            in_specs=[specs[k] for k in kinds],
            out_specs=[specs[k] for k in out_kinds],
            scratch_shapes=keys + scratch,
        ),
        out_shape=outputs,
        compiler_params=pltpu.CompilerParams(vmem_limit_bytes=VMEM_LIMIT),
        cost_estimate=pl.CostEstimate(flops=flops, bytes_accessed=8 << 20, transcendentals=8 << 20),
    )(*scalars, *inputs)


def attend(queries, kv_all, order, own):
    return attention_call(
        attend_kernel,
        (order, own),
        (queries, kv_all),
        ("q", "kv"),
        [jax.ShapeDtypeStruct((128, D), LOW), jax.ShapeDtypeStruct((4, 8, 512), F32)],
        ("rows", "lse"),
        [],
        1 << 33,
    )


def attend_back(queries, kv_all, attended, attended_grad, lse, cosine, sine, order, own):
    return attention_call(
        attend_back_kernel,
        (order, own),
        (queries, kv_all, attended, attended_grad, lse, cosine, sine),
        ("q", "kv", "rows", "rows", "lse", "table", "table"),
        [jax.ShapeDtypeStruct((128, D), LOW), jax.ShapeDtypeStruct((16, 128, 512), LOW)],
        ("rows", "kv"),
        [pltpu.VMEM((2048, 128), F32)],
        1 << 34,
    )


def local(
    tokens,
    positions,
    out_grad,
    attn_gain,
    w_query,
    w_key,
    w_value,
    w_out,
    ffn_gain,
    w_gate,
    w_up,
    w_down,
):
    rows = tokens.shape[0]
    shard, ctx = lax.axis_index("shard"), lax.axis_index("ctx")
    shard_pair, core = shard % 2, ctx % 2
    places = positions[0]
    own_places = lax.dynamic_slice_in_dim(places, ctx * rows, rows)
    blocks = lambda m: m.reshape(8, rows, -1)

    small = jnp.stack(
        [attn_gain, ffn_gain, jnp.concatenate([own_places // 64, own_places % 64]).astype(LOW)]
    )
    small = jnp.concatenate([small, jnp.zeros((13, 256), LOW)], axis=0)
    token_rows, smalls, kv_other, out_full = comm_call(
        front_kernel,
        0,
        [tokens, small, jnp.where(shard_pair == 0, w_value, w_key), w_out],
        [ANY] * 4,
        [shape((8, rows, D), LOW), shape((8, 16, 256), LOW), shape((32, D), LOW), shape((8, 256, D), LOW)],
        [ANY] * 4,
    )
    out_grad_late, token_rows = lax.optimization_barrier((out_grad, token_rows))
    out_grad_rows = lax.all_gather(out_grad_late, "shard", axis=0, tiled=True)
    token_rows, out_full = token_rows.reshape(-1, D), out_full.reshape(D, D)
    gain_one = smalls[:, 0].reshape(-1).astype(F32)
    gain_two = smalls[:, 1].reshape(-1).astype(F32)
    place_rows = (smalls[:, 2, :rows].astype(F32) * 64.0 + smalls[:, 2, rows:].astype(F32)).reshape(-1)
    cosine, sine = wide_tables(place_rows, 2)
    inputs_rows = token_rows.astype(F32)
    normed_rows, queries, kv_part = first_part(
        shard_pair[None], token_rows, gain_one[None], w_query, w_key, w_value, kv_other, cosine, sine
    )
    queries, kv_all = comm_call(
        qkv_kernel,
        1,
        [queries, kv_part],
        [ANY] * 2,
        [shape((8, rows, 256), LOW), shape((16, rows, 512), LOW)],
        [ANY] * 2,
        [pltpu.VMEM((8, rows, 128), LOW), pltpu.VMEM((rows, 512), LOW)],
    )

    order = places.reshape(16, rows)[:, 0] // 64
    own_order = own_places[:1] // 64
    attended, lse = attend(queries, kv_all, order, own_order)

    inputs = tokens.astype(F32)
    hidden_state = inputs + times(attended, out_full)
    normed_two, inverse_two = rms_forward(hidden_state, gain_two)
    (normed_two_rows,) = comm_call(
        gather_kernel, 2, [normed_two.astype(LOW)], [ANY], [shape((8, rows, D), LOW)], [ANY]
    )
    normed_two_rows = normed_two_rows.reshape(-1, D)

    gate = times_transposed(normed_two_rows, w_gate)
    up_part = times_transposed(normed_two_rows, w_up)
    inner_grad = times_transposed(out_grad_rows, w_down)
    sigmoid = jax.nn.sigmoid(gate)
    activated = gate * sigmoid
    inner = (activated * up_part).astype(LOW)
    gate_grad = (inner_grad * up_part * sigmoid * (1.0 + gate * (1.0 - sigmoid))).astype(LOW)
    up_grad = (inner_grad * activated).astype(LOW)
    normed_two_parts = (times(gate_grad, w_gate) + times(up_grad, w_up)).astype(LOW)
    down_parts = times(inner, w_down).astype(LOW)

    def halves(terms):
        def one(which):
            cut = lambda m: lax.dynamic_slice_in_dim(m, which * 1024, 1024, axis=1)
            return jnp.concatenate(
                [transposed_times(left, cut(right)).astype(LOW) for left, right in terms], axis=0
            )

        return one(1 - core), one(core)

    ff = w_gate.shape[0]
    theirs, mine = halves(
        [(gate_grad, normed_two_rows), (up_grad, normed_two_rows), (inner, out_grad_rows)]
    )
    vmem = lambda count, *dims: pltpu.VMEM((count, *dims), LOW)
    normed_two_grad, summed = comm_call(
        middle_kernel,
        3,
        [blocks(normed_two_parts), theirs, mine],
        [INSIDE, ANY, INSIDE],
        [shape((rows, D), F32), shape((3 * ff, LANES), LOW)],
        [INSIDE, INSIDE],
        [
            vmem(7, rows, D),
            vmem(3, rows, D),
            pltpu.VMEM((3 * ff, 1024), LOW),
            vmem(7, 3 * ff, LANES),
            vmem(3, 3 * ff, LANES),
        ],
    )

    down_sum = lax.psum_scatter(down_parts, "shard", scatter_dimension=0, tiled=True)
    outputs = (hidden_state + down_sum.astype(F32)).astype(LOW)
    gain_two_part = jnp.sum(normed_two_grad * hidden_state * inverse_two, axis=0)
    hidden_grad = out_grad.astype(F32) + rms_backward(
        hidden_state, inverse_two, gain_two, normed_two_grad
    )
    hidden_low = hidden_grad.astype(LOW)
    attended_grad = times_transposed(hidden_low, out_full).astype(LOW)
    own_table = lambda table: lax.dynamic_slice_in_dim(table, shard * rows, rows)
    cosine_own, sine_own = own_table(cosine), own_table(sine)
    query_pre_grad, kv_parts = attend_back(
        queries, kv_all, attended, attended_grad, lse, cosine_own, sine_own, order, own_order
    )
    ffn_full, hidden_rows, query_cols, attended_cols, kv_cols = comm_call(
        back_kernel,
        4,
        [kv_parts, summed, hidden_low, query_pre_grad, attended, cosine_own, sine_own],
        [INSIDE, INSIDE, ANY, ANY, ANY, INSIDE, INSIDE],
        [
            shape((3 * ff, D), LOW),
            shape((8, rows, D), LOW),
            shape((8, rows, 256), LOW),
            shape((8, rows, 256), LOW),
            shape((8, rows, 128), LOW),
        ],
        [ANY] * 5,
        [
            vmem(8, rows, 512),
            vmem(7, rows, 512),
            vmem(3, rows, 512),
            pltpu.VMEM((rows, 512), F32),
            pltpu.VMEM((rows, 512), LOW),
        ],
    )
    hidden_rows = hidden_rows.reshape(-1, D)
    gate_wgrad, up_wgrad, down_wgrad = (
        ffn_full[i * ff : (i + 1) * ff].astype(F32) for i in range(3)
    )
    query_cols, attended_cols = query_cols.reshape(-1, 256), attended_cols.reshape(-1, 256)
    kv_cols = kv_cols.reshape(-1, 128)
    nothing = jnp.zeros((32, D), LOW)
    kv_weights = jnp.where(
        shard_pair == 0,
        jnp.concatenate([w_key, nothing, w_value, nothing], axis=0),
        jnp.concatenate([nothing, w_key, nothing, w_value], axis=0),
    )
    kv_mine = jnp.where(
        shard_pair == 0,
        jnp.concatenate([kv_cols[:, :32], kv_cols[:, 64:96]], axis=1),
        jnp.concatenate([kv_cols[:, 32:64], kv_cols[:, 96:]], axis=1),
    )
    normed_parts = times(query_cols, w_query) + times(kv_cols, kv_weights)
    gain_one_part = jnp.sum(normed_parts * inputs_rows * inverse_of(inputs_rows), axis=0)
    theirs, mine = halves(
        [(query_cols, normed_rows), (kv_mine, normed_rows), (attended_cols, hidden_rows)]
    )
    gains = jnp.stack([gain_one_part, gain_two_part]).reshape(2, 8, 256).transpose(1, 0, 2)
    gains = jnp.concatenate([gains, jnp.zeros((8, 6, 256), F32)], axis=1)
    normed_grad, attn_full, gain_sum = comm_call(
        last_kernel,
        6,
        [blocks(normed_parts.astype(LOW)), theirs, mine, gains],
        [INSIDE, ANY, INSIDE, INSIDE],
        [shape((rows, D), F32), shape((576, D), LOW), shape((8, 256), F32)],
        [INSIDE, ANY, INSIDE],
        [
            vmem(7, rows, D),
            vmem(3, rows, D),
            pltpu.VMEM((576, 1024), LOW),
            vmem(7, 576, LANES),
            vmem(3, 576, LANES),
            pltpu.VMEM((576, LANES), LOW),
            pltpu.VMEM((8, 8, 256), F32),
            pltpu.VMEM((3, 8, 256), F32),
            pltpu.VMEM((7, 8, 256), F32),
        ],
    )
    inverse_one = inverse_of(inputs)
    input_grad = hidden_grad + rms_backward(inputs, inverse_one, gain_one, normed_grad)
    query_wgrad, key_wgrad, value_wgrad, out_wgrad = (
        attn_full[a:b].astype(F32) for a, b in ((0, 256), (256, 288), (288, 320), (320, 576))
    )
    return (
        outputs,
        input_grad,
        gain_sum[0],
        query_wgrad,
        key_wgrad,
        value_wgrad,
        out_wgrad,
        gain_sum[1],
        gate_wgrad,
        up_wgrad,
        down_wgrad,
    )


def solution(mesh):
    rows = P(("shard", "ctx"), None)
    matrix = P("shard", None)
    vector = P("shard")
    in_specs = (rows, matrix, rows, vector, matrix, matrix, matrix, matrix, vector) + (matrix,) * 3
    out_specs = (rows, rows, vector, matrix, matrix, matrix, matrix, vector) + (matrix,) * 3
    return jax.shard_map(local, mesh=mesh, in_specs=in_specs, out_specs=out_specs, check_vma=False)
```

time: 787 us -> 556 us (0.71)
  matrix products: 174 us -> 75.2 us
  other arithmetic: 106 us -> 41.9 us
  local copies, waits for them, and re-layouts: 70.3 us -> 15 us
  Pallas kernels: 415 us -> 404 us
    pallas_call x7 -> x6, Pallas kernels: 415 us -> 349 us  [comm_call(): pl.pallas_call(body, out_shape=outputs, in_specs=in_specs, out_specs=out_...]
    pallas_call x0 -> x3, Pallas kernels: none -> 55.6 us  [the longest x2 47.6 us: attention_call(): pl.pallas_call(kernel, grid_spec=pltpu.PrefetchScalarGridSpec(num_scalar_...]
    dot_general x18 -> x4, matrix products: 74.1 us -> 26.5 us  [times_transposed(): lax.dot_general(left, right, (((1,), (1,)), ((), ())), preferred_element_...]
    convert_element_type x9 -> x0, other arithmetic: 42.7 us -> none  [the longest x4 34.9 us: head_backward(): score_grad = (probs * (prob_grad - inner_sum)).astype(LOW)]
    dot_general x20 -> x12, matrix products: 45.9 us -> 18.4 us  [transposed_times(): lax.dot_general(left, right, (((0,), (0,)), ((), ())), preferred_element_...]
    dot_general x14 -> x6, matrix products: 54.1 us -> 30.3 us  [times(): return jnp.dot(left, right, preferred_element_type=F32)]
    unnamed x139 -> x63, local copies, waits for them, and re-layouts: 20.3 us -> 5.18 us
    reshape x5 -> x0, local copies, waits for them, and re-layouts: 10 us -> none  [the longest x1 4.26 us: attend_back(): return (query_grads, kv_grads.transpose(1, 0, 2).reshape(16, rows, 512))]
  transfers between devices with their start and end apart: 2 -> 2, of which waited for: 0 -> 0; matrix products, arithmetic and copies ran while one was open for 36% -> 16% of each run, Pallas kernels for 34% -> 63%
where the time goes in v3:
time: 556 us; the launch traced here: 552 us
  Pallas kernels  404 us (73%)
  matrix products  75.2 us (14%)
  other arithmetic  41.9 us (8%)
  between operations  15.2 us (3%)
  local copies, waits for them, and re-layouts  15 us (3%)
    pallas_call x6, Pallas kernels, comm_call(): pl.pallas_call(body, out_shape=outputs, in_specs=in_specs, out_specs=out_...  349 us
    pallas_call x2, Pallas kernels, attention_call(): pl.pallas_call(kernel, grid_spec=pltpu.PrefetchScalarGridSpec(num_scalar_...  47.6 us
    dot_general x6, matrix products, times(): return jnp.dot(left, right, preferred_element_type=F32)  30.3 us
    dot_general x4, matrix products, times_transposed(): lax.dot_general(left, right, (((1,), (1,)), ((), ())), preferred_element_...  26.5 us
    dot_general x12, matrix products, transposed_times(): lax.dot_general(left, right, (((0,), (0,)), ((), ())), preferred_element_...  18.4 us
  transfers between devices with their start and end apart: 2, of which 0 were waited for; matrix products, arithmetic and copies ran while one was open for 16% of the time, Pallas kernels for 63%

profile of v3, /device:TPU:1, one launch (start us, length us, event | category | flops | bytes accessed | tf_op | source)
XLA Modules:
  0.0 551.8 jit_solution(15117057226229773619)
XLA Ops:
  9.5 1.6 broadcast_select_fusion.refs_2_
  11.7 58.2 %shard_map.203 = (bf16[8,128,2048]{2,1,0:T(8,128)(2,1)}, bf16[8,16,256]{2,1,0:T(8,128)(2,1)}, bf16[32,2048]{1,0:T(8,128)(2,1)}, bf16[8,256,2048]{2,1,0:T(8,128)(2,1)}) custom-call(bf16[128,2048]{1,0:T(8,128)(2,1)} %refs_0_.1, bf16[16,256]{1,0:T(8,128)(2,1)} %maximum_maximum_fusion.refs_1_, bf16[32,2048]{1,0:T(8,128)(2,1)} %broadcast_select_fusion.refs_2_, ...), custom_call_target="tpu_custom_call" | custom-call | tf_op jit(solution)/shard_map/pallas_call | solution.py:248
  73.0 1.0 copy.25.cosine
  74.0 1.0 tile.20
  75.0 1.0 copy.26.sine
  76.0 1.4 slice_convert_fusion.7
  77.5 8.0 %shard_map.204 = (bf16[1024,2048]{1,0:T(8,128)(2,1)}, bf16[8,128,256]{2,1,0:T(8,128)(2,1)}, bf16[8,128,128]{2,1,0:T(8,128)(2,1)}) custom-call(s32[1]{0:T(128)} %bitcast.3.pair_ref, bf16[1024,2048]{1,0:T(8,128)(2,1)} %bitcast.70, f32[1,2048]{1,0:T(1,128)} %bitcast.90, bf16[256,2048]{1,0:T(8,128)(2,1)} %w_query.1, bf16[32,2048]{1,0:T(8,128)(2,1)} %w_key.1, ...), custom_call_target="tpu_custom_call" | custom-call | flops 2147483648 | bytes 10485760 | tf_op jit(solution)/shard_map/pallas_call | solution.py:495
  85.5 34.1 %shard_map.205 = (bf16[8,128,256]{2,1,0:T(8,128)(2,1)}, bf16[16,128,512]{2,1,0:T(8,128)(2,1)}) custom-call(bf16[8,128,256]{2,1,0:T(8,128)(2,1)} %get-tuple-element.40.refs_0_, bf16[8,128,128]{2,1,0:T(8,128)(2,1)} %get-tuple-element.41.refs_1_), custom_call_target="tpu_custom_call" | custom-call | tf_op jit(solution)/shard_map/pallas_call | solution.py:248
  120.2 22.7 %shard_map.206 = (bf16[128,2048]{1,0:T(8,128)(2,1)}, f32[4,8,512]{2,1,0:T(8,128)}) custom-call(s32[16]{0:T(128)} %and_select_fusion.2.order_ref, s32[1]{0:T(128)S(6)} %select_n.83.own_ref, bf16[8,128,256]{2,1,0:T(8,128)(2,1)} %get-tuple-element.42.q_ref, bf16[16,128,512]{2,1,0:T(8,128)(2,1)} %get-tuple-element.43.kv_ref), custom_call_target="tpu_custom_call" | custom-call | flops 8589934592 | bytes 8388608 | tf_op jit(solution)/shard_map/pallas_call | solution.py:652
  142.9 5.0 multiply_reduce_fusion.4
  147.9 1.0 copy-done.2
  148.9 1.0 multiply_convert_fusion.3.refs_0_
  149.8 40.9 %shard_map.207 = bf16[8,128,2048]{2,1,0:T(8,128)(2,1)} custom-call(bf16[128,2048]{1,0:T(8,128)(2,1)} %multiply_convert_fusion.3.refs_0_), custom_call_target="tpu_custom_call" | custom-call | tf_op jit(solution)/shard_map/pallas_call | solution.py:248
  190.7 1.6 constant_dynamic-slice_fusion.1.cos_ref.refs_5_
  192.3 1.5 constant_dynamic-slice_fusion.sin_ref.refs_6_
  193.8 3.1 multiply_reduce_fusion.1
  196.9 6.7 %fusion.103 = f32[1024,704]{0,1:T(8,128)} fusion(bf16[1024,2048]{1,0:T(8,128)(2,1)S(1)} %bitcast.75, bf16[704,2048]{1,0:T(8,128)(2,1)} %param.22), kind=kOutput, calls=%fused_computation.141 | convolution fusion | flops 2952790016 | bytes 9961472 | tf_op jit(solution)/shard_map/dot_general | solution.py:30
  203.6 4.8 fusion.102
  208.4 7.8 %multiply_convert_fusion = (bf16[1024,704]{0,1:T(8,128)(2,1)S(1)}, bf16[1024,704]{0,1:T(8,128)(2,1)S(1)}, bf16[1024,704]{0,1:T(8,128)(2,1)S(1)}) fusion(f32[1024,704]{0,1:T(8,128)} %fusion.102, f32[1024,704]{0,1:T(8,128)} %fusion.103, bf16[1024,2048]{1,0:T(8,128)(2,1)} %all-gather.2.cloned.1.call-done, bf16[704,2048]{1,0:T(8,128)(2,1)S(1)} %copy-done), kind=kOutput, calls=%fused_computation.10 | convolution fusion | flops 2963603456 | bytes 17170432 | tf_op jit(solution)/shard_map/dot_general | solution.py:30
  216.2 2.8 fusion.34
  219.0 2.8 fusion.28
  221.8 2.8 fusion.31
  224.6 2.8 fusion.25
  227.3 5.9 %fusion.104 = f32[1024,2048]{1,0:T(8,128)} fusion(bf16[1024,704]{0,1:T(8,128)(2,1)S(1)} %get-tuple-element.73, bf16[704,2048]{1,0:T(8,128)(2,1)S(1)} %copy-done.25), kind=kOutput, calls=%fused_computation.142 | convolution fusion | flops 2952790016 | bytes 12713984 | tf_op jit(solution)/shard_map/dot_general | solution.py:26
  233.2 5.1 convolution_convert_fusion
  238.4 1.8 copy-done.26
  240.2 8.0 %add_convert_fusion = bf16[1024,2048]{1,0:T(8,128)(2,1)} fusion(f32[1024,2048]{1,0:T(8,128)} %fusion.104, bf16[1024,704]{0,1:T(8,128)(2,1)} %copy-done.30, bf16[704,2048]{1,0:T(8,128)(2,1)S(1)} %copy-done.26), kind=kOutput, calls=%fused_computation.2 | convolution fusion | flops 2956984320 | bytes 16908288 | tf_op jit(solution)/shard_map/dot_general | solution.py:26
  248.2 1.7 fusion.37
  250.0 2.3 pad_maximum_fusion.refs_1_
  252.3 1.7 fusion.40
  254.1 2.3 pad_maximum_fusion.1.refs_2_
  256.4 81.5 %shard_map.208 = (f32[128,2048]{1,0:T(8,128)}, bf16[2112,128]{1,0:T(8,128)(2,1)}) custom-call(bf16[8,128,2048]{2,1,0:T(8,128)(2,1)} %bitcast.74, bf16[2112,1024]{1,0:T(8,128)(2,1)} %pad_maximum_fusion.refs_1_, bf16[2112,1024]{1,0:T(8,128)(2,1)} %pad_maximum_fusion.1.refs_2_), custom_call_target="tpu_custom_call" | custom-call | tf_op jit(solution)/shard_map/pallas_call | solution.py:248
  337.9 1.5 multiply_reduce_fusion.2
  339.5 1.6 fusion.99.refs_2_
  341.1 7.3 %convolution_convert_fusion.1.grad_ref = bf16[128,2048]{1,0:T(8,128)(2,1)} fusion(bf16[128,2048]{1,0:T(8,128)(2,1)S(1)} %fusion.99.refs_2_, bf16[2048,2048]{1,0:T(8,128)(2,1)} %bitcast.69), kind=kOutput, calls=%fused_computation.16 | convolution fusion | flops 1074003968 | bytes 9437184 | tf_op jit(solution)/shard_map/dot_general | solution.py:30
  348.3 24.8 %shard_map.209 = (bf16[128,2048]{1,0:T(8,128)(2,1)}, bf16[16,128,512]{2,1,0:T(8,128)(2,1)}) custom-call(s32[16]{0:T(128)} %and_select_fusion.2.order_ref, s32[1]{0:T(128)S(6)} %select_n.83.own_ref, bf16[8,128,256]{2,1,0:T(8,128)(2,1)} %get-tuple-element.42.q_ref, bf16[16,128,512]{2,1,0:T(8,128)(2,1)} %get-tuple-element.43.kv_ref, ...), custom_call_target="tpu_custom_call" | custom-call | flops 17179869184 | bytes 8388608 | tf_op jit(solution)/shard_map/pallas_call | solution.py:652
  373.2 67.9 %shard_map.210 = (bf16[2112,2048]{1,0:T(8,128)(2,1)}, bf16[8,128,2048]{2,1,0:T(8,128)(2,1)}, bf16[8,128,256]{2,1,0:T(8,128)(2,1)}, bf16[8,128,256]{2,1,0:T(8,128)(2,1)}, bf16[8,128,128]{2,1,0:T(8,128)(2,1)}) custom-call(bf16[16,128,512]{2,1,0:T(8,128)(2,1)} %get-tuple-element.49.refs_0_, bf16[2112,128]{1,0:T(8,128)(2,1)} %get-tuple-element.50.refs_1_, ...), custom_call_target="tpu_custom_call" | custom-call | tf_op jit(solution)/shard_map/pallas_call | solution.py:248
  441.2 2.3 fusion.68
  443.9 3.9 multiply_reduce_fusion
  452.1 1.1 pad_maximum_fusion.2.refs_1_
  455.2 1.1 pad_maximum_fusion.3.refs_2_
  456.3 66.3 %shard_map.211 = (f32[128,2048]{1,0:T(8,128)}, bf16[576,2048]{1,0:T(8,128)(2,1)}, f32[8,256]{1,0:T(8,128)}) custom-call(bf16[8,128,2048]{2,1,0:T(8,128)(2,1)} %bitcast.71, bf16[576,1024]{1,0:T(8,128)(2,1)} %pad_maximum_fusion.2.refs_1_, bf16[576,1024]{1,0:T(8,128)(2,1)} %pad_maximum_fusion.3.refs_2_, f32[8,8,256]{2,1,0:T(8,128)} %concatenate.60.refs_3_), custom_call_target="tpu_custom_call" | custom-call | tf_op jit(solution)/shard_map/pallas_call | solution.py:248
  522.6 1.7 fusion.61
  524.3 1.3 fusion.101
  525.6 1.8 slice_convert_fusion.5
  527.4 2.5 slice_convert_fusion.3
  530.0 10.6 %slice_convert_fusion = (f32[704,2048]{1,0:T(8,128)}, f32[704,2048]{1,0:T(8,128)}, f32[704,2048]{1,0:T(8,128)}) fusion(bf16[2112,2048]{1,0:T(8,128)(2,1)} %get-tuple-element.60), kind=kLoop, calls=%fused_computation.7 | loop fusion | flops 4325376 | bytes 25952256 | tf_op jit(solution)/shard_map/convert_element_type | solution.py:836
  540.6 3.9 fusion.66
  (96 shorter events, 13.3 us)
Async XLA Ops:
  7.2 201.2 %copy-start = (bf16[704,2048]{1,0:T(8,128)(2,1)S(1)}, bf16[704,2048]{1,0:T(8,128)(2,1)}, u32[]{:S(2)}) copy-start(bf16[704,2048]{1,0:T(8,128)(2,1)} %param.23) | copy-start | bytes 8650756
  7.2 201.2 %all-gather.2.cloned.1.call-start = ((), (), s32[]{:S(2)}) async-start(), calls=%async_computation.2 | async-start | bytes 4718592 | tf_op jit(solution)/shard_map/all_gather | solution.py:727
  69.9 470.6 %reduce-scatter.2.cloned.1.call-start = ((), (), s32[]{:S(2)}) async-start(), calls=%async_computation.1 | async-start | bytes 4718592 | tf_op jit(solution)/shard_map/reduce_scatter | solution.py:800
  120.2 22.7 %copy-start.5 = (bf16[128,2048]{1,0:T(8,128)(2,1)S(1)}, bf16[128,2048]{1,0:T(8,128)(2,1)}, u32[]{:S(2)}) copy-start(bf16[128,2048]{1,0:T(8,128)(2,1)} %refs_0_.1) | copy-start | bytes 1572868
  147.9 1.0 copy-start.2
  190.7 6.2 %copy-start.9 = (bf16[8,128,2048]{2,1,0:T(8,128)(2,1)S(1)}, bf16[8,128,2048]{2,1,0:T(8,128)(2,1)}, u32[]{:S(2)}) copy-start(bf16[8,128,2048]{2,1,0:T(8,128)(2,1)} %shard_map.207) | copy-start | bytes 12582916
  196.9 6.7 %copy-start.24 = (bf16[704,2048]{1,0:T(8,128)(2,1)S(1)}, bf16[704,2048]{1,0:T(8,128)(2,1)}, u32[]{:S(2)}) copy-start(bf16[704,2048]{1,0:T(8,128)(2,1)} %param.21) | copy-start | bytes 8650756
  208.4 7.8 %copy-start.10 = (bf16[8,128,2048]{2,1,0:T(8,128)(2,1)S(1)}, bf16[8,128,2048]{2,1,0:T(8,128)(2,1)}, u32[]{:S(2)}) copy-start(bf16[8,128,2048]{2,1,0:T(8,128)(2,1)} %shard_map.207) | copy-start | bytes 12582916
  216.2 2.8 copy-start.30
  216.2 17.0 %copy-start.28 = (bf16[1024,704]{0,1:T(8,128)(2,1)}, bf16[1024,704]{0,1:T(8,128)(2,1)S(1)}, u32[]{:S(2)}) copy-start(bf16[1024,704]{0,1:T(8,128)(2,1)S(1)} %get-tuple-element.74) | copy-start | bytes 4325380
  224.6 2.8 copy-start.25
  238.3 1.8 copy-start.26
  240.2 8.0 %copy-start.22 = (bf16[1024,2048]{1,0:T(8,128)(2,1)S(1)}, bf16[1024,2048]{1,0:T(8,128)(2,1)}, u32[]{:S(2)}) copy-start(bf16[1024,2048]{1,0:T(8,128)(2,1)} %all-gather.2.cloned.1.call-done) | copy-start | bytes 12582916
  240.2 8.0 %copy-start.29 = (bf16[1024,704]{0,1:T(8,128)(2,1)S(1)}, bf16[1024,704]{0,1:T(8,128)(2,1)}, u32[]{:S(2)}) copy-start(bf16[1024,704]{0,1:T(8,128)(2,1)} %copy-done.28) | copy-start | bytes 4325380
  248.2 1.7 copy-start.15
  248.2 1.8 copy-start.16
  252.3 1.7 copy-start.13
  252.3 1.8 copy-start.14
  256.4 81.5 %copy-start.3 = (f32[128,2048]{1,0:T(8,128)S(1)}, f32[128,2048]{1,0:T(8,128)}, u32[]{:S(2)}) copy-start(f32[128,2048]{1,0:T(8,128)} %copy-done.2) | copy-start | bytes 3145732
  256.4 83.0 %copy-start.8 = (bf16[128,2048]{1,0:T(8,128)(2,1)S(1)}, bf16[128,2048]{1,0:T(8,128)(2,1)}, u32[]{:S(2)}) copy-start(bf16[128,2048]{1,0:T(8,128)(2,1)} %param.14) | copy-start | bytes 1572868
  341.1 7.3 %copy-start.7 = (bf16[128,2048]{1,0:T(8,128)(2,1)}, bf16[128,2048]{1,0:T(8,128)(2,1)S(1)}, u32[]{:S(2)}) copy-start(bf16[128,2048]{1,0:T(8,128)(2,1)S(1)} %fusion.99.refs_2_) | copy-start | bytes 1572868
  373.2 68.0 %copy-start.18 = (bf16[32,2048]{1,0:T(8,128)(2,1)S(1)}, bf16[32,2048]{1,0:T(8,128)(2,1)}, u32[]{:S(2)}) copy-start(bf16[32,2048]{1,0:T(8,128)(2,1)} %w_value.1) | copy-start | bytes 393220
  373.2 68.0 %copy-start.19 = (bf16[32,2048]{1,0:T(8,128)(2,1)S(1)}, bf16[32,2048]{1,0:T(8,128)(2,1)}, u32[]{:S(2)}) copy-start(bf16[32,2048]{1,0:T(8,128)(2,1)} %w_key.1) | copy-start | bytes 393220
  441.2 2.4 copy-start.4
  441.2 2.6 copy-start.17
  441.2 2.7 copy-start.20
  443.9 4.6 copy-start.6
  443.9 5.2 copy-start.11
  449.0 2.2 copy-start.23
  449.1 2.3 copy-start.27
  456.3 66.3 %copy-start.21 = (f32[8,1,256]{2,1,0:T(1,128)S(1)}, f32[8,1,256]{2,1,0:T(1,128)}, u32[]{:S(2)}) copy-start(f32[8,1,256]{2,1,0:T(1,128)} %get-tuple-element.86) | copy-start | bytes 24580
  522.6 4.8 copy-start.12
  530.0 14.5 %copy-start.1 = (bf16[704,2048]{1,0:T(8,128)(2,1)S(1)}, bf16[704,2048]{1,0:T(8,128)(2,1)}, u32[]{:S(2)}) copy-start(bf16[704,2048]{1,0:T(8,128)(2,1)} %param.23) | copy-start | bytes 8650756
Sparse Core Ops, SparseCore 0:
  70.1 74.6 all-gather.1
  238.5 93.7 reduce-scatter.1

commit v4 on v3

--- a/solution.py
+++ b/solution.py
@@ -180,16 +180,68 @@
     link.kept_now(kept)
 
 
-def add_rows(target, terms, step=16):
+def gather_halves(link, axis, own, slot, share=None, start=0.0, block=10.5):
+    half = own.shape[0] // 2
+    cut = lambda ref, k: ref.at[pl.ds(k * half, half)]
+    piece = lambda index, k: cut(slot(index), k)
+    me, pair, far = chip(axis), chip(axis, 0, 1), chip(axis, 2, 0)
+    above_one, below_one = chip(axis, 1, 0), chip(axis, -1, 0)
+    last_pair, next_pair, far_pair = chip(axis, -1, 1), chip(axis, 1, 1), chip(axis, 2, 1)
+    sharing = lambda index, k: share(piece(index, k), index, k) if share else None
+    pass_on = lambda index, k, ring, pair_: link.send(piece(index, k), piece(index, k), axis, ring, pair_)
+    yield start
+    kept = link.keep(own, slot(me))
+    across, down, up = [], [], []
+    for k in range(2):
+        across.append(link.send(cut(own, k), piece(me, k), axis, 0, 1))
+        down.append(link.send(cut(own, k), piece(me, k), axis, -1, 0))
+        up.append(link.send(cut(own, k), piece(me, k), axis, 1, 0))
+    if share:
+        for k in range(2):
+            share(cut(own, k), me, k)
+    far_in, pair_up, pair_down, over = [], [], [], []
+    for k in range(2):
+        yield start + (k + 1) * block / 2 + 3.5
+        down[k].wait_recv()
+        up[k].wait_recv()
+        far_in.append(pass_on(above_one, k, -1, 0) if k == 0 else pass_on(below_one, k, 1, 0))
+        sharing(above_one, k)
+        sharing(below_one, k)
+        across[k].wait_recv()
+        pair_up.append(pass_on(pair, k, 1, 0))
+        pair_down.append(pass_on(pair, k, -1, 0))
+        sharing(pair, k)
+    link.kept_now(kept)
+    for k in range(2):
+        yield start + block + 7.0 + k * block / 2
+        far_in[k].wait_recv()
+        over.append(pass_on(far, k, 0, 1))
+        sharing(far, k)
+    yield start + 2.5 * block + 6.0
+    for k in range(2):
+        pair_up[k].wait_recv()
+        sharing(last_pair, k)
+        pair_down[k].wait_recv()
+        sharing(next_pair, k)
+    yield start + 2.5 * block + 9.0
+    for k in range(2):
+        over[k].wait_recv()
+        sharing(far_pair, k)
+
+
+def add_rows(target, terms):
+    rows, width = target.shape
+    step = max(s for s in range(16, rows + 1, 16) if rows % s == 0 and (s == 16 or s * width <= 32768))
+
     def body(i, _):
-        rows = pl.ds(pl.multiple_of(i * step, step), step)
-        total = terms[0][rows, :].astype(F32)
+        some = pl.ds(pl.multiple_of(i * step, 16), step)
+        total = terms[0][some, :].astype(F32)
         for term in terms[1:]:
-            total = total + term[rows, :].astype(F32)
-        target[rows, :] = total.astype(target.dtype)
+            total = total + term[some, :].astype(F32)
+        target[some, :] = total.astype(target.dtype)
         return 0
 
-    lax.fori_loop(0, target.shape[0] // step, body, 0)
+    lax.fori_loop(0, rows // step, body, 0)
 
 
 def scatter_job(link, axis, part, landing, work, result, start=0.0, block=10.5):
@@ -198,28 +250,27 @@
     to_last = link.send(here(2, 1), landing.at[1], axis, -1, 0)
     to_next = link.send(here(2, 0), landing.at[0], axis, 1, 0)
     pair_up = link.send(here(1, 1), landing.at[2], axis, 1, 0)
-    mine_down = link.send(here(3, 0), landing.at[3], axis, -1, 0)
-    spare = [here(3, 1), here(1, 0), here(0, 1), here(0, 0)]
     yield start + block + 3.0
     to_last.wait_recv()
-    add_rows(work.at[0], [spare[0], landing.at[1]])
+    add_rows(work.at[0], [here(3, 1), landing.at[1]])
     pair_down = link.send(work.at[0], landing.at[4], axis, -1, 0)
-    yield start + block + 3.1
+    yield start + block + 4.0
     to_next.wait_recv()
-    add_rows(work.at[1], [spare[1], landing.at[0]])
-    mine_up = link.send(work.at[1], landing.at[5], axis, 1, 0)
+    add_rows(work.at[1], [here(1, 0), landing.at[0]])
     yield start + 2 * block + 3.0
     pair_up.wait_recv()
+    mine_up = link.send(work.at[1], landing.at[5], axis, 1, 0)
+    mine_down = link.send(here(3, 0), landing.at[3], axis, -1, 0)
+    yield start + 2 * block + 6.0
+    pair_down.wait_recv()
+    add_rows(work.at[2], [here(0, 1), landing.at[2], landing.at[4]])
+    across = link.send(work.at[2], landing.at[6], axis, 0, 1)
+    yield start + 3 * block + 7.0
     mine_down.wait_recv()
-    yield start + 3 * block + 4.0
-    pair_down.wait_recv()
-    add_rows(work.at[2], [spare[2], landing.at[2], landing.at[4]])
-    across = link.send(work.at[2], landing.at[6], axis, 0, 1)
-    yield start + 3 * block + 4.1
     mine_up.wait_recv()
-    yield start + 4 * block + 8.0
+    yield start + 3 * block + 10.0
     across.wait_recv()
-    add_rows(result, [spare[3], landing.at[3], landing.at[5], landing.at[6]])
+    add_rows(result, [here(0, 0), landing.at[3], landing.at[5], landing.at[6]])
 
 
 def exchange_job(link, axis, part, slot, start=0.0, length=8.0):
@@ -237,7 +288,7 @@
 INSIDE = pl.BlockSpec(memory_space=pltpu.VMEM)
 
 
-def comm_call(kernel, number, inputs, in_specs, outputs, out_specs, scratch=()):
+def comm_call(kernel, number, inputs, in_specs, outputs, out_specs, scratch=(), limit=VMEM_LIMIT):
     sems = [pltpu.SemaphoreType.DMA((96,)), pltpu.SemaphoreType.DMA((96,)), pltpu.SemaphoreType.DMA((8,))]
 
     def body(*refs):
@@ -252,7 +303,7 @@
         out_specs=out_specs,
         scratch_shapes=[*scratch, *sems],
         compiler_params=pltpu.CompilerParams(
-            collective_id=number, has_side_effects=True, vmem_limit_bytes=VMEM_LIMIT
+            collective_id=number, has_side_effects=True, vmem_limit_bytes=limit
         ),
     )(*inputs)
 
@@ -309,7 +360,7 @@
         gather_job(link, "shard", w_out.at[mine], lambda i: out_full.at[i, mine], share, 0.0, 4.0),
         exchange_job(link, "shard", lambda i: small, lambda i: smalls.at[i], 0.0, 9.0),
         kv_job(),
-        gather_job(link, "shard", tokens, lambda i: token_rows.at[i], None, 0.1, 12.0),
+        gather_halves(link, "shard", tokens, lambda i: token_rows.at[i], None, 0.1, 12.0),
         ring_job(),
     )
 
@@ -338,56 +389,165 @@
     )
 
 
-def gather_kernel(link, own, slots):
-    link.greet(near("shard"))
-    run(gather_job(link, "shard", own, lambda i: slots.at[i]))
-
-
-REDUCE_ORDER = [(2, 1), (2, 0), (1, 1), (3, 0), (3, 1), (1, 0), (0, 1), (0, 0)]
+def column_block(ref, index, width=LANES):
+    return ref.at[:, pl.ds(pl.multiple_of(index * width, width), width)]
 
 
 def reduced(link, theirs, mine, from_sibling, landing, work, summed, start=0.0, block=10.8):
-    columns = lambda ref, i: ref.at[:, pl.ds(pl.multiple_of(i * LANES, LANES), LANES)]
-    copies = {}
-    for r, p in REDUCE_ORDER:
-        i = chip("ctx", r, p)
-        copies[r, p] = link.send(columns(theirs, i), columns(from_sibling, i), "ctx", 0, 0, 1)
-    offsets = iter(REDUCE_ORDER)
-
-    def part(i):
-        r, p = reduce_at[0]
-        copies[r, p].wait_recv()
-        add_rows(columns(from_sibling, i), [columns(mine, i), columns(from_sibling, i)])
-        return columns(from_sibling, i)
-
-    reduce_at = [None]
-
-    class Parts:
-        def __call__(self, i):
-            reduce_at[0] = next(offsets)
-            return part(i)
-
-    yield from scatter_job(link, "ctx", Parts(), landing, work, summed, start, block)
-
-
-def spread(link, summed, full, start=0.0, block=10.8):
+    copy = link.send(theirs, from_sibling, "ctx", 0, 0, 1)
+    yield start
+    copy.wait_recv()
+    add_rows(from_sibling, [mine, from_sibling])
+    part = lambda i: column_block(from_sibling, i)
+    yield from scatter_job(link, "ctx", part, landing, work, summed, start + 2.0, block)
+
+
+def spread(link, summed, full, gather, start=0.0, block=10.8):
     core = lax.rem(lax.axis_index("ctx"), 2)
-    slot = lambda i: full.at[:, pl.ds(pl.multiple_of((core * 8 + i) * LANES, LANES), LANES)]
+    slot = lambda i: column_block(full, core * 8 + i)
     sibs = []
 
-    def share(index, block):
-        sibs.append(link.send(block, slot(index), "ctx", 0, 0, 1))
-
-    yield from gather_job(link, "ctx", summed, slot, share, start, block)
+    def share(index, source):
+        sibs.append(link.send(source, slot(index), "ctx", 0, 0, 1))
+
+    def share_half(source, index, k):
+        half = source.shape[0]
+        sibs.append(link.send(source, slot(index).at[pl.ds(k * half, half)], "ctx", 0, 0, 1))
+
+    yield from gather(link, "ctx", summed, slot, share if gather is gather_job else share_half, start, block)
     for copy in sibs:
         copy.wait_recv()
 
 
-def middle_kernel(link, parts, theirs, mine, result, summed, land_a, work_a, sib, land_b, work_b):
+def contract_rows(left, right):
+    return lax.dot_general(left, right, (((0,), (0,)), ((), ())), preferred_element_type=F32)
+
+
+def ffn_kernel(link, own, og, w_gate, w_up, w_down, result, down_parts, summed,
+               rows_all, gate_t, up_t, inner_t, parts, land_a, work_a, theirs, sib, land_b, work_b):
     link.greet(near("shard") + near("ctx") + SIBLING)
+    core = lax.rem(lax.axis_index("ctx"), 2)
+    count = own.shape[0]
+    ff = w_gate.shape[0]
+    here = lambda ref, i: ref.at[pl.ds(pl.multiple_of(i * count, count), count)]
+    token_lanes = lambda i: pl.ds(pl.multiple_of(i * count, count), count)
+
+    def pair_of(ref, slots):
+        return jnp.concatenate([here(ref, i)[...] for i in slots], axis=0)
+
+    def forward(*offsets):
+        slots = [chip("shard", r, p) for r, p in offsets]
+        x = pair_of(rows_all, slots)
+        gate = times_transposed(w_gate[...], x)
+        up = times_transposed(w_up[...], x)
+        inner_grad = times_transposed(w_down[...], pair_of(og, slots))
+        sigmoid = 1.0 / (1.0 + jnp.exp(-gate))
+        activated = gate * sigmoid
+        inner = (activated * up).astype(LOW)
+        gate_grad = (inner_grad * up * sigmoid * (1.0 + gate * (1.0 - sigmoid))).astype(LOW)
+        up_grad = (inner_grad * activated).astype(LOW)
+        for k, i in enumerate(slots):
+            lanes = slice(k * count, k * count + count)
+            inner_t[:, token_lanes(i)] = inner[:, lanes]
+            gate_t[:, token_lanes(i)] = gate_grad[:, lanes]
+            up_t[:, token_lanes(i)] = up_grad[:, lanes]
+        return slots
+
+    def tokens_of(ref, slots):
+        return jnp.concatenate([ref[:, token_lanes(i)] for i in slots], axis=1)
+
+    def back(slots):
+        gates, ups = tokens_of(gate_t, slots), tokens_of(up_t, slots)
+        for c in range(2):
+            some = slice(c * 1024, c * 1024 + 1024)
+            block = contract_rows(gates, w_gate[:, some]) + contract_rows(ups, w_up[:, some])
+            for k, i in enumerate(slots):
+                parts[i, :, some] = block[k * count : k * count + count].astype(LOW)
+
+    def down(slots):
+        inners = tokens_of(inner_t, slots)
+        for c in range(2):
+            some = slice(c * 1024, c * 1024 + 1024)
+            block = contract_rows(inners, w_down[:, some])
+            for k, i in enumerate(slots):
+                down_parts[i, :, some] = block[k * count : k * count + count].astype(LOW)
+
+    def every(*offsets):
+        slots = forward(*offsets)
+        back(slots)
+        down(slots)
+
+    last_pair_slots = []
+
+    def compute_job():
+        yield 15.0
+        every((0, 0), (0, 1))
+        yield 21.5
+        every((1, 0), (3, 0))
+        yield 33.0
+        every((2, 0), (1, 1))
+        yield 36.0
+        slots = forward((3, 1), (2, 1))
+        back(slots)
+        last_pair_slots.append(slots)
+
+    run(
+        gather_halves(link, "shard", own, lambda i: here(rows_all, i)),
+        compute_job(),
+    )
+
+    ring = chip("ctx") // 2
+
+    def weight_columns(target, half, further, extra=None):
+        wide = lax.rem(ring + further, 4)
+        columns = pl.ds(pl.multiple_of(half * 1024 + wide * 256, 256), 256)
+        into = pl.ds(pl.multiple_of(wide * 256, 256), 256)
+        for i, (left, right) in enumerate(((gate_t, rows_all), (up_t, rows_all), (inner_t, og))):
+            some = slice(i * ff, i * ff + ff)
+            block = times(left[...], right[:, columns])
+            if extra is not None:
+                block = block + extra[some, into].astype(F32)
+            target[some, into] = block.astype(LOW)
+        return wide
+
+    def weight_job():
+        copies = {}
+
+        def give(further):
+            wide = weight_columns(theirs, 1 - core, further)
+            copies[further] = link.send(
+                column_block(theirs, wide, 256), column_block(sib, wide, 256), "ctx", 0, 0, 1
+            )
+
+        def take(further):
+            copies[further].wait_recv()
+            weight_columns(sib, core, further, sib)
+
+        yield 0.1
+        give(2)
+        yield 1.0
+        give(1)
+        yield 2.0
+        take(2)
+        scatter = scatter_job(link, "ctx", lambda i: column_block(sib, i), land_b, work_b, summed, 6.0, 10.8)
+        yield 3.0
+        give(3)
+        take(1)
+        next(scatter)
+        later = next(scatter)
+        yield 4.0
+        down(last_pair_slots[0])
+        yield 5.0
+        give(0)
+        take(3)
+        yield 6.0
+        take(0)
+        yield later
+        yield from scatter
+
     run(
         scatter_job(link, "shard", lambda i: parts.at[i], land_a, work_a, result),
-        reduced(link, theirs, mine, sib, land_b, work_b, summed, 4.0),
+        weight_job(),
     )
 
 
@@ -425,8 +585,8 @@
     columns = lambda ref: lambda i: ref.at[:, pl.ds(pl.multiple_of(i * 256, 256), 256)]
     run(
         kv_job(),
-        gather_job(link, "shard", hidden, lambda i: hidden_rows.at[i], None, 0.2),
-        spread(link, summed, full, 5.0),
+        gather_halves(link, "shard", hidden, lambda i: hidden_rows.at[i], None, 0.2),
+        spread(link, summed, full, gather_halves, 5.0),
         exchange_job(link, "shard", columns(queries), lambda i: query_cols.at[i], 27.0, 20.0),
         exchange_job(link, "shard", columns(attended), lambda i: attended_cols.at[i], 27.1, 21.0),
     )
@@ -438,7 +598,7 @@
 
     def weight_job():
         yield from reduced(link, theirs, mine, sib, land_b, work_b, summed, 0.0, 3.0)
-        yield from spread(link, summed, full, 24.0, 3.0)
+        yield from spread(link, summed, full, gather_job, 24.0, 3.0)
 
     def gain_job():
         yield from exchange_job(link, "shard", lambda i: gains.at[i], lambda i: gain_land.at[i], 0.2, 8.0)
@@ -751,22 +911,31 @@
     inputs = tokens.astype(F32)
     hidden_state = inputs + times(attended, out_full)
     normed_two, inverse_two = rms_forward(hidden_state, gain_two)
-    (normed_two_rows,) = comm_call(
-        gather_kernel, 2, [normed_two.astype(LOW)], [ANY], [shape((8, rows, D), LOW)], [ANY]
-    )
-    normed_two_rows = normed_two_rows.reshape(-1, D)
-
-    gate = times_transposed(normed_two_rows, w_gate)
-    up_part = times_transposed(normed_two_rows, w_up)
-    inner_grad = times_transposed(out_grad_rows, w_down)
-    sigmoid = jax.nn.sigmoid(gate)
-    activated = gate * sigmoid
-    inner = (activated * up_part).astype(LOW)
-    gate_grad = (inner_grad * up_part * sigmoid * (1.0 + gate * (1.0 - sigmoid))).astype(LOW)
-    up_grad = (inner_grad * activated).astype(LOW)
-    normed_two_parts = (times(gate_grad, w_gate) + times(up_grad, w_up)).astype(LOW)
-    down_parts = times(inner, w_down).astype(LOW)
-
+    ff = w_gate.shape[0]
+    vmem = lambda count, *dims: pltpu.VMEM((count, *dims), LOW)
+    normed_two_grad, down_parts, summed = comm_call(
+        ffn_kernel,
+        3,
+        [normed_two.astype(LOW), out_grad_rows, w_gate, w_up, w_down],
+        [ANY] + [INSIDE] * 4,
+        [shape((rows, D), F32), shape((8, rows, D), LOW), shape((3 * ff, LANES), LOW)],
+        [INSIDE] * 3,
+        [
+            vmem(8 * rows, D),
+            vmem(ff, 8 * rows),
+            vmem(ff, 8 * rows),
+            vmem(ff, 8 * rows),
+            vmem(8, rows, D),
+            vmem(7, rows, D),
+            vmem(3, rows, D),
+            vmem(3 * ff, 1024),
+            vmem(3 * ff, 1024),
+            vmem(7, 3 * ff, LANES),
+            vmem(3, 3 * ff, LANES),
+        ],
+        62 * 1024 * 1024,
+    )
+    down_parts = down_parts.reshape(-1, D)
     def halves(terms):
         def one(which):
             cut = lambda m: lax.dynamic_slice_in_dim(m, which * 1024, 1024, axis=1)
@@ -775,27 +944,6 @@
             )
 
         return one(1 - core), one(core)
-
-    ff = w_gate.shape[0]
-    theirs, mine = halves(
-        [(gate_grad, normed_two_rows), (up_grad, normed_two_rows), (inner, out_grad_rows)]
-    )
-    vmem = lambda count, *dims: pltpu.VMEM((count, *dims), LOW)
-    normed_two_grad, summed = comm_call(
-        middle_kernel,
-        3,
-        [blocks(normed_two_parts), theirs, mine],
-        [INSIDE, ANY, INSIDE],
-        [shape((rows, D), F32), shape((3 * ff, LANES), LOW)],
-        [INSIDE, INSIDE],
-        [
-            vmem(7, rows, D),
-            vmem(3, rows, D),
-            pltpu.VMEM((3 * ff, 1024), LOW),
-            vmem(7, 3 * ff, LANES),
-            vmem(3, 3 * ff, LANES),
-        ],
-    )
 
     down_sum = lax.psum_scatter(down_parts, "shard", scatter_dimension=0, tiled=True)
     outputs = (hidden_state + down_sum.astype(F32)).astype(LOW)

time: 556 us -> 487 us (0.88)
  matrix products: 75.2 us -> 22.6 us
  other arithmetic: 41.9 us -> 33.4 us
  Pallas kernels: 404 us -> 398 us
    dot_general x4 -> x1, matrix products: 26.5 us -> 7.28 us  [times_transposed(): lax.dot_general(left, right, (((1,), (1,)), ((), ())), preferred_element_...]
    dot_general x6 -> x3, matrix products: 30.3 us -> 11.4 us  [times(): return jnp.dot(left, right, preferred_element_type=F32)]
    dot_general x12 -> x6, matrix products: 18.4 us -> 3.97 us  [transposed_times(): lax.dot_general(left, right, (((0,), (0,)), ((), ())), preferred_element_...]
    pallas_call x6 -> x5, Pallas kernels: 349 us -> 342 us  [comm_call(): pl.pallas_call(body, out_shape=outputs, in_specs=in_specs, out_specs=out_...]
  transfers between devices with their start and end apart: 2 -> 2, of which waited for: 0 -> 0; matrix products, arithmetic and copies ran while one was open for 16% -> 12% of each run, Pallas kernels for 63% -> 50%
where the time goes in v4:
time: 487 us; the launch traced here: 481 us
  Pallas kernels  398 us (82%)
  other arithmetic  33.4 us (7%)
  matrix products  22.6 us (5%)
  between operations  14.8 us (3%)
  local copies, waits for them, and re-layouts  11.5 us (2%)
    pallas_call x5, Pallas kernels, comm_call(): pl.pallas_call(body, out_shape=outputs, in_specs=in_specs, out_specs=out_...  342 us
    pallas_call x2, Pallas kernels, attention_call(): pl.pallas_call(kernel, grid_spec=pltpu.PrefetchScalarGridSpec(num_scalar_...  48.5 us
    dot_general x3, matrix products, times(): return jnp.dot(left, right, preferred_element_type=F32)  11.4 us
    convert_element_type x1, other arithmetic, local(): ffn_full[i * ff:(i + 1) * ff].astype(F32)  10.5 us
  transfers between devices with their start and end apart: 2, of which 0 were waited for; matrix products, arithmetic and copies ran while one was open for 12% of the time, Pallas kernels for 50%

profile of v4, /device:TPU:1, one launch (start us, length us, event | category | flops | bytes accessed | tf_op | source)
XLA Modules:
  0.0 480.9 jit_solution(8968002472904101960)
XLA Ops:
  7.2 0.7 fusion.60
  7.9 0.7 stack.16
  8.6 0.7 stack.17
  9.3 1.6 broadcast_select_fusion.refs_2_
  10.9 0.7 maximum_maximum_fusion.refs_1_
  11.6 54.6 %shard_map.203 = (bf16[8,128,2048]{2,1,0:T(8,128)(2,1)}, bf16[8,16,256]{2,1,0:T(8,128)(2,1)}, bf16[32,2048]{1,0:T(8,128)(2,1)}, bf16[8,256,2048]{2,1,0:T(8,128)(2,1)}) custom-call(bf16[128,2048]{1,0:T(8,128)(2,1)} %refs_0_.1, bf16[16,256]{1,0:T(8,128)(2,1)} %maximum_maximum_fusion.refs_1_, bf16[32,2048]{1,0:T(8,128)(2,1)} %broadcast_select_fusion.refs_2_, ...), custom_call_target="tpu_custom_call" | custom-call | tf_op jit(solution)/shard_map/pallas_call | solution.py:299
  66.3 0.8 copy.29
  67.2 0.7 convert_add_fusion
  68.0 0.5 fusion.52
  68.6 1.0 copy.25.cosine
  69.6 1.0 copy.26.sine
  70.6 1.4 slice_convert_fusion.7
  72.1 7.5 %shard_map.204 = (bf16[1024,2048]{1,0:T(8,128)(2,1)}, bf16[8,128,256]{2,1,0:T(8,128)(2,1)}, bf16[8,128,128]{2,1,0:T(8,128)(2,1)}) custom-call(s32[1]{0:T(128)} %bitcast.3.pair_ref, bf16[1024,2048]{1,0:T(8,128)(2,1)} %bitcast.51, f32[1,2048]{1,0:T(1,128)} %bitcast.65, bf16[256,2048]{1,0:T(8,128)(2,1)} %w_query.1, bf16[32,2048]{1,0:T(8,128)(2,1)} %w_key.1, ...), custom_call_target="tpu_custom_call" | custom-call | flops 2147483648 | bytes 10485760 | tf_op jit(solution)/shard_map/pallas_call | solution.py:655
  79.6 34.4 %shard_map.205 = (bf16[8,128,256]{2,1,0:T(8,128)(2,1)}, bf16[16,128,512]{2,1,0:T(8,128)(2,1)}) custom-call(bf16[8,128,256]{2,1,0:T(8,128)(2,1)} %get-tuple-element.41.refs_0_, bf16[8,128,128]{2,1,0:T(8,128)(2,1)} %get-tuple-element.42.refs_1_), custom_call_target="tpu_custom_call" | custom-call | tf_op jit(solution)/shard_map/pallas_call | solution.py:299
  114.0 1.5 constant_dynamic-slice_fusion.1.cos_ref.refs_5_
  115.5 1.5 constant_dynamic-slice_fusion.sin_ref.refs_6_
  116.9 0.5 and_select_fusion.2.order_ref
  117.5 23.2 %shard_map.206 = (bf16[128,2048]{1,0:T(8,128)(2,1)}, f32[4,8,512]{2,1,0:T(8,128)}) custom-call(s32[16]{0:T(128)} %and_select_fusion.2.order_ref, s32[1]{0:T(128)S(6)} %select_n.77.own_ref, bf16[8,128,256]{2,1,0:T(8,128)(2,1)} %get-tuple-element.43.q_ref, bf16[16,128,512]{2,1,0:T(8,128)(2,1)} %get-tuple-element.44.kv_ref), custom_call_target="tpu_custom_call" | custom-call | flops 8589934592 | bytes 8388608 | tf_op jit(solution)/shard_map/pallas_call | solution.py:812
  140.7 5.1 %multiply_reduce_fusion.4 = (f32[128]{0:T(128)S(1)}, f32[128,2048]{1,0:T(8,128)S(1)}) fusion(bf16[128,2048]{1,0:T(8,128)(2,1)} %get-tuple-element.45.out_ref.refs_4_, bf16[2048,2048]{1,0:T(8,128)(2,1)} %bitcast.49, bf16[128,2048]{1,0:T(8,128)(2,1)S(1)} %copy-done.3), kind=kOutput, calls=%fused_computation.45 | convolution fusion | flops 1074790272 | bytes 10486272 | tf_op jit(solution)/shard_map/dot_general | solution.py:26
  145.8 0.9 multiply_reduce_fusion.1
  146.7 1.0 multiply_convert_fusion.refs_0_
  147.7 102.6 %shard_map.207 = (f32[128,2048]{1,0:T(8,128)}, bf16[8,128,2048]{2,1,0:T(8,128)(2,1)}, bf16[2112,128]{1,0:T(8,128)(2,1)}) custom-call(bf16[128,2048]{1,0:T(8,128)(2,1)} %multiply_convert_fusion.refs_0_, bf16[1024,2048]{1,0:T(8,128)(2,1)} %all-gather.2.cloned.1.call-done.refs_1_, bf16[704,2048]{1,0:T(8,128)(2,1)} %refs_2_.1, bf16[704,2048]{1,0:T(8,128)(2,1)} %refs_3_.3, ...), custom_call_target="tpu_custom_call" | custom-call | tf_op jit(solution)/shard_map/pallas_call | solution.py:299
  250.3 1.2 copy-done.2
  251.5 0.3 multiply_reduce_fusion.2
  251.8 1.4 fusion.62.refs_2_
  253.2 7.3 %convolution_convert_fusion.grad_ref = bf16[128,2048]{1,0:T(8,128)(2,1)} fusion(bf16[128,2048]{1,0:T(8,128)(2,1)S(1)} %fusion.62.refs_2_, bf16[2048,2048]{1,0:T(8,128)(2,1)} %bitcast.50), kind=kOutput, calls=%fused_computation.7 | convolution fusion | flops 1074003968 | bytes 9437184 | tf_op jit(solution)/shard_map/dot_general | solution.py:30
  260.5 25.2 %shard_map.208 = (bf16[128,2048]{1,0:T(8,128)(2,1)}, bf16[16,128,512]{2,1,0:T(8,128)(2,1)}) custom-call(s32[16]{0:T(128)} %and_select_fusion.2.order_ref, s32[1]{0:T(128)S(6)} %select_n.77.own_ref, bf16[8,128,256]{2,1,0:T(8,128)(2,1)} %get-tuple-element.43.q_ref, bf16[16,128,512]{2,1,0:T(8,128)(2,1)} %get-tuple-element.44.kv_ref, ...), custom_call_target="tpu_custom_call" | custom-call | flops 17179869184 | bytes 8388608 | tf_op jit(solution)/shard_map/pallas_call | solution.py:812
  285.8 87.1 %shard_map.209 = (bf16[2112,2048]{1,0:T(8,128)(2,1)}, bf16[8,128,2048]{2,1,0:T(8,128)(2,1)}, bf16[8,128,256]{2,1,0:T(8,128)(2,1)}, bf16[8,128,256]{2,1,0:T(8,128)(2,1)}, bf16[8,128,128]{2,1,0:T(8,128)(2,1)}) custom-call(bf16[16,128,512]{2,1,0:T(8,128)(2,1)} %get-tuple-element.51.refs_0_, bf16[2112,128]{1,0:T(8,128)(2,1)} %get-tuple-element.52.refs_1_, ...), custom_call_target="tpu_custom_call" | custom-call | tf_op jit(solution)/shard_map/pallas_call | solution.py:299
  373.0 2.3 fusion.37
  375.7 3.9 multiply_reduce_fusion
  379.6 0.6 concatenate.52.refs_3_
  380.6 0.3 maximum_select_fusion.2
  380.9 0.5 fusion.24
  381.4 0.7 fusion.12
  382.1 0.3 copy-done.12
  382.6 0.7 fusion.18
  383.3 1.1 pad_maximum_fusion.refs_1_
  384.4 0.5 fusion.27
  384.9 0.7 fusion.15
  385.7 0.7 fusion.21
  386.5 1.1 pad_maximum_fusion.1.refs_2_
  387.6 63.8 %shard_map.210 = (f32[128,2048]{1,0:T(8,128)}, bf16[576,2048]{1,0:T(8,128)(2,1)}, f32[8,256]{1,0:T(8,128)}) custom-call(bf16[8,128,2048]{2,1,0:T(8,128)(2,1)} %bitcast.52, bf16[576,1024]{1,0:T(8,128)(2,1)} %pad_maximum_fusion.refs_1_, bf16[576,1024]{1,0:T(8,128)(2,1)} %pad_maximum_fusion.1.refs_2_, f32[8,8,256]{2,1,0:T(8,128)} %concatenate.52.refs_3_), custom_call_target="tpu_custom_call" | custom-call | tf_op jit(solution)/shard_map/pallas_call | solution.py:299
  451.3 1.5 fusion.30
  452.9 1.3 fusion.64
  454.2 1.8 slice_convert_fusion.5
  456.0 4.1 slice_convert_fusion.3
  460.1 10.5 %slice_convert_fusion = (f32[704,2048]{1,0:T(8,128)}, f32[704,2048]{1,0:T(8,128)}, f32[704,2048]{1,0:T(8,128)}) fusion(bf16[2112,2048]{1,0:T(8,128)(2,1)} %get-tuple-element.62), kind=kLoop, calls=%fused_computation.3 | loop fusion | flops 4325376 | bytes 25952256 | tf_op jit(solution)/shard_map/convert_element_type | solution.py:984
  470.5 3.3 fusion.35
  (47 shorter events, 1.1 us)
Async XLA Ops:
  7.2 140.5 %all-gather.2.cloned.1.call-start = ((), (), s32[]{:S(2)}) async-start(), calls=%async_computation.1 | async-start | bytes 4718592 | tf_op jit(solution)/shard_map/all_gather | solution.py:887
  66.2 404.4 %reduce-scatter.2.cloned.1.call-start = ((), (), s32[]{:S(2)}) async-start(), calls=%async_computation.2 | async-start | bytes 4718592 | tf_op jit(solution)/shard_map/reduce_scatter | solution.py:948
  117.5 23.2 %copy-start.3 = (bf16[128,2048]{1,0:T(8,128)(2,1)S(1)}, bf16[128,2048]{1,0:T(8,128)(2,1)}, u32[]{:S(2)}) copy-start(bf16[128,2048]{1,0:T(8,128)(2,1)} %refs_0_.1) | copy-start | bytes 1572868
  140.7 5.1 %copy-start = (bf16[8,128,2048]{2,1,0:T(8,128)(2,1)S(1)}, bf16[8,128,2048]{2,1,0:T(8,128)(2,1)}, u32[]{:S(2)}) copy-start(bf16[8,128,2048]{2,1,0:T(8,128)(2,1)} %get-tuple-element.38) | copy-start | bytes 12582916
  250.3 1.2 copy-start.2
  253.2 7.3 %copy-start.5 = (bf16[128,2048]{1,0:T(8,128)(2,1)}, bf16[128,2048]{1,0:T(8,128)(2,1)S(1)}, u32[]{:S(2)}) copy-start(bf16[128,2048]{1,0:T(8,128)(2,1)S(1)} %fusion.62.refs_2_) | copy-start | bytes 1572868
  285.8 87.2 %copy-start.8 = (bf16[32,2048]{1,0:T(8,128)(2,1)S(1)}, bf16[32,2048]{1,0:T(8,128)(2,1)}, u32[]{:S(2)}) copy-start(bf16[32,2048]{1,0:T(8,128)(2,1)} %w_value.1) | copy-start | bytes 393220
  285.8 87.2 %copy-start.9 = (bf16[32,2048]{1,0:T(8,128)(2,1)S(1)}, bf16[32,2048]{1,0:T(8,128)(2,1)}, u32[]{:S(2)}) copy-start(bf16[32,2048]{1,0:T(8,128)(2,1)} %w_key.1) | copy-start | bytes 393220
  373.0 2.4 copy-start.1
  373.0 2.6 copy-start.7
  373.0 2.7 copy-start.10
  375.7 4.6 copy-start.4
  375.7 5.2 %copy-start.6 = (bf16[1024,2048]{1,0:T(8,128)(2,1)S(1)}, bf16[1024,2048]{1,0:T(8,128)(2,1)}, u32[]{:S(2)}) copy-start(bf16[1024,2048]{1,0:T(8,128)(2,1)} %get-tuple-element.56) | copy-start | bytes 12582916
  380.3 2.2 copy-start.12
  380.3 2.3 copy-start.13
  386.4 64.9 %copy-start.11 = (f32[8,1,256]{2,1,0:T(1,128)S(1)}, f32[8,1,256]{2,1,0:T(1,128)}, u32[]{:S(2)}) copy-start(f32[8,1,256]{2,1,0:T(1,128)} %get-tuple-element.85) | copy-start | bytes 24580
Sparse Core Ops, SparseCore 0:
  66.3 75.5 all-gather.1
  250.4 109.9 reduce-scatter.1

commit v5 on v4

--- a/solution.py
+++ b/solution.py
@@ -289,7 +289,7 @@
 
 
 def comm_call(kernel, number, inputs, in_specs, outputs, out_specs, scratch=(), limit=VMEM_LIMIT):
-    sems = [pltpu.SemaphoreType.DMA((96,)), pltpu.SemaphoreType.DMA((96,)), pltpu.SemaphoreType.DMA((8,))]
+    sems = [pltpu.SemaphoreType.DMA((160,)), pltpu.SemaphoreType.DMA((160,)), pltpu.SemaphoreType.DMA((8,))]
 
     def body(*refs):
         link = Link(*refs[-3:])
@@ -391,15 +391,6 @@
 
 def column_block(ref, index, width=LANES):
     return ref.at[:, pl.ds(pl.multiple_of(index * width, width), width)]
-
-
-def reduced(link, theirs, mine, from_sibling, landing, work, summed, start=0.0, block=10.8):
-    copy = link.send(theirs, from_sibling, "ctx", 0, 0, 1)
-    yield start
-    copy.wait_recv()
-    add_rows(from_sibling, [mine, from_sibling])
-    part = lambda i: column_block(from_sibling, i)
-    yield from scatter_job(link, "ctx", part, landing, work, summed, start + 2.0, block)
 
 
 def spread(link, summed, full, gather, start=0.0, block=10.8):
@@ -557,22 +548,41 @@
     return jnp.where(low_half, pltpu.roll(values, width - 32, 1), pltpu.roll(values, 32, 1))
 
 
-def back_kernel(link, kv_parts, summed, hidden, queries, attended, cosine, sine,
-                full, hidden_rows, query_cols, attended_cols, kv_cols,
-                sib, land_k, work_k, kv_grad, kv_turned):
-    link.greet(whole("shard") + near("ctx") + SIBLING)
+def tail_kernel(link, kv_parts, summed, hidden, queries, attended, cosine, sine, normed, w_query, w_key, w_value,
+                gains, full, attn_full, result, gain_sum,
+                hidden_rows, query_cols, attended_cols, kv_cols, kv_w, left_t, parts, land_a, work_a,
+                theirs, sib, land_b, work_b, attn_summed, sib_k, land_k, work_k, kv_grad, kv_turned,
+                gain_buf, gain_land, gain_work, gain_ctx):
+    link.greet(whole("shard") + whole("ctx") + SIBLING)
     core = lax.rem(lax.axis_index("ctx"), 2)
-
-    def kv_job():
+    leads = lax.rem(lax.axis_index("shard"), 2) == 0
+    count = hidden.shape[0]
+    here = lambda ref, i: ref.at[pl.ds(pl.multiple_of(i * count, count), count)]
+    scatter = scatter_job(link, "shard", lambda i: parts.at[i], land_a, work_a, result, 37.0)
+
+    def make(*offsets):
+        slots = [chip("shard", r, p) for r, p in offsets]
+        pair_of = lambda ref: jnp.concatenate([here(ref, i)[...] for i in slots], axis=0)
+        block = times(pair_of(query_cols), w_query[...]) + times(pair_of(kv_cols), kv_w[...])
+        for k, i in enumerate(slots):
+            parts[i] = block[k * count : k * count + count].astype(LOW)
+        terms = block * pair_of(normed).astype(F32)
+        return jnp.sum(terms, axis=0, keepdims=True)
+
+    def main_job():
         yield 0.0
         copies = [
-            link.send(kv_parts.at[i * 2 + 1 - core], sib.at[i], "ctx", 0, 0, 1) for i in range(8)
+            link.send(kv_parts.at[i * 2 + 1 - core], sib_k.at[i], "ctx", 0, 0, 1) for i in range(8)
         ]
+        for half, mine in enumerate((leads, jnp.logical_not(leads))):
+            for which, weight in enumerate((w_key, w_value)):
+                row = which * 64 + half * 32
+                kv_w[row : row + 32, :] = jnp.where(mine, weight[...], jnp.zeros((32, D), LOW))
         yield 3.0
         for i, copy in enumerate(copies):
             copy.wait_recv()
-            add_rows(sib.at[i], [sib.at[i], kv_parts.at[i * 2 + core]])
-        yield from scatter_job(link, "ctx", lambda i: sib.at[i], land_k, work_k, kv_grad, 4.0, 2.7)
+            add_rows(sib_k.at[i], [sib_k.at[i], kv_parts.at[i * 2 + core]])
+        yield from scatter_job(link, "ctx", lambda i: sib_k.at[i], land_k, work_k, kv_grad, 4.0, 2.7)
         key_lanes = lax.broadcasted_iota(jnp.int32, cosine.shape, 1) < HEAD
         for head in range(KV_HEADS):
             lanes = slice(head * 128, head * 128 + 128)
@@ -580,45 +590,68 @@
             turned = both * cosine[...] - swap_lanes(both) * sine[...]
             kv_turned[:, lanes] = jnp.where(key_lanes, turned, both).astype(LOW)
         part = lambda i: kv_turned.at[:, pl.ds(pl.multiple_of(i // 2 * 128, 128), 128)]
-        yield from exchange_job(link, "shard", part, lambda i: kv_cols.at[i], 26.0, 12.0)
-
-    columns = lambda ref: lambda i: ref.at[:, pl.ds(pl.multiple_of(i * 256, 256), 256)]
-    run(
-        kv_job(),
-        gather_halves(link, "shard", hidden, lambda i: hidden_rows.at[i], None, 0.2),
-        spread(link, summed, full, gather_halves, 5.0),
-        exchange_job(link, "shard", columns(queries), lambda i: query_cols.at[i], 27.0, 20.0),
-        exchange_job(link, "shard", columns(attended), lambda i: attended_cols.at[i], 27.1, 21.0),
-    )
-
-
-def last_kernel(link, parts, theirs, mine, gains, result, full, gain_sum,
-                land_a, work_a, sib, land_b, work_b, summed, gain_land, gain_work, gain_ctx):
-    link.greet(whole("shard") + whole("ctx") + SIBLING)
+        yield from exchange_job(link, "shard", part, lambda i: here(kv_cols, i), 24.0, 10.0)
+        total = make((2, 0), (2, 1))
+        total = total + make((1, 1), (3, 1))
+        next(scatter)
+        later = next(scatter)
+        total = total + make((1, 0), (3, 0))
+        total = total + make((0, 0), (0, 1))
+        for i in range(8):
+            gain_buf[i] = gains[i]
+            gain_buf[i, 0:1, :] = total[:, i * 256 : i * 256 + 256]
+        yield later
+        yield from scatter
 
     def weight_job():
-        yield from reduced(link, theirs, mine, sib, land_b, work_b, summed, 0.0, 3.0)
-        yield from spread(link, summed, full, gather_job, 24.0, 3.0)
+        yield 41.0
+        left_t[0:256, :] = jnp.transpose(query_cols[...].astype(F32)).astype(LOW)
+        left_t[256:384, :] = jnp.transpose(kv_cols[...].astype(F32)).astype(LOW)
+        left_t[384:640, :] = jnp.transpose(attended_cols[...].astype(F32)).astype(LOW)
+
+        def columns(target, half, add):
+            for c in range(4):
+                wide = pl.ds(pl.multiple_of(half * 1024 + c * 256, 256), 256)
+                into = slice(c * 256, c * 256 + 256)
+                for rows, right in ((slice(0, 384), normed), (slice(384, 640), hidden_rows)):
+                    block = times(left_t[rows, :], right[:, wide])
+                    if add:
+                        block = block + target[rows, into].astype(F32)
+                    target[rows, into] = block.astype(LOW)
+
+        columns(theirs, 1 - core, False)
+        copy = link.send(theirs, sib, "ctx", 0, 0, 1)
+        yield 43.5
+        copy.wait_recv()
+        columns(sib, core, True)
+        block = lambda i: column_block(sib, i)
+        yield from scatter_job(link, "ctx", block, land_b, work_b, attn_summed, 46.0, 4.5)
+        yield from spread(link, attn_summed, attn_full, gather_job, 70.0, 4.0)
 
     def gain_job():
-        yield from exchange_job(link, "shard", lambda i: gains.at[i], lambda i: gain_land.at[i], 0.2, 8.0)
+        yield from exchange_job(link, "shard", lambda i: gain_buf.at[i], lambda i: gain_land.at[i], 40.0, 10.0)
         gain_work[0] = sum(gain_land[i] for i in range(8))
         copy = link.send(gain_work.at[0], gain_work.at[1], "ctx", 0, 0, 1)
-        yield 11.0
+        yield 53.0
         copy.wait_recv()
         gain_work[2] = gain_work[0] + gain_work[1]
         copies = [
             link.send(gain_work.at[2], gain_ctx.at[i], "ctx", r, p) for i, (r, p) in enumerate(ALL)
         ]
-        yield 40.0
+        yield 69.0
         for copy in copies:
             copy.wait_recv()
         gain_sum[...] = gain_work[2] + sum(gain_ctx[i] for i in range(7))
 
+    columns_of = lambda ref: lambda i: ref.at[:, pl.ds(pl.multiple_of(i * 256, 256), 256)]
     run(
-        scatter_job(link, "shard", lambda i: parts.at[i], land_a, work_a, result),
+        main_job(),
+        exchange_job(link, "shard", columns_of(queries), lambda i: here(query_cols, i), 0.1, 22.0),
+        gather_halves(link, "shard", hidden, lambda i: here(hidden_rows, i), None, 0.2, 12.0),
+        exchange_job(link, "shard", columns_of(attended), lambda i: here(attended_cols, i), 0.3, 29.0),
+        spread(link, summed, full, gather_halves, 10.0),
+        gain_job(),
         weight_job(),
-        gain_job(),
     )
 
 
@@ -869,7 +902,6 @@
     shard_pair, core = shard % 2, ctx % 2
     places = positions[0]
     own_places = lax.dynamic_slice_in_dim(places, ctx * rows, rows)
-    blocks = lambda m: m.reshape(8, rows, -1)
 
     small = jnp.stack(
         [attn_gain, ffn_gain, jnp.concatenate([own_places // 64, own_places % 64]).astype(LOW)]
@@ -890,7 +922,6 @@
     gain_two = smalls[:, 1].reshape(-1).astype(F32)
     place_rows = (smalls[:, 2, :rows].astype(F32) * 64.0 + smalls[:, 2, rows:].astype(F32)).reshape(-1)
     cosine, sine = wide_tables(place_rows, 2)
-    inputs_rows = token_rows.astype(F32)
     normed_rows, queries, kv_part = first_part(
         shard_pair[None], token_rows, gain_one[None], w_query, w_key, w_value, kv_other, cosine, sine
     )
@@ -936,15 +967,6 @@
         62 * 1024 * 1024,
     )
     down_parts = down_parts.reshape(-1, D)
-    def halves(terms):
-        def one(which):
-            cut = lambda m: lax.dynamic_slice_in_dim(m, which * 1024, 1024, axis=1)
-            return jnp.concatenate(
-                [transposed_times(left, cut(right)).astype(LOW) for left, right in terms], axis=0
-            )
-
-        return one(1 - core), one(core)
-
     down_sum = lax.psum_scatter(down_parts, "shard", scatter_dimension=0, tiled=True)
     outputs = (hidden_state + down_sum.astype(F32)).astype(LOW)
     gain_two_part = jnp.sum(normed_two_grad * hidden_state * inverse_two, axis=0)
@@ -958,79 +980,53 @@
     query_pre_grad, kv_parts = attend_back(
         queries, kv_all, attended, attended_grad, lse, cosine_own, sine_own, order, own_order
     )
-    ffn_full, hidden_rows, query_cols, attended_cols, kv_cols = comm_call(
-        back_kernel,
+    gains = jnp.zeros((8, 8, 256), F32).at[:, 1].set(gain_two_part.reshape(8, 256))
+    ffn_full, attn_full, normed_grad, gain_sum = comm_call(
+        tail_kernel,
         4,
-        [kv_parts, summed, hidden_low, query_pre_grad, attended, cosine_own, sine_own],
-        [INSIDE, INSIDE, ANY, ANY, ANY, INSIDE, INSIDE],
+        [kv_parts, summed, hidden_low, query_pre_grad, attended, cosine_own, sine_own, normed_rows]
+        + [w_query, w_key, w_value, gains],
+        [INSIDE, INSIDE, ANY, ANY, ANY] + [INSIDE] * 7,
+        [shape((3 * ff, D), LOW), shape((640, D), LOW), shape((rows, D), F32), shape((8, 256), F32)],
+        [ANY, ANY, INSIDE, INSIDE],
         [
-            shape((3 * ff, D), LOW),
-            shape((8, rows, D), LOW),
-            shape((8, rows, 256), LOW),
-            shape((8, rows, 256), LOW),
-            shape((8, rows, 128), LOW),
-        ],
-        [ANY] * 5,
-        [
+            vmem(8 * rows, D),
+            vmem(8 * rows, 256),
+            vmem(8 * rows, 256),
+            vmem(8 * rows, 128),
+            vmem(128, D),
+            vmem(640, 8 * rows),
+            vmem(8, rows, D),
+            vmem(7, rows, D),
+            vmem(3, rows, D),
+            vmem(640, 1024),
+            vmem(640, 1024),
+            vmem(7, 640, LANES),
+            vmem(3, 640, LANES),
+            vmem(640, LANES),
             vmem(8, rows, 512),
             vmem(7, rows, 512),
             vmem(3, rows, 512),
             pltpu.VMEM((rows, 512), F32),
-            pltpu.VMEM((rows, 512), LOW),
-        ],
-    )
-    hidden_rows = hidden_rows.reshape(-1, D)
-    gate_wgrad, up_wgrad, down_wgrad = (
-        ffn_full[i * ff : (i + 1) * ff].astype(F32) for i in range(3)
-    )
-    query_cols, attended_cols = query_cols.reshape(-1, 256), attended_cols.reshape(-1, 256)
-    kv_cols = kv_cols.reshape(-1, 128)
-    nothing = jnp.zeros((32, D), LOW)
-    kv_weights = jnp.where(
-        shard_pair == 0,
-        jnp.concatenate([w_key, nothing, w_value, nothing], axis=0),
-        jnp.concatenate([nothing, w_key, nothing, w_value], axis=0),
-    )
-    kv_mine = jnp.where(
-        shard_pair == 0,
-        jnp.concatenate([kv_cols[:, :32], kv_cols[:, 64:96]], axis=1),
-        jnp.concatenate([kv_cols[:, 32:64], kv_cols[:, 96:]], axis=1),
-    )
-    normed_parts = times(query_cols, w_query) + times(kv_cols, kv_weights)
-    gain_one_part = jnp.sum(normed_parts * inputs_rows * inverse_of(inputs_rows), axis=0)
-    theirs, mine = halves(
-        [(query_cols, normed_rows), (kv_mine, normed_rows), (attended_cols, hidden_rows)]
-    )
-    gains = jnp.stack([gain_one_part, gain_two_part]).reshape(2, 8, 256).transpose(1, 0, 2)
-    gains = jnp.concatenate([gains, jnp.zeros((8, 6, 256), F32)], axis=1)
-    normed_grad, attn_full, gain_sum = comm_call(
-        last_kernel,
-        6,
-        [blocks(normed_parts.astype(LOW)), theirs, mine, gains],
-        [INSIDE, ANY, INSIDE, INSIDE],
-        [shape((rows, D), F32), shape((576, D), LOW), shape((8, 256), F32)],
-        [INSIDE, ANY, INSIDE],
-        [
-            vmem(7, rows, D),
-            vmem(3, rows, D),
-            pltpu.VMEM((576, 1024), LOW),
-            vmem(7, 576, LANES),
-            vmem(3, 576, LANES),
-            pltpu.VMEM((576, LANES), LOW),
+            vmem(rows, 512),
+            pltpu.VMEM((8, 8, 256), F32),
             pltpu.VMEM((8, 8, 256), F32),
             pltpu.VMEM((3, 8, 256), F32),
             pltpu.VMEM((7, 8, 256), F32),
         ],
     )
+    gate_wgrad, up_wgrad, down_wgrad = (
+        ffn_full[i * ff : (i + 1) * ff].astype(F32) for i in range(3)
+    )
     inverse_one = inverse_of(inputs)
     input_grad = hidden_grad + rms_backward(inputs, inverse_one, gain_one, normed_grad)
-    query_wgrad, key_wgrad, value_wgrad, out_wgrad = (
-        attn_full[a:b].astype(F32) for a, b in ((0, 256), (256, 288), (288, 320), (320, 576))
-    )
+    attn_rows = lambda start, size: lax.dynamic_slice_in_dim(attn_full, start, size).astype(F32)
+    query_wgrad, out_wgrad = attn_rows(0, 256), attn_rows(384, 256)
+    key_wgrad, value_wgrad = attn_rows(256 + shard_pair * 32, 32), attn_rows(320 + shard_pair * 32, 32)
     return (
         outputs,
         input_grad,
-        gain_sum[0],
+        gain_sum[0] / attn_gain.astype(F32),
         query_wgrad,
         key_wgrad,
         value_wgrad,

time: 487 us -> 463 us (0.951)
  matrix products: 22.6 us -> 12.2 us
  Pallas kernels: 398 us -> 390 us
    pallas_call x5 -> x4, Pallas kernels: 342 us -> 335 us  [comm_call(): pl.pallas_call(body, out_shape=outputs, in_specs=in_specs, out_specs=out_...]
    dot_general x3 -> x1, matrix products: 11.4 us -> 4.96 us  [times(): return jnp.dot(left, right, preferred_element_type=F32)]
  transfers between devices with their start and end apart: 2 -> 2, of which waited for: 0 -> 0; matrix products, arithmetic and copies ran while one was open for 12% -> 10% of each run, Pallas kernels for 50% -> 51%
where the time goes in v5:
time: 463 us; the launch traced here: 457 us
  Pallas kernels  390 us (84%)
  other arithmetic  30.6 us (7%)
  between operations  14.8 us (3%)
  matrix products  12.2 us (3%)
  local copies, waits for them, and re-layouts  9.29 us (2%)
    pallas_call x4, Pallas kernels, comm_call(): pl.pallas_call(body, out_shape=outputs, in_specs=in_specs, out_specs=out_...  335 us
    pallas_call x2, Pallas kernels, attention_call(): pl.pallas_call(kernel, grid_spec=pltpu.PrefetchScalarGridSpec(num_scalar_...  48 us
    convert_element_type x1, other arithmetic, local(): ffn_full[i * ff:(i + 1) * ff].astype(F32)  10.5 us
  transfers between devices with their start and end apart: 2, of which 0 were waited for; matrix products, arithmetic and copies ran while one was open for 10% of the time, Pallas kernels for 51%

profile of v5, /device:TPU:1, one launch (start us, length us, event | category | flops | bytes accessed | tf_op | source)
XLA Modules:
  0.0 457.1 jit_solution(6316697915351486219)
XLA Ops:
  7.2 0.0 all-gather.2.cloned.1.call-start
  7.2 0.7 fusion.9
  7.9 0.7 stack.8
  8.6 0.7 stack.7
  9.2 0.1 pad.11.clone
  9.3 1.6 broadcast_select_fusion.refs_2_
  10.9 0.7 maximum_maximum_fusion.refs_1_
  11.6 55.7 %shard_map.203 = (bf16[8,128,2048]{2,1,0:T(8,128)(2,1)}, bf16[8,16,256]{2,1,0:T(8,128)(2,1)}, bf16[32,2048]{1,0:T(8,128)(2,1)}, bf16[8,256,2048]{2,1,0:T(8,128)(2,1)}) custom-call(bf16[128,2048]{1,0:T(8,128)(2,1)} %refs_0_.1, bf16[16,256]{1,0:T(8,128)(2,1)} %maximum_maximum_fusion.refs_1_, bf16[32,2048]{1,0:T(8,128)(2,1)} %broadcast_select_fusion.refs_2_, ...), custom_call_target="tpu_custom_call" | custom-call | tf_op jit(solution)/shard_map/pallas_call | solution.py:299
  67.3 0.0 all-gather.2.cloned.1.call-update
  67.3 0.0 reduce-scatter.2.cloned.1.call-start
  67.5 0.8 copy.29
  68.3 0.7 convert_add_fusion
  69.1 0.5 fusion.7
  69.7 1.0 copy.25.cosine
  70.8 1.0 copy.26.sine
  71.8 1.4 slice_convert_fusion.5
  73.2 7.5 %shard_map.204 = (bf16[1024,2048]{1,0:T(8,128)(2,1)}, bf16[8,128,256]{2,1,0:T(8,128)(2,1)}, bf16[8,128,128]{2,1,0:T(8,128)(2,1)}) custom-call(s32[1]{0:T(128)} %bitcast.3.pair_ref, bf16[1024,2048]{1,0:T(8,128)(2,1)} %bitcast.50, f32[1,2048]{1,0:T(1,128)} %bitcast.38, bf16[256,2048]{1,0:T(8,128)(2,1)} %refs_8_.1, bf16[32,2048]{1,0:T(8,128)(2,1)} %refs_9_.1, ...), custom_call_target="tpu_custom_call" | custom-call | flops 2147483648 | bytes 10485760 | tf_op jit(solution)/shard_map/pallas_call | solution.py:688
  80.7 35.6 %shard_map.205 = (bf16[8,128,256]{2,1,0:T(8,128)(2,1)}, bf16[16,128,512]{2,1,0:T(8,128)(2,1)}) custom-call(bf16[8,128,256]{2,1,0:T(8,128)(2,1)} %get-tuple-element.49.refs_0_, bf16[8,128,128]{2,1,0:T(8,128)(2,1)} %get-tuple-element.50.refs_1_), custom_call_target="tpu_custom_call" | custom-call | tf_op jit(solution)/shard_map/pallas_call | solution.py:299
  116.3 0.5 and_select_fusion.2.order_ref
  116.8 0.0 copy-start.1
  116.8 23.2 %shard_map.206 = (bf16[128,2048]{1,0:T(8,128)(2,1)}, f32[4,8,512]{2,1,0:T(8,128)}) custom-call(s32[16]{0:T(128)} %and_select_fusion.2.order_ref, s32[1]{0:T(128)S(6)} %select_n.53.own_ref, bf16[8,128,256]{2,1,0:T(8,128)(2,1)} %get-tuple-element.51.q_ref, bf16[16,128,512]{2,1,0:T(8,128)(2,1)} %get-tuple-element.52.kv_ref), custom_call_target="tpu_custom_call" | custom-call | flops 8589934592 | bytes 8388608 | tf_op jit(solution)/shard_map/pallas_call | solution.py:845
  140.0 0.0 copy-done.1
  140.0 5.0 %multiply_reduce_fusion.2 = (f32[128]{0:T(128)S(1)}, f32[128,2048]{1,0:T(8,128)S(1)}) fusion(bf16[128,2048]{1,0:T(8,128)(2,1)} %get-tuple-element.53.out_ref.refs_4_, bf16[2048,2048]{1,0:T(8,128)(2,1)} %bitcast.29, bf16[128,2048]{1,0:T(8,128)(2,1)S(1)} %copy-done.1), kind=kOutput, calls=%fused_computation.22 | convolution fusion | flops 1074790272 | bytes 10486272 | tf_op jit(solution)/shard_map/dot_general | solution.py:26
  145.0 1.0 multiply_convert_fusion.refs_0_
  146.0 103.4 %shard_map.207 = (f32[128,2048]{1,0:T(8,128)}, bf16[8,128,2048]{2,1,0:T(8,128)(2,1)}, bf16[2112,128]{1,0:T(8,128)(2,1)}) custom-call(bf16[128,2048]{1,0:T(8,128)(2,1)} %multiply_convert_fusion.refs_0_, bf16[1024,2048]{1,0:T(8,128)(2,1)} %all-gather.2.cloned.1.call-done.refs_1_, bf16[704,2048]{1,0:T(8,128)(2,1)} %refs_2_.1, bf16[704,2048]{1,0:T(8,128)(2,1)} %refs_3_.3, ...), custom_call_target="tpu_custom_call" | custom-call | tf_op jit(solution)/shard_map/pallas_call | solution.py:299
  249.3 0.0 copy-start
  249.3 0.0 reduce-scatter.2.cloned.1.call-update
  249.4 1.6 constant_dynamic-slice_fusion.1.cos_ref.refs_5_
  250.9 1.5 constant_dynamic-slice_fusion.sin_ref.refs_6_
  252.4 0.0 copy-done
  252.4 0.3 multiply_reduce_fusion
  252.7 0.6 scatter.4.refs_11_
  253.3 1.4 fusion.10.refs_2_
  254.8 0.0 copy-start.2
  254.8 7.3 %convolution_convert_fusion.grad_ref = bf16[128,2048]{1,0:T(8,128)(2,1)} fusion(bf16[128,2048]{1,0:T(8,128)(2,1)S(1)} %fusion.10.refs_2_, bf16[2048,2048]{1,0:T(8,128)(2,1)} %bitcast.30), kind=kOutput, calls=%fused_computation.4 | convolution fusion | flops 1074003968 | bytes 9437184 | tf_op jit(solution)/shard_map/dot_general | solution.py:30
  262.1 0.0 copy-done.2
  262.1 24.8 %shard_map.208 = (bf16[128,2048]{1,0:T(8,128)(2,1)}, bf16[16,128,512]{2,1,0:T(8,128)(2,1)}) custom-call(s32[16]{0:T(128)} %and_select_fusion.2.order_ref, s32[1]{0:T(128)S(6)} %select_n.53.own_ref, bf16[8,128,256]{2,1,0:T(8,128)(2,1)} %get-tuple-element.51.q_ref, bf16[16,128,512]{2,1,0:T(8,128)(2,1)} %get-tuple-element.52.kv_ref, ...), custom_call_target="tpu_custom_call" | custom-call | flops 17179869184 | bytes 8388608 | tf_op jit(solution)/shard_map/pallas_call | solution.py:845
  286.9 0.0 copy-start.4
  286.9 139.8 %shard_map.209 = (bf16[2112,2048]{1,0:T(8,128)(2,1)}, bf16[640,2048]{1,0:T(8,128)(2,1)}, f32[128,2048]{1,0:T(8,128)}, f32[8,256]{1,0:T(8,128)}) custom-call(bf16[16,128,512]{2,1,0:T(8,128)(2,1)} %get-tuple-element.59.refs_0_, bf16[2112,128]{1,0:T(8,128)(2,1)} %get-tuple-element.60.refs_1_, bf16[128,2048]{1,0:T(8,128)(2,1)} %copy-done.2, ...), custom_call_target="tpu_custom_call" | custom-call | tf_op jit(solution)/shard_map/pallas_call | solution.py:299
  426.7 0.0 copy-done.3
  426.8 1.5 fusion
  428.3 1.3 fusion.11
  429.6 0.0 copy-done.4
  429.6 0.6 convert_divide_fusion
  430.2 1.8 dynamic-slice_convert_fusion
  432.0 4.1 slice_convert_fusion.3
  436.1 10.5 %slice_convert_fusion = (f32[704,2048]{1,0:T(8,128)}, f32[704,2048]{1,0:T(8,128)}, f32[704,2048]{1,0:T(8,128)}) fusion(bf16[2112,2048]{1,0:T(8,128)(2,1)} %get-tuple-element.66), kind=kLoop, calls=%fused_computation | loop fusion | flops 4325376 | bytes 25952256 | tf_op jit(solution)/shard_map/convert_element_type | solution.py:1019
  446.5 3.3 fusion.5
  (13 shorter events, 0.2 us)
Async XLA Ops:
  7.2 138.8 %all-gather.2.cloned.1.call-start = ((), (), s32[]{:S(2)}) async-start(), calls=%async_computation.1 | async-start | bytes 4718592 | tf_op jit(solution)/shard_map/all_gather | solution.py:919
  67.3 379.2 %reduce-scatter.2.cloned.1.call-start = ((), (), s32[]{:S(2)}) async-start(), calls=%async_computation.2 | async-start | bytes 4718592 | tf_op jit(solution)/shard_map/reduce_scatter | solution.py:970
  116.8 23.2 %copy-start.1 = (bf16[128,2048]{1,0:T(8,128)(2,1)S(1)}, bf16[128,2048]{1,0:T(8,128)(2,1)}, u32[]{:S(2)}) copy-start(bf16[128,2048]{1,0:T(8,128)(2,1)} %refs_0_.1) | copy-start | bytes 1572868
  249.3 3.1 copy-start
  254.8 7.3 %copy-start.2 = (bf16[128,2048]{1,0:T(8,128)(2,1)}, bf16[128,2048]{1,0:T(8,128)(2,1)S(1)}, u32[]{:S(2)}) copy-start(bf16[128,2048]{1,0:T(8,128)(2,1)S(1)} %fusion.10.refs_2_) | copy-start | bytes 1572868
  286.9 139.8 %copy-start.3 = (f32[8,1,256]{2,1,0:T(1,128)S(1)}, f32[8,1,256]{2,1,0:T(1,128)}, u32[]{:S(2)}) copy-start(f32[8,1,256]{2,1,0:T(1,128)} %get-tuple-element.83) | copy-start | bytes 24580
  286.9 142.7 %copy-start.4 = (bf16[256]{0:T(256)(128)(2,1)S(1)}, bf16[256]{0:T(256)(128)(2,1)}, u32[]{:S(2)}) copy-start(bf16[256]{0:T(256)(128)(2,1)} %param.17) | copy-start | bytes 1540
Sparse Core Ops, SparseCore 0:
  67.5 75.4 all-gather.1
  249.5 103.8 reduce-scatter.1

commit v6 on v5

--- a/solution.py
+++ b/solution.py
@@ -273,6 +273,40 @@
     add_rows(result, [here(0, 0), landing.at[3], landing.at[5], landing.at[6]])
 
 
+def scatter_halves(link, axis, part, landing, work, result, start=0.0, block=10.5):
+    here = lambda ring, pair: part(chip(axis, ring, pair))
+    half = result.shape[0] // 2
+    cut = lambda ref, k: ref.at[pl.ds(k * half, half)]
+    yield start
+    far = link.send(here(2, 1), landing.at[0], axis, 0, 1)
+    pair_up = link.send(here(1, 1), landing.at[1], axis, 1, 0)
+    pair_down = link.send(here(3, 1), landing.at[2], axis, -1, 0)
+    mine_up = [link.send(cut(here(1, 0), 1), cut(landing.at[5], 1), axis, 1, 0)]
+    mine_down = [link.send(cut(here(3, 0), 0), cut(landing.at[6], 0), axis, -1, 0)]
+    yield start + block + 3.5
+    far.wait_recv()
+    add_rows(work.at[0], [here(2, 0), landing.at[0]])
+    half_up = link.send(cut(work.at[0], 0), cut(landing.at[3], 0), axis, 1, 0)
+    half_down = link.send(cut(work.at[0], 1), cut(landing.at[3], 1), axis, -1, 0)
+    yield start + 1.5 * block + 3.0
+    pair_up.wait_recv()
+    pair_down.wait_recv()
+    add_rows(work.at[1], [here(0, 1), landing.at[1], landing.at[2]])
+    across = link.send(work.at[1], landing.at[4], axis, 0, 1)
+    yield start + 2 * block + 5.0
+    half_up.wait_recv()
+    add_rows(cut(work.at[2], 0), [cut(here(1, 0), 0), cut(landing.at[3], 0)])
+    mine_up.append(link.send(cut(work.at[2], 0), cut(landing.at[5], 0), axis, 1, 0))
+    half_down.wait_recv()
+    add_rows(cut(work.at[2], 1), [cut(here(3, 0), 1), cut(landing.at[3], 1)])
+    mine_down.append(link.send(cut(work.at[2], 1), cut(landing.at[6], 1), axis, -1, 0))
+    yield start + 3 * block + 4.0
+    across.wait_recv()
+    for copy in mine_up + mine_down:
+        copy.wait_recv()
+    add_rows(result, [here(0, 0), landing.at[4], landing.at[5], landing.at[6]])
+
+
 def exchange_job(link, axis, part, slot, start=0.0, length=8.0):
     me = chip(axis)
     yield start
@@ -414,9 +448,9 @@
     return lax.dot_general(left, right, (((0,), (0,)), ((), ())), preferred_element_type=F32)
 
 
-def ffn_kernel(link, own, og, w_gate, w_up, w_down, result, down_parts, summed,
+def ffn_kernel(link, own, og, w_gate, w_up, w_down, attended, result, down_parts, summed, attended_cols,
                rows_all, gate_t, up_t, inner_t, parts, land_a, work_a, theirs, sib, land_b, work_b):
-    link.greet(near("shard") + near("ctx") + SIBLING)
+    link.greet(whole("shard") + near("ctx") + SIBLING)
     core = lax.rem(lax.axis_index("ctx"), 2)
     count = own.shape[0]
     ff = w_gate.shape[0]
@@ -539,6 +573,9 @@
     run(
         scatter_job(link, "shard", lambda i: parts.at[i], land_a, work_a, result),
         weight_job(),
+        exchange_job(
+            link, "shard", lambda i: column_block(attended, i, 256), lambda i: here(attended_cols, i), 42.0, 14.0
+        ),
     )
 
 
@@ -548,9 +585,9 @@
     return jnp.where(low_half, pltpu.roll(values, width - 32, 1), pltpu.roll(values, 32, 1))
 
 
-def tail_kernel(link, kv_parts, summed, hidden, queries, attended, cosine, sine, normed, w_query, w_key, w_value,
+def tail_kernel(link, kv_parts, summed, hidden, queries, attended_cols, cosine, sine, normed, w_query, w_key, w_value,
                 gains, full, attn_full, result, gain_sum,
-                hidden_rows, query_cols, attended_cols, kv_cols, kv_w, left_t, parts, land_a, work_a,
+                hidden_rows, query_cols, kv_cols, kv_w, left_t, parts, land_a, work_a,
                 theirs, sib, land_b, work_b, attn_summed, sib_k, land_k, work_k, kv_grad, kv_turned,
                 gain_buf, gain_land, gain_work, gain_ctx):
     link.greet(whole("shard") + whole("ctx") + SIBLING)
@@ -558,7 +595,7 @@
     leads = lax.rem(lax.axis_index("shard"), 2) == 0
     count = hidden.shape[0]
     here = lambda ref, i: ref.at[pl.ds(pl.multiple_of(i * count, count), count)]
-    scatter = scatter_job(link, "shard", lambda i: parts.at[i], land_a, work_a, result, 37.0)
+    scatter = scatter_halves(link, "shard", lambda i: parts.at[i], land_a, work_a, result, 37.0)
 
     def make(*offsets):
         slots = [chip("shard", r, p) for r, p in offsets]
@@ -583,19 +620,21 @@
             copy.wait_recv()
             add_rows(sib_k.at[i], [sib_k.at[i], kv_parts.at[i * 2 + core]])
         yield from scatter_job(link, "ctx", lambda i: sib_k.at[i], land_k, work_k, kv_grad, 4.0, 2.7)
-        key_lanes = lax.broadcasted_iota(jnp.int32, cosine.shape, 1) < HEAD
+        me = chip("shard")
+        own_cosine, own_sine = here(cosine, me)[...], here(sine, me)[...]
+        key_lanes = lax.broadcasted_iota(jnp.int32, own_cosine.shape, 1) < HEAD
         for head in range(KV_HEADS):
             lanes = slice(head * 128, head * 128 + 128)
             both = kv_grad[:, lanes]
-            turned = both * cosine[...] - swap_lanes(both) * sine[...]
+            turned = both * own_cosine - swap_lanes(both) * own_sine
             kv_turned[:, lanes] = jnp.where(key_lanes, turned, both).astype(LOW)
         part = lambda i: kv_turned.at[:, pl.ds(pl.multiple_of(i // 2 * 128, 128), 128)]
         yield from exchange_job(link, "shard", part, lambda i: here(kv_cols, i), 24.0, 10.0)
-        total = make((2, 0), (2, 1))
-        total = total + make((1, 1), (3, 1))
+        total = make((2, 1), (1, 1))
+        total = total + make((3, 1), (3, 0))
+        total = total + make((1, 0), (2, 0))
         next(scatter)
         later = next(scatter)
-        total = total + make((1, 0), (3, 0))
         total = total + make((0, 0), (0, 1))
         for i in range(8):
             gain_buf[i] = gains[i]
@@ -648,7 +687,6 @@
         main_job(),
         exchange_job(link, "shard", columns_of(queries), lambda i: here(query_cols, i), 0.1, 22.0),
         gather_halves(link, "shard", hidden, lambda i: here(hidden_rows, i), None, 0.2, 12.0),
-        exchange_job(link, "shard", columns_of(attended), lambda i: here(attended_cols, i), 0.3, 29.0),
         spread(link, summed, full, gather_halves, 10.0),
         gain_job(),
         weight_job(),
@@ -700,8 +738,10 @@
     )(pair, token_rows, gain, w_query, w_key, w_value, kv_other, cosine, sine)
 
 
-BLOCK = 256
+BLOCK = 512
 LOG2E = 1.4426950408889634
+GROUPS = 1
+COLUMNS = 512 // GROUPS
 
 
 def sort_keys(order_ref, kv_ref, sorted_ref, flipped_ref):
@@ -710,7 +750,7 @@
         trail = pl.multiple_of((31 - order_ref[c]) * 64, 64)
         sorted_ref[pl.ds(lead, 64), :] = kv_ref[c, 0:64, :]
         sorted_ref[pl.ds(trail, 64), :] = kv_ref[c, 64:128, :]
-    for i in range(8):
+    for i in range(2048 // BLOCK):
         rows = slice(i * BLOCK, (i + 1) * BLOCK)
         flipped_ref[i] = jnp.transpose(sorted_ref[rows, :].astype(F32)).astype(LOW)
 
@@ -746,8 +786,8 @@
 
 
 def above(block, first_place):
-    key = lax.broadcasted_iota(jnp.int32, (BLOCK, 512), 0) + block * BLOCK
-    query = lax.broadcasted_iota(jnp.int32, (BLOCK, 512), 1) % 64 + first_place
+    key = lax.broadcasted_iota(jnp.int32, (BLOCK, COLUMNS), 0) + block * BLOCK
+    query = lax.broadcasted_iota(jnp.int32, (BLOCK, COLUMNS), 1) % 64 + first_place
     return key > query
 
 
@@ -755,37 +795,59 @@
     return lax.dot_general(left, right, (((1,), (1,)), ((), ())), preferred_element_type=F32)
 
 
-def attend_kernel(order_ref, own_ref, q_ref, kv_ref, out_ref, lse_ref, sorted_ref, flipped_ref):
+def column_groups(values, axis):
+    pieces = [slice(i * COLUMNS, (i + 1) * COLUMNS) for i in range(GROUPS)]
+    return [values[p] if axis == 0 else values[:, p] for p in pieces]
+
+
+def attend_kernel(order_ref, own_ref, q_ref, kv_ref, w_ref, x_ref, gain_ref, out_ref, lse_ref, hidden_ref, normed_ref,
+                  sorted_ref, flipped_ref):
     sort_keys(order_ref, kv_ref, sorted_ref, flipped_ref)
     factor = HEAD**-0.5 * LOG2E
     for run in range(2):
         first_place = jnp.where(run == 0, own_ref[0], 31 - own_ref[0]) * 64
         last = first_place // BLOCK
-        q = spread_heads(query_blocks(q_ref, run), False).astype(LOW)
+        q = column_groups(spread_heads(query_blocks(q_ref, run), False).astype(LOW), 0)
 
         def step(block, carry, masked):
-            largest, total, mixed = carry
             rows = pl.ds(pl.multiple_of(block * BLOCK, BLOCK), BLOCK)
-            scores = dot_kt(sorted_ref[rows, :], q) * factor
-            if masked:
-                scores = jnp.where(above(block, first_place), NEG, scores)
-            top = jnp.maximum(largest, jnp.max(scores, axis=0, keepdims=True))
-            fade = jnp.exp2(largest - top)
-            exps = jnp.exp2(scores - top)
-            total = total * fade + jnp.sum(exps, axis=0, keepdims=True)
-            mixed = mixed * fade + times(flipped_ref[block, 64:128, :], exps.astype(LOW))
-            return top, total, mixed
-
-        carry = (jnp.full((1, 512), NEG, F32), jnp.zeros((1, 512), F32), jnp.zeros((64, 512), F32))
+            keys, values = sorted_ref[rows, :], flipped_ref[block, 64:128, :]
+            after = []
+            for queries, (largest, total, mixed) in zip(q, carry):
+                scores = dot_kt(keys, queries) * factor
+                if masked:
+                    scores = jnp.where(above(block, first_place), NEG, scores)
+                top = jnp.maximum(largest, jnp.max(scores, axis=0, keepdims=True))
+                fade = jnp.exp2(largest - top)
+                exps = jnp.exp2(scores - top)
+                total = total * fade + jnp.sum(exps, axis=0, keepdims=True)
+                mixed = mixed * fade + times(values, exps.astype(LOW))
+                after.append((top, total, mixed))
+            return tuple(after)
+
+        nothing = lambda rows, fill: jnp.full((rows, COLUMNS), fill, F32)
+        carry = tuple((nothing(1, NEG), nothing(1, 0.0), nothing(64, 0.0)) for _ in range(GROUPS))
         carry = lax.fori_loop(0, last, functools.partial(step, masked=False), carry)
-        largest, total, mixed = step(last, carry, True)
-        for i, block in enumerate(join_heads(mixed / total)):
+        carry = step(last, carry, True)
+        mixed = jnp.concatenate([m / t for _, t, m in carry], axis=1)
+        for i, block in enumerate(join_heads(mixed)):
             out_ref[run * 64 : run * 64 + 64, i * 128 : i * 128 + 128] = block.astype(LOW)
-        lse_ref[0, run : run + 1, :] = largest + jnp.log2(total)
-
-
-def attend_back_kernel(order_ref, own_ref, q_ref, kv_ref, out_ref, grad_ref, lse_ref, cos_ref, sin_ref,
-                       dq_ref, dkv_ref, sorted_ref, flipped_ref, total_ref):
+        lse_ref[0, run : run + 1, :] = jnp.concatenate([l + jnp.log2(t) for l, t, _ in carry], axis=1)
+
+    @pl.when(pl.program_id(0) == 0)
+    def _():
+        hidden_ref[...] = x_ref[...].astype(F32)
+
+    hidden_ref[...] += times(out_ref[...], w_ref[...])
+
+    @pl.when(pl.program_id(0) == KV_HEADS - 1)
+    def _():
+        normed_ref[...] = rms_forward(hidden_ref[...], gain_ref[...])[0].astype(LOW)
+
+
+def attend_back_kernel(order_ref, own_ref, q_ref, kv_ref, out_ref, hidden_ref, w_ref, lse_ref, cos_ref, sin_ref,
+                       dq_ref, dkv_ref, sorted_ref, flipped_ref, total_ref, grad_ref):
+    grad_ref[...] = times_transposed(hidden_ref[...], w_ref[...]).astype(LOW)
     sort_keys(order_ref, kv_ref, sorted_ref, flipped_ref)
     total_ref[...] = jnp.zeros_like(total_ref)
     scale = HEAD**-0.5
@@ -793,10 +855,10 @@
     for run in range(2):
         first_place = jnp.where(run == 0, own_ref[0], 31 - own_ref[0]) * 64
         last = first_place // BLOCK
-        q = spread_heads(query_blocks(q_ref, run), False).astype(LOW)
+        q = column_groups(spread_heads(query_blocks(q_ref, run), False).astype(LOW), 0)
         grad_wide = spread_heads(row_blocks(grad_ref, run), True)
         out_wide = spread_heads(row_blocks(out_ref, run), True)
-        grad = grad_wide.astype(LOW)
+        grad = column_groups(grad_wide.astype(LOW), 0)
         inner = lax.dot_general(
             jnp.ones((8, 128), F32),
             grad_wide * out_wide,
@@ -804,20 +866,26 @@
             precision=lax.Precision.HIGHEST,
             preferred_element_type=F32,
         )[:1]
-        lse = lse_ref[0, run : run + 1, :]
+        inner = column_groups(inner, 1)
+        lse = column_groups(lse_ref[0, run : run + 1, :], 1)
 
         def step(block, dq, masked):
             rows = pl.ds(pl.multiple_of(block * BLOCK, BLOCK), BLOCK)
-            kv = sorted_ref[rows, :]
-            probs = jnp.exp2(dot_kt(kv, q) * factor - lse)
-            if masked:
-                probs = jnp.where(above(block, first_place), 0.0, probs)
-            score_grad = (probs * (dot_kt(kv, grad) - inner)).astype(LOW)
-            total_ref[rows, :] += times(score_grad, q) + times(probs.astype(LOW), grad)
-            return dq + times(flipped_ref[block, 0:64, :], score_grad)
-
-        dq = lax.fori_loop(0, last, functools.partial(step, masked=False), jnp.zeros((64, 512), F32))
-        dq = step(last, dq, True)
+            kv, keys = sorted_ref[rows, :], flipped_ref[block, 0:64, :]
+            after, total = [], total_ref[rows, :]
+            for i in range(GROUPS):
+                probs = jnp.exp2(dot_kt(kv, q[i]) * factor - lse[i])
+                if masked:
+                    probs = jnp.where(above(block, first_place), 0.0, probs)
+                score_grad = (probs * (dot_kt(kv, grad[i]) - inner[i])).astype(LOW)
+                total = total + times(score_grad, q[i]) + times(probs.astype(LOW), grad[i])
+                after.append(dq[i] + times(keys, score_grad))
+            total_ref[rows, :] = total
+            return tuple(after)
+
+        dq = tuple(jnp.zeros((64, COLUMNS), F32) for _ in range(GROUPS))
+        dq = lax.fori_loop(0, last, functools.partial(step, masked=False), dq)
+        dq = jnp.concatenate(step(last, dq, True), axis=1)
         cosine, sine = cos_ref[run * 64 : run * 64 + 64, :], sin_ref[run * 64 : run * 64 + 64, :]
         low_half = lax.broadcasted_iota(jnp.int32, (64, 128), 1) % 64 < 32
         for i, block in enumerate(join_heads(dq * scale)):
@@ -839,9 +907,12 @@
         "kv": pl.BlockSpec((16, 128, 128), lambda g, *_: (0, 0, g)),
         "rows": pl.BlockSpec((128, 512), lambda g, *_: (0, g)),
         "lse": pl.BlockSpec((1, 8, 512), lambda g, *_: (g, 0, 0)),
-        "table": pl.BlockSpec((128, 128), lambda g, *_: (0, 0)),
+        "table": pl.BlockSpec((128, 128), lambda g, order, own: (own[1], 0)),
+        "weight": pl.BlockSpec((512, D), lambda g, *_: (g, 0)),
+        "held": pl.BlockSpec((128, D), lambda g, *_: (0, 0)),
+        "gain": pl.BlockSpec((1, D), lambda g, *_: (0, 0)),
     }
-    keys = [pltpu.VMEM((2048, 128), LOW), pltpu.VMEM((8, 128, BLOCK), LOW)]
+    keys = [pltpu.VMEM((2048, 128), LOW), pltpu.VMEM((2048 // BLOCK, 128, BLOCK), LOW)]
     return pl.pallas_call(
         kernel,
         grid_spec=pltpu.PrefetchScalarGridSpec(
@@ -857,28 +928,29 @@
     )(*scalars, *inputs)
 
 
-def attend(queries, kv_all, order, own):
+def attend(queries, kv_all, w_out, tokens, gain, order, own):
+    whole_rows = lambda kind: jax.ShapeDtypeStruct((128, D), kind)
     return attention_call(
         attend_kernel,
         (order, own),
-        (queries, kv_all),
-        ("q", "kv"),
-        [jax.ShapeDtypeStruct((128, D), LOW), jax.ShapeDtypeStruct((4, 8, 512), F32)],
-        ("rows", "lse"),
+        (queries, kv_all, w_out, tokens, gain),
+        ("q", "kv", "weight", "held", "gain"),
+        [whole_rows(LOW), jax.ShapeDtypeStruct((4, 8, 512), F32), whole_rows(F32), whole_rows(LOW)],
+        ("rows", "lse", "held", "held"),
         [],
         1 << 33,
     )
 
 
-def attend_back(queries, kv_all, attended, attended_grad, lse, cosine, sine, order, own):
+def attend_back(queries, kv_all, attended, hidden_low, w_out, lse, cosine, sine, order, own):
     return attention_call(
         attend_back_kernel,
         (order, own),
-        (queries, kv_all, attended, attended_grad, lse, cosine, sine),
-        ("q", "kv", "rows", "rows", "lse", "table", "table"),
+        (queries, kv_all, attended, hidden_low, w_out, lse, cosine, sine),
+        ("q", "kv", "rows", "held", "weight", "lse", "table", "table"),
         [jax.ShapeDtypeStruct((128, D), LOW), jax.ShapeDtypeStruct((16, 128, 512), LOW)],
         ("rows", "kv"),
-        [pltpu.VMEM((2048, 128), F32)],
+        [pltpu.VMEM((2048, 128), F32), pltpu.VMEM((128, 512), LOW)],
         1 << 34,
     )
 
@@ -936,21 +1008,19 @@
     )
 
     order = places.reshape(16, rows)[:, 0] // 64
-    own_order = own_places[:1] // 64
-    attended, lse = attend(queries, kv_all, order, own_order)
-
-    inputs = tokens.astype(F32)
-    hidden_state = inputs + times(attended, out_full)
-    normed_two, inverse_two = rms_forward(hidden_state, gain_two)
+    own_order = jnp.stack([own_places[0] // 64, shard])
+    attended, lse, hidden_state, normed_two = attend(
+        queries, kv_all, out_full, tokens, gain_two[None], order, own_order
+    )
     ff = w_gate.shape[0]
     vmem = lambda count, *dims: pltpu.VMEM((count, *dims), LOW)
-    normed_two_grad, down_parts, summed = comm_call(
+    normed_two_grad, down_parts, summed, attended_cols = comm_call(
         ffn_kernel,
         3,
-        [normed_two.astype(LOW), out_grad_rows, w_gate, w_up, w_down],
-        [ANY] + [INSIDE] * 4,
-        [shape((rows, D), F32), shape((8, rows, D), LOW), shape((3 * ff, LANES), LOW)],
-        [INSIDE] * 3,
+        [normed_two, out_grad_rows, w_gate, w_up, w_down, attended],
+        [ANY] + [INSIDE] * 4 + [ANY],
+        [shape((rows, D), F32), shape((8, rows, D), LOW), shape((3 * ff, LANES), LOW), shape((8 * rows, 256), LOW)],
+        [INSIDE] * 3 + [ANY],
         [
             vmem(8 * rows, D),
             vmem(ff, 8 * rows),
@@ -969,29 +1039,27 @@
     down_parts = down_parts.reshape(-1, D)
     down_sum = lax.psum_scatter(down_parts, "shard", scatter_dimension=0, tiled=True)
     outputs = (hidden_state + down_sum.astype(F32)).astype(LOW)
+    inverse_two = inverse_of(hidden_state)
     gain_two_part = jnp.sum(normed_two_grad * hidden_state * inverse_two, axis=0)
     hidden_grad = out_grad.astype(F32) + rms_backward(
         hidden_state, inverse_two, gain_two, normed_two_grad
     )
     hidden_low = hidden_grad.astype(LOW)
-    attended_grad = times_transposed(hidden_low, out_full).astype(LOW)
-    own_table = lambda table: lax.dynamic_slice_in_dim(table, shard * rows, rows)
-    cosine_own, sine_own = own_table(cosine), own_table(sine)
     query_pre_grad, kv_parts = attend_back(
-        queries, kv_all, attended, attended_grad, lse, cosine_own, sine_own, order, own_order
-    )
+        queries, kv_all, attended, hidden_low, out_full, lse, cosine, sine, order, own_order
+    )
+    inputs = tokens.astype(F32)
     gains = jnp.zeros((8, 8, 256), F32).at[:, 1].set(gain_two_part.reshape(8, 256))
     ffn_full, attn_full, normed_grad, gain_sum = comm_call(
         tail_kernel,
         4,
-        [kv_parts, summed, hidden_low, query_pre_grad, attended, cosine_own, sine_own, normed_rows]
+        [kv_parts, summed, hidden_low, query_pre_grad, attended_cols, cosine, sine, normed_rows]
         + [w_query, w_key, w_value, gains],
-        [INSIDE, INSIDE, ANY, ANY, ANY] + [INSIDE] * 7,
+        [INSIDE, INSIDE, ANY, ANY] + [INSIDE] * 8,
         [shape((3 * ff, D), LOW), shape((640, D), LOW), shape((rows, D), F32), shape((8, 256), F32)],
         [ANY, ANY, INSIDE, INSIDE],
         [
             vmem(8 * rows, D),
-            vmem(8 * rows, 256),
             vmem(8 * rows, 256),
             vmem(8 * rows, 128),
             vmem(128, D),

time: 463 us -> 459 us (level)
  matrix products: 12.2 us -> 0 us
  Pallas kernels: 390 us -> 397 us
    dot_general x2 -> x0, matrix products: 12.2 us -> none  [the longest x1 7.28 us: times_transposed(): lax.dot_general(left, right, (((1,), (1,)), ((), ())), preferred_element_...]
    pallas_call x2, Pallas kernels: 48 us -> 53.4 us  [attention_call(): pl.pallas_call(kernel, grid_spec=pltpu.PrefetchScalarGridSpec(num_scalar_...]
  transfers between devices with their start and end apart: 2 -> 2, of which waited for: 0 -> 1; matrix products, arithmetic and copies ran while one was open for 10% -> 6% of each run, Pallas kernels for 51% -> 50%
where the time goes in v6:
time: 459 us; the launch traced here: 452 us
  Pallas kernels  397 us (86%)
  other arithmetic  30.1 us (7%)
  between operations  14.8 us (3%)
  local copies, waits for them, and re-layouts  7.57 us (2%)
    pallas_call x4, Pallas kernels, comm_call(): pl.pallas_call(body, out_shape=outputs, in_specs=in_specs, out_specs=out_...  336 us
    pallas_call x2, Pallas kernels, attention_call(): pl.pallas_call(kernel, grid_spec=pltpu.PrefetchScalarGridSpec(num_scalar_...  53.4 us
    convert_element_type x1, other arithmetic, local(): ffn_full[i * ff:(i + 1) * ff].astype(F32)  10.5 us
  transfers between devices with their start and end apart: 2, of which 1 were waited for; matrix products, arithmetic and copies ran while one was open for 6% of the time, Pallas kernels for 50%

profile of v6, /device:TPU:1, one launch (start us, length us, event | category | flops | bytes accessed | tf_op | source)
XLA Modules:
  0.0 452.5 jit_solution(14163552194103650621)
XLA Ops:
  7.2 0.0 all-gather.2.cloned.1.call-start
  7.2 0.7 fusion.9
  7.9 0.7 stack.20
  8.6 0.7 stack.19
  9.2 0.1 pad.11.clone
  9.3 1.6 broadcast_select_fusion.refs_2_
  10.9 0.7 maximum_maximum_fusion.refs_1_
  11.6 55.7 %shard_map.203 = (bf16[8,128,2048]{2,1,0:T(8,128)(2,1)}, bf16[8,16,256]{2,1,0:T(8,128)(2,1)}, bf16[32,2048]{1,0:T(8,128)(2,1)}, bf16[8,256,2048]{2,1,0:T(8,128)(2,1)}) custom-call(bf16[128,2048]{1,0:T(8,128)(2,1)} %x_ref.1, bf16[16,256]{1,0:T(8,128)(2,1)} %maximum_maximum_fusion.refs_1_, bf16[32,2048]{1,0:T(8,128)(2,1)} %broadcast_select_fusion.refs_2_, ...), custom_call_target="tpu_custom_call" | custom-call | tf_op jit(solution)/shard_map/pallas_call | solution.py:333
  67.3 0.0 all-gather.2.cloned.1.call-update
  67.3 0.0 reduce-scatter.2.cloned.1.call-start
  67.5 0.8 copy.31
  68.3 0.7 convert_add_fusion
  69.1 0.5 fusion.7
  69.7 1.0 copy.25.cosine.cos_ref.refs_5_
  70.8 1.0 copy.26.sine.sin_ref.refs_6_
  71.8 1.4 slice_convert_fusion.5
  73.2 7.5 %shard_map.204 = (bf16[1024,2048]{1,0:T(8,128)(2,1)}, bf16[8,128,256]{2,1,0:T(8,128)(2,1)}, bf16[8,128,128]{2,1,0:T(8,128)(2,1)}) custom-call(s32[1]{0:T(128)} %bitcast.5.pair_ref, bf16[1024,2048]{1,0:T(8,128)(2,1)} %bitcast.49, f32[1,2048]{1,0:T(1,128)} %bitcast.35, bf16[256,2048]{1,0:T(8,128)(2,1)} %refs_8_.1, bf16[32,2048]{1,0:T(8,128)(2,1)} %refs_9_.1, ...), custom_call_target="tpu_custom_call" | custom-call | flops 2147483648 | bytes 10485760 | tf_op jit(solution)/shard_map/pallas_call | solution.py:726
  80.7 35.5 %shard_map.205 = (bf16[8,128,256]{2,1,0:T(8,128)(2,1)}, bf16[16,128,512]{2,1,0:T(8,128)(2,1)}) custom-call(bf16[8,128,256]{2,1,0:T(8,128)(2,1)} %get-tuple-element.52.refs_0_, bf16[8,128,128]{2,1,0:T(8,128)(2,1)} %get-tuple-element.53.refs_1_), custom_call_target="tpu_custom_call" | custom-call | tf_op jit(solution)/shard_map/pallas_call | solution.py:333
  116.3 0.7 pad_add_fusion.own_ref
  116.9 0.5 and_select_fusion.2.order_ref
  117.4 22.1 %shard_map.206 = (bf16[128,2048]{1,0:T(8,128)(2,1)}, f32[4,8,512]{2,1,0:T(8,128)}, f32[128,2048]{1,0:T(8,128)}, bf16[128,2048]{1,0:T(8,128)(2,1)}) custom-call(s32[16]{0:T(128)} %and_select_fusion.2.order_ref, s32[2]{0:T(128)} %pad_add_fusion.own_ref, bf16[8,128,256]{2,1,0:T(8,128)(2,1)} %get-tuple-element.54.q_ref, ...), custom_call_target="tpu_custom_call" | custom-call | flops 8589934592 | bytes 8388608 | tf_op jit(solution)/shard_map/pallas_call | solution.py:916
  139.6 3.3 all-gather.2.cloned.1.call-done.refs_1_
  142.9 112.9 %shard_map.207 = (f32[128,2048]{1,0:T(8,128)}, bf16[8,128,2048]{2,1,0:T(8,128)(2,1)}, bf16[2112,128]{1,0:T(8,128)(2,1)}, bf16[1024,256]{1,0:T(8,128)(2,1)}) custom-call(bf16[128,2048]{1,0:T(8,128)(2,1)} %get-tuple-element.58.refs_0_, bf16[1024,2048]{1,0:T(8,128)(2,1)} %all-gather.2.cloned.1.call-done.refs_1_, bf16[704,2048]{1,0:T(8,128)(2,1)} %refs_2_.1, ...), custom_call_target="tpu_custom_call" | custom-call | tf_op jit(solution)/shard_map/pallas_call | solution.py:333
  255.8 0.0 copy-start
  255.8 0.0 copy-start.1
  255.8 0.0 copy-start.4
  255.8 0.0 copy-start.3
  255.8 0.0 reduce-scatter.2.cloned.1.call-update
  255.8 1.2 copy-done
  257.0 0.2 multiply_reduce_fusion.2
  257.2 0.2 copy-done.1
  257.3 0.0 copy-done.4
  257.3 0.3 multiply_reduce_fusion
  257.6 0.6 scatter.4.refs_11_
  258.3 1.2 fusion.10.hidden_ref.refs_2_
  259.4 31.2 %shard_map.208 = (bf16[128,2048]{1,0:T(8,128)(2,1)}, bf16[16,128,512]{2,1,0:T(8,128)(2,1)}) custom-call(s32[16]{0:T(128)} %and_select_fusion.2.order_ref, s32[2]{0:T(128)} %pad_add_fusion.own_ref, bf16[8,128,256]{2,1,0:T(8,128)(2,1)} %get-tuple-element.54.q_ref, bf16[16,128,512]{2,1,0:T(8,128)(2,1)} %get-tuple-element.55.kv_ref, ...), custom_call_target="tpu_custom_call" | custom-call | flops 17179869184 | bytes 8388608 | tf_op jit(solution)/shard_map/pallas_call | solution.py:916
  290.7 0.0 copy-start.6
  290.7 131.5 %shard_map.209 = (bf16[2112,2048]{1,0:T(8,128)(2,1)}, bf16[640,2048]{1,0:T(8,128)(2,1)}, f32[128,2048]{1,0:T(8,128)}, f32[8,256]{1,0:T(8,128)}) custom-call(bf16[16,128,512]{2,1,0:T(8,128)(2,1)} %get-tuple-element.64.refs_0_, bf16[2112,128]{1,0:T(8,128)(2,1)} %get-tuple-element.65.refs_1_, bf16[128,2048]{1,0:T(8,128)(2,1)} %fusion.10.hidden_ref.refs_2_, ...), custom_call_target="tpu_custom_call" | custom-call | tf_op jit(solution)/shard_map/pallas_call | solution.py:333
  422.2 0.0 copy-done.2
  422.2 0.0 copy-done.5
  422.3 1.5 fusion
  423.8 1.3 fusion.11
  425.1 0.0 copy-done.6
  425.1 0.6 convert_divide_fusion
  425.7 1.8 dynamic-slice_convert_fusion
  427.5 4.1 slice_convert_fusion.3
  431.6 10.5 %slice_convert_fusion = (f32[704,2048]{1,0:T(8,128)}, f32[704,2048]{1,0:T(8,128)}, f32[704,2048]{1,0:T(8,128)}) fusion(bf16[2112,2048]{1,0:T(8,128)(2,1)} %get-tuple-element.72), kind=kLoop, calls=%fused_computation | loop fusion | flops 4325376 | bytes 25952256 | tf_op jit(solution)/shard_map/convert_element_type | solution.py:1087
  442.1 3.1 fusion.5
  (14 shorter events, 0.2 us)
Async XLA Ops:
  7.2 135.7 %all-gather.2.cloned.1.call-start = ((), (), s32[]{:S(2)}) async-start(), calls=%async_computation.1 | async-start | bytes 4718592 | tf_op jit(solution)/shard_map/all_gather | solution.py:991
  67.3 374.7 %reduce-scatter.2.cloned.1.call-start = ((), (), s32[]{:S(2)}) async-start(), calls=%async_computation.2 | async-start | bytes 4718592 | tf_op jit(solution)/shard_map/reduce_scatter | solution.py:1040
  255.8 1.2 copy-start
  255.8 1.5 copy-start.1
  255.8 1.5 copy-start.4
  255.8 2.4 copy-start.3
  290.7 131.6 %copy-start.2 = (bf16[128,2048]{1,0:T(8,128)(2,1)S(1)}, bf16[128,2048]{1,0:T(8,128)(2,1)}, u32[]{:S(2)}) copy-start(bf16[128,2048]{1,0:T(8,128)(2,1)} %x_ref.1) | copy-start | bytes 1572868
  290.7 131.6 %copy-start.5 = (f32[8,1,256]{2,1,0:T(1,128)S(1)}, f32[8,1,256]{2,1,0:T(1,128)}, u32[]{:S(2)}) copy-start(f32[8,1,256]{2,1,0:T(1,128)} %get-tuple-element.89) | copy-start | bytes 24580
  290.7 134.5 %copy-start.6 = (bf16[256]{0:T(256)(128)(2,1)S(1)}, bf16[256]{0:T(256)(128)(2,1)}, u32[]{:S(2)}) copy-start(bf16[256]{0:T(256)(128)(2,1)} %param.17) | copy-start | bytes 1540
Sparse Core Ops, SparseCore 0:
  67.5 75.3 all-gather.1
  256.0 108.2 reduce-scatter.1

commit v7 on v6

--- a/solution.py
+++ b/solution.py
@@ -643,7 +643,7 @@
         yield from scatter
 
     def weight_job():
-        yield 41.0
+        yield 46.0
         left_t[0:256, :] = jnp.transpose(query_cols[...].astype(F32)).astype(LOW)
         left_t[256:384, :] = jnp.transpose(kv_cols[...].astype(F32)).astype(LOW)
         left_t[384:640, :] = jnp.transpose(attended_cols[...].astype(F32)).astype(LOW)
@@ -660,12 +660,12 @@
 
         columns(theirs, 1 - core, False)
         copy = link.send(theirs, sib, "ctx", 0, 0, 1)
-        yield 43.5
+        yield 48.5
         copy.wait_recv()
         columns(sib, core, True)
         block = lambda i: column_block(sib, i)
-        yield from scatter_job(link, "ctx", block, land_b, work_b, attn_summed, 46.0, 4.5)
-        yield from spread(link, attn_summed, attn_full, gather_job, 70.0, 4.0)
+        yield from scatter_job(link, "ctx", block, land_b, work_b, attn_summed, 51.0, 4.5)
+        yield from spread(link, attn_summed, attn_full, gather_job, 75.0, 4.0)
 
     def gain_job():
         yield from exchange_job(link, "shard", lambda i: gain_buf.at[i], lambda i: gain_land.at[i], 40.0, 10.0)
@@ -686,7 +686,7 @@
     run(
         main_job(),
         exchange_job(link, "shard", columns_of(queries), lambda i: here(query_cols, i), 0.1, 22.0),
-        gather_halves(link, "shard", hidden, lambda i: here(hidden_rows, i), None, 0.2, 12.0),
+        gather_halves(link, "shard", hidden, lambda i: here(hidden_rows, i), None, 0.2, 14.5),
         spread(link, summed, full, gather_halves, 10.0),
         gain_job(),
         weight_job(),

time: 459 us -> 459 us (level)
  no operation moved by 1% of the time
where the time goes in v7:
time: 459 us; the launch traced here: 452 us
  Pallas kernels  397 us (86%)
  other arithmetic  30.1 us (7%)
  between operations  14.8 us (3%)
  local copies, waits for them, and re-layouts  7.57 us (2%)
    pallas_call x4, Pallas kernels, comm_call(): pl.pallas_call(body, out_shape=outputs, in_specs=in_specs, out_specs=out_...  336 us
    pallas_call x2, Pallas kernels, attention_call(): pl.pallas_call(kernel, grid_spec=pltpu.PrefetchScalarGridSpec(num_scalar_...  53.3 us
    convert_element_type x1, other arithmetic, local(): ffn_full[i * ff:(i + 1) * ff].astype(F32)  10.5 us
  transfers between devices with their start and end apart: 2, of which 1 were waited for; matrix products, arithmetic and copies ran while one was open for 6% of the time, Pallas kernels for 50%

profile of v7, /device:TPU:1, one launch (start us, length us, event | category | flops | bytes accessed | tf_op | source)
XLA Modules:
  0.0 452.5 jit_solution(17245602166915345059)
XLA Ops:
  7.2 0.0 all-gather.2.cloned.1.call-start
  7.2 0.7 fusion.9
  7.9 0.7 stack.20
  8.6 0.7 stack.19
  9.2 0.1 pad.11.clone
  9.3 1.6 broadcast_select_fusion.refs_2_
  10.9 0.7 maximum_maximum_fusion.refs_1_
  11.6 55.7 %shard_map.203 = (bf16[8,128,2048]{2,1,0:T(8,128)(2,1)}, bf16[8,16,256]{2,1,0:T(8,128)(2,1)}, bf16[32,2048]{1,0:T(8,128)(2,1)}, bf16[8,256,2048]{2,1,0:T(8,128)(2,1)}) custom-call(bf16[128,2048]{1,0:T(8,128)(2,1)} %x_ref.1, bf16[16,256]{1,0:T(8,128)(2,1)} %maximum_maximum_fusion.refs_1_, bf16[32,2048]{1,0:T(8,128)(2,1)} %broadcast_select_fusion.refs_2_, ...), custom_call_target="tpu_custom_call" | custom-call | tf_op jit(solution)/shard_map/pallas_call | solution.py:333
  67.3 0.0 all-gather.2.cloned.1.call-update
  67.3 0.0 reduce-scatter.2.cloned.1.call-start
  67.5 0.8 copy.31
  68.3 0.7 convert_add_fusion
  69.1 0.5 fusion.7
  69.7 1.0 copy.25.cosine.cos_ref.refs_5_
  70.8 1.0 copy.26.sine.sin_ref.refs_6_
  71.8 1.4 slice_convert_fusion.5
  73.2 7.5 %shard_map.204 = (bf16[1024,2048]{1,0:T(8,128)(2,1)}, bf16[8,128,256]{2,1,0:T(8,128)(2,1)}, bf16[8,128,128]{2,1,0:T(8,128)(2,1)}) custom-call(s32[1]{0:T(128)} %bitcast.5.pair_ref, bf16[1024,2048]{1,0:T(8,128)(2,1)} %bitcast.49, f32[1,2048]{1,0:T(1,128)} %bitcast.35, bf16[256,2048]{1,0:T(8,128)(2,1)} %refs_8_.1, bf16[32,2048]{1,0:T(8,128)(2,1)} %refs_9_.1, ...), custom_call_target="tpu_custom_call" | custom-call | flops 2147483648 | bytes 10485760 | tf_op jit(solution)/shard_map/pallas_call | solution.py:726
  80.7 35.5 %shard_map.205 = (bf16[8,128,256]{2,1,0:T(8,128)(2,1)}, bf16[16,128,512]{2,1,0:T(8,128)(2,1)}) custom-call(bf16[8,128,256]{2,1,0:T(8,128)(2,1)} %get-tuple-element.52.refs_0_, bf16[8,128,128]{2,1,0:T(8,128)(2,1)} %get-tuple-element.53.refs_1_), custom_call_target="tpu_custom_call" | custom-call | tf_op jit(solution)/shard_map/pallas_call | solution.py:333
  116.3 0.7 pad_add_fusion.own_ref
  116.9 0.5 and_select_fusion.2.order_ref
  117.4 22.1 %shard_map.206 = (bf16[128,2048]{1,0:T(8,128)(2,1)}, f32[4,8,512]{2,1,0:T(8,128)}, f32[128,2048]{1,0:T(8,128)}, bf16[128,2048]{1,0:T(8,128)(2,1)}) custom-call(s32[16]{0:T(128)} %and_select_fusion.2.order_ref, s32[2]{0:T(128)} %pad_add_fusion.own_ref, bf16[8,128,256]{2,1,0:T(8,128)(2,1)} %get-tuple-element.54.q_ref, ...), custom_call_target="tpu_custom_call" | custom-call | flops 8589934592 | bytes 8388608 | tf_op jit(solution)/shard_map/pallas_call | solution.py:916
  139.5 3.4 all-gather.2.cloned.1.call-done.refs_1_
  142.9 112.9 %shard_map.207 = (f32[128,2048]{1,0:T(8,128)}, bf16[8,128,2048]{2,1,0:T(8,128)(2,1)}, bf16[2112,128]{1,0:T(8,128)(2,1)}, bf16[1024,256]{1,0:T(8,128)(2,1)}) custom-call(bf16[128,2048]{1,0:T(8,128)(2,1)} %get-tuple-element.58.refs_0_, bf16[1024,2048]{1,0:T(8,128)(2,1)} %all-gather.2.cloned.1.call-done.refs_1_, bf16[704,2048]{1,0:T(8,128)(2,1)} %refs_2_.1, ...), custom_call_target="tpu_custom_call" | custom-call | tf_op jit(solution)/shard_map/pallas_call | solution.py:333
  255.8 0.0 copy-start
  255.8 0.0 copy-start.1
  255.8 0.0 copy-start.4
  255.8 0.0 copy-start.3
  255.8 0.0 reduce-scatter.2.cloned.1.call-update
  255.8 1.2 copy-done
  257.0 0.2 multiply_reduce_fusion.2
  257.2 0.2 copy-done.1
  257.3 0.0 copy-done.4
  257.3 0.3 multiply_reduce_fusion
  257.6 0.6 scatter.4.refs_11_
  258.3 0.0 copy-done.3
  258.3 1.2 fusion.10.hidden_ref.refs_2_
  259.4 31.2 %shard_map.208 = (bf16[128,2048]{1,0:T(8,128)(2,1)}, bf16[16,128,512]{2,1,0:T(8,128)(2,1)}) custom-call(s32[16]{0:T(128)} %and_select_fusion.2.order_ref, s32[2]{0:T(128)} %pad_add_fusion.own_ref, bf16[8,128,256]{2,1,0:T(8,128)(2,1)} %get-tuple-element.54.q_ref, bf16[16,128,512]{2,1,0:T(8,128)(2,1)} %get-tuple-element.55.kv_ref, ...), custom_call_target="tpu_custom_call" | custom-call | flops 17179869184 | bytes 8388608 | tf_op jit(solution)/shard_map/pallas_call | solution.py:916
  290.6 0.0 copy-start.6
  290.6 131.6 %shard_map.209 = (bf16[2112,2048]{1,0:T(8,128)(2,1)}, bf16[640,2048]{1,0:T(8,128)(2,1)}, f32[128,2048]{1,0:T(8,128)}, f32[8,256]{1,0:T(8,128)}) custom-call(bf16[16,128,512]{2,1,0:T(8,128)(2,1)} %get-tuple-element.64.refs_0_, bf16[2112,128]{1,0:T(8,128)(2,1)} %get-tuple-element.65.refs_1_, bf16[128,2048]{1,0:T(8,128)(2,1)} %fusion.10.hidden_ref.refs_2_, ...), custom_call_target="tpu_custom_call" | custom-call | tf_op jit(solution)/shard_map/pallas_call | solution.py:333
  422.3 0.0 copy-done.2
  422.3 0.0 copy-done.5
  422.3 1.5 fusion
  423.8 1.3 fusion.11
  425.2 0.6 convert_divide_fusion
  425.7 1.8 dynamic-slice_convert_fusion
  427.5 4.1 slice_convert_fusion.3
  431.6 10.5 %slice_convert_fusion = (f32[704,2048]{1,0:T(8,128)}, f32[704,2048]{1,0:T(8,128)}, f32[704,2048]{1,0:T(8,128)}) fusion(bf16[2112,2048]{1,0:T(8,128)(2,1)} %get-tuple-element.72), kind=kLoop, calls=%fused_computation | loop fusion | flops 4325376 | bytes 25952256 | tf_op jit(solution)/shard_map/convert_element_type | solution.py:1087
  442.1 3.1 fusion.5
  (14 shorter events, 0.2 us)
Async XLA Ops:
  7.2 135.7 %all-gather.2.cloned.1.call-start = ((), (), s32[]{:S(2)}) async-start(), calls=%async_computation.1 | async-start | bytes 4718592 | tf_op jit(solution)/shard_map/all_gather | solution.py:991
  67.3 374.7 %reduce-scatter.2.cloned.1.call-start = ((), (), s32[]{:S(2)}) async-start(), calls=%async_computation.2 | async-start | bytes 4718592 | tf_op jit(solution)/shard_map/reduce_scatter | solution.py:1040
  255.8 1.2 copy-start
  255.8 1.5 copy-start.1
  255.8 1.5 copy-start.4
  255.8 2.4 copy-start.3
  290.6 131.6 %copy-start.2 = (bf16[128,2048]{1,0:T(8,128)(2,1)S(1)}, bf16[128,2048]{1,0:T(8,128)(2,1)}, u32[]{:S(2)}) copy-start(bf16[128,2048]{1,0:T(8,128)(2,1)} %x_ref.1) | copy-start | bytes 1572868
  290.6 131.6 %copy-start.5 = (f32[8,1,256]{2,1,0:T(1,128)S(1)}, f32[8,1,256]{2,1,0:T(1,128)}, u32[]{:S(2)}) copy-start(f32[8,1,256]{2,1,0:T(1,128)} %get-tuple-element.89) | copy-start | bytes 24580
  290.6 134.5 %copy-start.6 = (bf16[256]{0:T(256)(128)(2,1)S(1)}, bf16[256]{0:T(256)(128)(2,1)}, u32[]{:S(2)}) copy-start(bf16[256]{0:T(256)(128)(2,1)} %param.17) | copy-start | bytes 1540
Sparse Core Ops, SparseCore 0:
  67.5 75.3 all-gather.1
  256.0 108.0 reduce-scatter.1
